TPU v7x, 512 devices: a whole 4x8x8 slice. The times are simulated.
512 devices in a mesh: task: 8 (over y_lo, core), fsdp: 64 (over x, y_hi, z).
Axes of the slice: x: 4, y: 8 (y_hi: 2, y_lo: 4; y = y_hi * 4 + y_lo), z: 8, core: 2. Of those that a mesh axis runs over, the one named last changes fastest.
Arguments:
- embeddings: bfloat16 [1024, 4096], P(('task', 'fsdp')), may hold values from -6 to 6
- head_in: bfloat16 [8, 4096, 8192], P('task', None, 'fsdp'), may hold values from -0.09375 to 0.09375
- bias_in: float32 [8, 8192], P('task', 'fsdp'), may hold values from -3 to 3
- head_out: bfloat16 [8, 8192, 128], P('task', 'fsdp'), may hold values from -0.1875 to 0.1875
- bias_out: float32 [8192], P('task'), may hold values from -3 to 3
- block_owner: int32 [8, 8], P('task'), may hold values from 0 to 7, each once within a row
- targets: bfloat16 [1024, 8192], P('fsdp', 'task'), may hold values from -5 to 5
- entry_mask: int32 [1024, 8192], P('fsdp', 'task'), may hold values 0 or 1
- block_mask: int32 [128, 64], P('fsdp', 'task'), may hold values from 0 to 1
Outputs:
- head_in_grad: float32 [8, 4096, 8192], P('task', None, 'fsdp')
- bias_in_grad: float32 [8, 8192], P('task', 'fsdp')
- head_out_grad: float32 [8, 8192, 128], P('task', 'fsdp')
Inputs may be any that keep to these rules, and one draw needn't show every extreme that they name: `block_owner`: each row lists every one of the 8 assay blocks of its group once.
All inputs are finite; a program needn't handle non-finite values. No bound on the sum of `entry_mask` on one device may be relied on, other than what follows from the above.
Results may differ from a plain program's by a relative error of at most 0.0043.
Values may be sent and summed in bfloat16 or wider, within the bound.
No kernel may reach another device: no remote copies, remote signals or barrier semaphores. Data moves between devices by JAX's collectives and lax.ppermute only.
A program may use at most 64 MiB of HBM per device.

v0:
```python
import math

import jax
import jax.numpy as jnp
from jax import lax
from jax.sharding import PartitionSpec as P

H = 1024
A = 128
CBLK = 8


inv_root_two = 0.7071067811865476
inv_root_two_pi = 0.3989422804014327


def gelu_parts(values):
    normal_cdf = 0.5 * (1.0 + jax.scipy.special.erf(values * inv_root_two))
    density = jnp.exp(-0.5 * values * values) * inv_root_two_pi
    return (values * normal_cdf, normal_cdf + values * density)


def local(
    embeddings, head_in, bias_in, head_out, bias_out, block_owner, targets, entry_mask, block_mask
):
    fsdp_count = lax.axis_size("fsdp")
    hid_dev = head_in.shape[2]
    shards_per_head = H // hid_dev
    blocks = fsdp_count // shards_per_head
    gathered = lax.all_gather(embeddings, ("task", "fsdp"), axis=0, tiled=True)
    whole_rows = gathered.shape[0]
    local_rows = whole_rows // fsdp_count
    scaling = 1.0 / math.sqrt(whole_rows)
    pre_gelu = (
        jnp.dot(gathered, head_in[0], preferred_element_type=jnp.float32) + bias_in[0][None, :]
    )
    activated, slopes = gelu_parts(pre_gelu)
    hidden = activated.astype(jnp.bfloat16)
    partial_value = jnp.dot(hidden, head_out[0], preferred_element_type=jnp.float32)
    slot_ids = jnp.arange(blocks, dtype=jnp.int32)
    selector = (block_owner[0][:, None] == slot_ids[None, :]).astype(jnp.float32)
    received = lax.all_to_all(partial_value, "fsdp", split_axis=0, concat_axis=1, tiled=True)
    grouped = jnp.sum(received.reshape(local_rows, blocks, shards_per_head, A), axis=2)
    logit_sum = jnp.einsum(
        "cba,bo->coa", grouped, selector, precision=lax.Precision.HIGHEST
    ).reshape(local_rows, blocks * A)
    logits = (logit_sum + bias_out[None, :]).reshape(local_rows, blocks, A)
    measured = (
        entry_mask.reshape(local_rows, blocks, A) * jnp.repeat(block_mask, CBLK, axis=0)[:, :, None]
    )
    target_three = targets.reshape(local_rows, blocks, A).astype(jnp.float32)
    residual = (measured.astype(jnp.float32) * (logits - target_three) * scaling).astype(
        jnp.bfloat16
    )
    slotted = jnp.einsum(
        "coa,bo->cba", residual.astype(jnp.float32), selector, precision=lax.Precision.HIGHEST
    ).astype(jnp.bfloat16)
    spread_out = jnp.broadcast_to(
        slotted[:, :, None, :], (local_rows, blocks, shards_per_head, A)
    ).reshape(local_rows, fsdp_count * A)
    my_residual = lax.all_to_all(spread_out, "fsdp", split_axis=1, concat_axis=0, tiled=True)
    back_hidden = lax.dot_general(
        my_residual, head_out[0], (((1,), (1,)), ((), ())), preferred_element_type=jnp.float32
    )
    hidden_grad = (back_hidden * slopes).astype(jnp.bfloat16)
    head_in_grad = lax.dot_general(
        gathered, hidden_grad, (((0,), (0,)), ((), ())), preferred_element_type=jnp.float32
    )
    bias_in_grad = jnp.sum(hidden_grad.astype(jnp.float32), axis=0)
    head_out_grad = lax.dot_general(
        hidden, my_residual, (((0,), (0,)), ((), ())), preferred_element_type=jnp.float32
    )
    return (head_in_grad[None], bias_in_grad[None], head_out_grad[None])


def solution(mesh):
    in_specs = (
        P(("task", "fsdp"), None),
        P("task", None, "fsdp"),
        P("task", "fsdp"),
        P("task", "fsdp", None),
        P("task"),
        P("task", None),
        P("fsdp", "task"),
        P("fsdp", "task"),
        P("fsdp", "task"),
    )
    out_specs = (P("task", None, "fsdp"), P("task", "fsdp"), P("task", "fsdp", None))
    return jax.shard_map(local, mesh=mesh, in_specs=in_specs, out_specs=out_specs, check_vma=False)
```

profile of v0, /device:TPU:1, one launch (start us, length us, event | category | flops | bytes accessed | tf_op | source)
XLA Modules:
  0.0 1520.0 jit_solution(3319172575725995961)
XLA Ops:
  7.2 0.0 copy-start
  7.2 0.0 all-gather.3.cloned.1.call-start
  7.2 0.7 all-gather.3.cloned.1.call-update
  7.9 0.0 copy-start.7
  7.9 1419.3 %all-gather.3.cloned.1.call-done = bf16[512,2,4096]{2,1,0:T(2,128)(2,1)} async-done(((bf16[1,2,4096]{2,1,0:T(2,128)(2,1)}), bf16[512,2,4096]{2,1,0:T(2,128)(2,1)}) %all-gather.3.cloned.1.call-update) | async-done | bytes 8388624 | tf_op jit(solution)/shard_map/all_gather | solution.py:30
  1427.3 13.1 reshape.40
  1440.4 0.0 copy-start.3
  1440.4 0.0 copy-start.2
  1440.4 0.0 copy-start.1
  1440.4 0.0 copy-start.6
  1440.4 0.0 copy-start.4
  1440.4 0.0 copy-start.5
  1440.4 0.0 copy-done
  1440.4 0.0 copy-done.7
  1440.4 5.8 multiply_convert_fusion
  1446.3 0.0 copy-done.3
  1446.3 1.0 fusion.14
  1447.3 16.2 %all-to-all-start = ((f32[64,16,128]{2,1,0:T(8,128)}), f32[64,16,128]{2,1,0:T(8,128)S(1)}, u32[]{:S(2)}, u32[]{:S(2)}) async-start(f32[64,16,128]{2,1,0:T(8,128)} %fusion.14), calls=%async_computation | async-start | bytes 1048576 | tf_op jit(solution)/shard_map/all_to_all | solution.py:42
  1463.5 0.0 copy-done.2
  1463.5 0.0 copy-done.1
  1463.6 0.0 copy-done.6
  1463.6 0.1 fusion.12
  1463.7 16.2 %all-to-all-done = f32[64,16,128]{2,1,0:T(8,128)S(1)} async-done(((f32[64,16,128]{2,1,0:T(8,128)}), f32[64,16,128]{2,1,0:T(8,128)S(1)}, u32[]{:S(2)}, u32[]{:S(2)}) %all-to-all-start) | async-done | bytes 524320 | tf_op jit(solution)/shard_map/all_to_all | solution.py:42
  1479.9 0.0 copy-done.4
  1479.9 0.0 copy-done.5
  1479.9 0.3 fusion.5
  1480.2 0.2 fusion.6
  1480.5 24.4 %all_to_all.32 = bf16[16,64,128]{2,0,1:T(8,128)(2,1)S(1)} all-to-all(bf16[16,64,128]{2,0,1:T(8,128)(2,1)S(1)} %bitcast.71), channel_id=1, replica_groups=mesh['task'=8,'fsdp'=64] {'fsdp'}, dimensions={1} | all-to-all | bytes 524288 | tf_op jit(solution)/shard_map/all_to_all | solution.py:61
  1504.9 0.9 convolution_bitcast_fusion.1
  1505.8 0.9 convert_reduce_fusion
  1506.7 4.7 convolution_bitcast_fusion
  1511.4 1.8 copy.24
  (7 shorter events, 0.1 us)
Async XLA Ops:
  7.2 1433.2 %copy-start = (bf16[1,4096,128]{2,1,0:T(8,128)(2,1)S(1)}, bf16[1,4096,128]{2,1,0:T(8,128)(2,1)}, u32[]{:S(2)}) copy-start(bf16[1,4096,128]{2,1,0:T(8,128)(2,1)} %param.10) | copy-start | bytes 3145732
  7.2 1420.1 %all-gather.3.cloned.1.call-start = ((), (), s32[]{:S(2)}) async-start(), calls=%async_computation.2 | async-start | bytes 8404992 | tf_op jit(solution)/shard_map/all_gather | solution.py:30
  7.9 1432.5 %copy-start.7 = (f32[1,128]{1,0:T(1,128)S(1)}, f32[1,128]{1,0:T(1,128)}, u32[]{:S(2)}) copy-start(f32[1,128]{1,0:T(1,128)} %param.11) | copy-start | bytes 1540
  1440.4 5.9 copy-start.3
  1440.4 23.1 %copy-start.2 = (bf16[16,1024]{1,0:T(8,128)(2,1)S(1)}, bf16[16,1024]{1,0:T(8,128)(2,1)}, u32[]{:S(2)}) copy-start(bf16[16,1024]{1,0:T(8,128)(2,1)} %param.15) | copy-start | bytes 98308
  1440.4 23.2 %copy-start.1 = (s32[16,1024]{1,0:T(8,128)S(1)}, s32[16,1024]{1,0:T(8,128)}, u32[]{:S(2)}) copy-start(s32[16,1024]{1,0:T(8,128)} %param.16) | copy-start | bytes 196612
  1440.4 23.2 %copy-start.6 = (s32[2,8]{1,0:T(2,128)S(1)}, s32[2,8]{1,0:T(2,128)}, u32[]{:S(2)}) copy-start(s32[2,8]{1,0:T(2,128)} %param.17) | copy-start | bytes 196
  1440.4 39.5 %copy-start.4 = (f32[1024]{0:T(1024)S(1)}, f32[1024]{0:T(1024)}, u32[]{:S(2)}) copy-start(f32[1024]{0:T(1024)} %param.13) | copy-start | bytes 12292
  1440.4 39.5 %copy-start.5 = (s32[1,8]{1,0:T(1,128)S(1)}, s32[1,8]{1,0:T(1,128)}, u32[]{:S(2)}) copy-start(s32[1,8]{1,0:T(1,128)} %param.14) | copy-start | bytes 100
  1447.3 32.6 %all-to-all-start = ((f32[64,16,128]{2,1,0:T(8,128)}), f32[64,16,128]{2,1,0:T(8,128)S(1)}, u32[]{:S(2)}, u32[]{:S(2)}) async-start(f32[64,16,128]{2,1,0:T(8,128)} %fusion.14), calls=%async_computation | async-start | bytes 1048576 | tf_op jit(solution)/shard_map/all_to_all | solution.py:42
Sparse Core Ops, SparseCore 0:
  10.2 1416.9 all-gather.2
where the time goes:
time: 1520 us
  waiting for transfers between devices  1440 us (95%)
  blocking collectives  24.4 us (2%)
  starting transfers between devices  16.2 us (1%)
    all_gather x1, waiting for transfers between devices, local(): gathered = lax.all_gather(embeddings, ('task', 'fsdp'), axis=0, tiled=True)  1420 us
  transfers between devices with their start and end apart: 2, of which 2 were waited for; matrix products, arithmetic and copies ran while one was open for 0% of the time, Pallas kernels for 0%

commit v1 on v0

v1 whole, which is shorter than its diff:
```python
import math

import jax
import jax.numpy as jnp
from jax import lax
from jax.sharding import PartitionSpec as P

H = 1024
A = 128
CBLK = 8
ALL = ("task", "fsdp")

inv_root_two = 0.7071067811865476
inv_root_two_pi = 0.3989422804014327


def gelu_parts(values):
    normal_cdf = 0.5 * (1.0 + jax.scipy.special.erf(values * inv_root_two))
    density = jnp.exp(-0.5 * values * values) * inv_root_two_pi
    return (values * normal_cdf, normal_cdf + values * density)


def place(i):
    t, f = divmod(i, 64)
    ylo, core = divmod(t, 2)
    x, rest = divmod(f, 16)
    yhi, z = divmod(rest, 8)
    return x, yhi * 4 + ylo, z, core


def grouped(key, order):
    groups = {}
    for i in range(512):
        groups.setdefault(key(i), []).append(i)
    return [sorted(groups[k], key=order) for k in sorted(groups)]


def parity(i):
    x, y, z, core = place(i)
    return x % 2, y % 2, z % 2


def cube(i):
    x, y, z, core = place(i)
    return (x + core) % 4 // 2, (y + core) % 8 // 2, (z + core) % 8 // 2, core


CLASSES = grouped(lambda i: parity(i) + (place(i)[3],), place)
CUBES = grouped(cube, parity)
ALONG_Z = [[8 * j + z for z in range(8)] for j in range(8)]
ACROSS_Z = [[8 * j + z for j in range(8)] for z in range(8)]


def exchange(blocks, axis, groups):
    return lax.all_to_all(blocks, axis, 0, 0, tiled=True, axis_index_groups=groups)


def spread(block, axis, groups):
    copies = jnp.broadcast_to(block[None], (len(groups[0]),) + block.shape)
    return exchange(copies, axis, groups)


def local(
    embeddings, head_in, bias_in, head_out, bias_out, block_owner, targets, entry_mask, block_mask
):
    core = lax.axis_index("task") % 2
    slot = lax.axis_index("fsdp") // 8
    scaling = 1.0 / math.sqrt(1024)
    bf16, f32 = jnp.bfloat16, jnp.float32

    measured = entry_mask.reshape(16, 8, A) * jnp.repeat(block_mask, CBLK, axis=0)[:, :, None]
    pair = jnp.stack([targets.reshape(16, 8, A), measured.astype(bf16)])
    pair = pair.reshape(2, 2, 2, 2, 2, 8, A).transpose(5, 0, 3, 1, 2, 4, 6).reshape(8, 2 * 16 * A)
    selector = (block_owner[0][:, None] == jnp.arange(8, dtype=jnp.int32)[None, :]).astype(bf16)
    pair = jnp.dot(selector, pair, preferred_element_type=f32).astype(bf16).reshape(8, 32, A)
    bias_slot = lax.dynamic_slice_in_dim(
        bias_out.reshape(8, A), lax.dynamic_index_in_dim(block_owner[0], slot, keepdims=False), 1
    )

    rows = spread(embeddings, ALL, CLASSES).reshape(64, -1)
    own = spread(rows, ALL, CUBES).reshape(512, -1)
    own, pair = lax.optimization_barrier((own, pair))
    other = lax.ppermute(own, "task", [(i, i ^ 1) for i in range(8)])
    pair = exchange(pair, "fsdp", ACROSS_Z).reshape(8, 2, 16, A)

    def forward(part):
        pre = jnp.dot(part, head_in[0], preferred_element_type=f32) + bias_in[0][None, :]
        activated, slopes = gelu_parts(pre)
        hidden = activated.astype(bf16)
        return hidden, slopes, jnp.dot(hidden, head_out[0], preferred_element_type=f32)

    hidden_own, slopes_own, share_own = forward(own)
    hidden_other, slopes_other, share_other = forward(other)
    first = jnp.where(core == 0, share_own, share_other)
    second = jnp.where(core == 0, share_other, share_own)
    shares = jnp.stack([first, second]).reshape(2, 2, 2, 2, 2, 2, 2, 8, A)
    shares = shares.transpose(4, 1, 5, 6, 2, 0, 3, 7, 8).reshape(8, 128, A)
    logits = jnp.sum(exchange(shares, "fsdp", ALONG_Z).reshape(8, 128, A), axis=0) + bias_slot
    residual = pair[:, 1].reshape(128, A).astype(f32) * (
        logits - pair[:, 0].reshape(128, A).astype(f32)
    )
    residual = (residual * scaling).astype(bf16)
    back = spread(residual, "fsdp", ALONG_Z).reshape(2, 2, 2, 2, 2, 2, 2, 8, A)
    back = back.transpose(5, 1, 4, 6, 0, 2, 3, 7, 8).reshape(2, 512, A)
    res_own = jnp.where(core == 0, back[0], back[1])
    res_other = jnp.where(core == 0, back[1], back[0])

    def backward(part, hidden, slopes, res):
        grad = lax.dot_general(
            res, head_out[0], (((1,), (1,)), ((), ())), preferred_element_type=f32
        )
        grad = (grad * slopes).astype(bf16)
        rows_first = (((0,), (0,)), ((), ()))
        return (
            lax.dot_general(part, grad, rows_first, preferred_element_type=f32),
            jnp.sum(grad.astype(f32), axis=0),
            lax.dot_general(hidden, res, rows_first, preferred_element_type=f32),
        )

    one = backward(own, hidden_own, slopes_own, res_own)
    two = backward(other, hidden_other, slopes_other, res_other)
    return tuple((a + b)[None] for a, b in zip(one, two))


def solution(mesh):
    in_specs = (
        P(("task", "fsdp"), None),
        P("task", None, "fsdp"),
        P("task", "fsdp"),
        P("task", "fsdp", None),
        P("task"),
        P("task", None),
        P("fsdp", "task"),
        P("fsdp", "task"),
        P("fsdp", "task"),
    )
    out_specs = (P("task", None, "fsdp"), P("task", "fsdp"), P("task", "fsdp", None))
    return jax.shard_map(local, mesh=mesh, in_specs=in_specs, out_specs=out_specs, check_vma=False)
```

time: 1520 us -> 150 us (0.10)
  the two profiles are of different devices: /device:TPU:1 before, /device:TPU:56 now
where the time goes in v1:
time: 150 us
  blocking collectives  50.4 us (34%)
  waiting for transfers between devices  47.7 us (32%)
  starting transfers between devices  23.8 us (16%)
  matrix products  17.4 us (12%)
  local copies, waits for them, and re-layouts  6.87 us (5%)
  between operations  2.82 us (2%)
    all_to_all x2, blocking collectives, exchange(): lax.all_to_all(blocks, axis, 0, 0, tiled=True, axis_index_groups=groups)  50.4 us
    all_to_all x3, waiting for transfers between devices, exchange(): lax.all_to_all(blocks, axis, 0, 0, tiled=True, axis_index_groups=groups)  47.7 us
    all_to_all x3, starting transfers between devices, exchange(): lax.all_to_all(blocks, axis, 0, 0, tiled=True, axis_index_groups=groups)  21.9 us
    dot_general x2, matrix products, backward(): lax.dot_general(part, grad, rows_first, preferred_element_type=f32)  8.33 us
    dot_general x2, matrix products, forward(): jnp.dot(part, head_in[0], preferred_element_type=f32) + bias_in[0][None, :]  6.98 us
    broadcast_in_dim x4, local copies, waits for them, and re-layouts, spread(): copies = jnp.broadcast_to(block[None], (len(groups[0]),) + block.shape)  3.97 us
  transfers between devices with their start and end apart: 4, of which 2 were waited for; matrix products, arithmetic and copies ran while one was open for 7% of the time, Pallas kernels for 0%

profile of v1, /device:TPU:56, one launch (start us, length us, event | category | flops | bytes accessed | tf_op | source)
XLA Modules:
  0.0 149.8 jit_solution(9254292049971090512)
XLA Ops:
  0.6 0.0 copy-start
  0.6 1.3 broadcast_in_dim.12
  1.9 35.6 %all_to_all.25 = bf16[32,2,4096]{2,1,0:T(2,128)(2,1)S(1)} all-to-all(bf16[32,2,4096]{2,1,0:T(2,128)(2,1)S(1)} %broadcast_in_dim.12), channel_id=1, replica_groups={{0,2,4,6,256,258,260,262,8,10,12,14,264,266,268,270,32,34,36,38,288,290..., dimensions={0} | all-to-all | bytes 1048576 | tf_op jit(solution)/shard_map/all_to_all | solution.py:55
  37.6 0.2 broadcast_in_dim.13
  37.8 2.5 %broadcast_in_dim.14 = bf16[8,64,4096]{2,1,0:T(8,128)(2,1)} broadcast(bf16[64,4096]{1,0:T(8,128)(2,1)S(1)} %broadcast_in_dim.13), dimensions={1,2} | broadcast | bytes 4718592 | tf_op jit(solution)/shard_map/broadcast_in_dim | solution.py:59
  40.2 0.0 copy-start.2
  40.2 0.0 copy-start.3
  40.2 0.0 copy-start.4
  40.2 0.0 copy-start.5
  40.2 0.0 copy-start.6
  40.2 9.4 %all-to-all-start.1 = ((bf16[8,64,4096]{2,1,0:T(8,128)(2,1)}), bf16[8,64,4096]{2,1,0:T(8,128)(2,1)}, u32[]{:S(2)}, u32[]{:S(2)}) async-start(bf16[8,64,4096]{2,1,0:T(8,128)(2,1)} %broadcast_in_dim.14), calls=%async_computation.1 | async-start | bytes 8388608 | tf_op jit(solution)/shard_map/all_to_all | solution.py:55
  49.7 0.0 copy-done.2
  49.7 0.0 copy-done.3
  49.7 0.0 copy-done.4
  49.7 0.1 multiply_convert_fusion.2
  49.8 0.0 copy-done.5
  49.8 0.2 fusion.2
  50.0 33.2 %all-to-all-done.1 = bf16[8,64,4096]{2,1,0:T(8,128)(2,1)} async-done(((bf16[8,64,4096]{2,1,0:T(8,128)(2,1)}), bf16[8,64,4096]{2,1,0:T(8,128)(2,1)}, u32[]{:S(2)}, u32[]{:S(2)}) %all-to-all-start.1) | async-done | bytes 4194336 | tf_op jit(solution)/shard_map/all_to_all | solution.py:55
  83.2 1.9 %collective-permute-start = (bf16[512,4096]{1,0:T(8,128)(2,1)}, bf16[512,4096]{1,0:T(8,128)(2,1)}, u32[]{:S(2)}, u32[]{:S(2)}) collective-permute-start(bf16[512,4096]{1,0:T(8,128)(2,1)} %bitcast), channel_id=1, source_target_pairs={{0,64},{64,0},{128,192},{192,128},{256,320},{320,256},{384,448},{4... | collective-permute-start | bytes 12582920 | tf_op jit(solution)/shard_map/ppermute | solution.py:83
  85.1 0.6 copy.15
  85.8 9.0 %all-to-all-start.2 = ((bf16[8,32,128]{2,1,0:T(8,128)(2,1)}), bf16[8,32,128]{2,1,0:T(8,128)(2,1)S(1)}, u32[]{:S(2)}, u32[]{:S(2)}) async-start(bf16[8,32,128]{2,1,0:T(8,128)(2,1)} %copy.15), calls=%async_computation.2 | async-start | bytes 131072 | tf_op jit(solution)/shard_map/all_to_all | solution.py:55
  94.8 0.0 copy-done
  94.8 0.0 copy-done.6
  94.8 3.5 %multiply_convert_fusion.1 = (bf16[512,128]{1,0:T(8,128)(2,1)S(1)}, f32[512,128]{1,0:T(8,128)S(1)}) fusion(f32[128]{0:T(128)S(1)} %bitcast.97, bf16[512,4096]{1,0:T(8,128)(2,1)} %bitcast, bf16[1,4096,128]{2,1,0:T(8,128)(2,1)S(1)} %copy-done), kind=kOutput, calls=%fused_computation.29 | convolution fusion | flops 537264128 | bytes 5636608 | tf_op jit(solution)/shard_map/dot_general | solution.py:87
  98.3 0.0 copy-start.1
  98.3 0.0 collective-permute-done
  98.4 3.5 %multiply_convert_fusion = (bf16[512,128]{1,0:T(8,128)(2,1)S(1)}, f32[512,128]{1,0:T(8,128)S(1)}) fusion(f32[128]{0:T(128)S(1)} %bitcast.98, bf16[512,4096]{1,0:T(8,128)(2,1)} %collective-permute-done, bf16[1,4096,128]{2,1,0:T(8,128)(2,1)S(1)} %copy-done), kind=kOutput, calls=%fused_computation.27 | convolution fusion | flops 537264128 | bytes 5636608 | tf_op jit(solution)/shard_map/dot_general | solution.py:87
  101.9 0.0 copy-done.1
  101.9 0.2 fusion.22
  102.0 0.2 broadcast_select_fusion.1
  102.3 0.9 copy.20
  103.1 0.0 all-to-all-done.2
  103.1 3.5 %all-to-all-start.3 = ((f32[8,128,128]{2,1,0:T(8,128)}), f32[8,128,128]{2,1,0:T(8,128)S(1)}, u32[]{:S(2)}, u32[]{:S(2)}) async-start(f32[8,128,128]{2,1,0:T(8,128)} %bitcast.13), calls=%async_computation.3 | async-start | bytes 1048576 | tf_op jit(solution)/shard_map/all_to_all | solution.py:55
  106.6 0.6 constant_dynamic-slice_fusion
  109.2 0.7 dynamic-slice_bitcast_fusion
  109.9 14.5 %all-to-all-done.3 = f32[8,128,128]{2,1,0:T(8,128)S(1)} async-done(((f32[8,128,128]{2,1,0:T(8,128)}), f32[8,128,128]{2,1,0:T(8,128)S(1)}, u32[]{:S(2)}, u32[]{:S(2)}) %all-to-all-start.3) | async-done | bytes 524320 | tf_op jit(solution)/shard_map/all_to_all | solution.py:55
  124.5 14.7 %all_to_all.26 = bf16[8,128,128]{2,1,0:T(8,128)(2,1)S(1)} all-to-all(bf16[8,128,128]{2,1,0:T(8,128)(2,1)S(1)} %broadcast_in_dim.15), channel_id=1, replica_groups={{0,1,2,3,4,5,6,7},{8,9,10,11,12,13,14,15},{16,17,18,19,20,21,22,23},{24..., dimensions={0} | all-to-all | bytes 524288 | tf_op jit(solution)/shard_map/all_to_all | solution.py:55
  139.3 0.2 fusion.31
  139.6 0.9 fusion.3
  140.5 0.2 convert_reduce_fusion
  140.7 0.2 convert_reduce_fusion.1
  140.9 3.5 %fusion.30 = f32[4096,128]{1,0:T(8,128)S(1)} fusion(bf16[512,4096]{1,0:T(8,128)(2,1)} %bitcast, bf16[512,128]{1,0:T(8,128)(2,1)S(1)} %get-tuple-element.18), kind=kOutput, calls=%fused_computation.54 | convolution fusion | flops 536870912 | bytes 6422528 | tf_op jit(solution)/shard_map/dot_general | solution.py:115
  144.4 0.5 add_bitcast_fusion
  144.9 4.8 %fusion = f32[1,4096,128]{2,1,0:T(8,128)} fusion(f32[4096,128]{1,0:T(8,128)S(1)} %fusion.30, bf16[512,4096]{1,0:T(8,128)(2,1)} %collective-permute-done, bf16[512,128]{1,0:T(8,128)(2,1)S(1)} %get-tuple-element.20), kind=kOutput, calls=%fused_computation.1 | convolution fusion | flops 537395200 | bytes 8519680 | tf_op jit(solution)/shard_map/dot_general | solution.py:115
  (12 shorter events, 0.2 us)
Async XLA Ops:
  0.6 94.2 %copy-start = (bf16[1,4096,128]{2,1,0:T(8,128)(2,1)S(1)}, bf16[1,4096,128]{2,1,0:T(8,128)(2,1)}, u32[]{:S(2)}) copy-start(bf16[1,4096,128]{2,1,0:T(8,128)(2,1)} %param.10) | copy-start | bytes 3145732
  40.2 9.4 %copy-start.2 = (s32[16,1024]{1,0:T(8,128)S(1)}, s32[16,1024]{1,0:T(8,128)}, u32[]{:S(2)}) copy-start(s32[16,1024]{1,0:T(8,128)} %param.16) | copy-start | bytes 196612
  40.2 9.4 %copy-start.3 = (bf16[16,1024]{1,0:T(8,128)(2,1)S(1)}, bf16[16,1024]{1,0:T(8,128)(2,1)}, u32[]{:S(2)}) copy-start(bf16[16,1024]{1,0:T(8,128)(2,1)} %param.15) | copy-start | bytes 98308
  40.2 9.5 %copy-start.4 = (s32[2,8]{1,0:T(2,128)S(1)}, s32[2,8]{1,0:T(2,128)}, u32[]{:S(2)}) copy-start(s32[2,8]{1,0:T(2,128)} %param.17) | copy-start | bytes 196
  40.2 9.6 %copy-start.5 = (s32[1,8]{1,0:T(1,128)S(1)}, s32[1,8]{1,0:T(1,128)}, u32[]{:S(2)}) copy-start(s32[1,8]{1,0:T(1,128)} %param.14) | copy-start | bytes 100
  40.2 54.6 %copy-start.6 = (f32[1,128]{1,0:T(1,128)S(1)}, f32[1,128]{1,0:T(1,128)}, u32[]{:S(2)}) copy-start(f32[1,128]{1,0:T(1,128)} %param.11) | copy-start | bytes 1540
  40.2 43.0 %all-to-all-start.1 = ((bf16[8,64,4096]{2,1,0:T(8,128)(2,1)}), bf16[8,64,4096]{2,1,0:T(8,128)(2,1)}, u32[]{:S(2)}, u32[]{:S(2)}) async-start(bf16[8,64,4096]{2,1,0:T(8,128)(2,1)} %broadcast_in_dim.14), calls=%async_computation.1 | async-start | bytes 8388608 | tf_op jit(solution)/shard_map/all_to_all | solution.py:55
  83.2 15.1 %collective-permute-start = (bf16[512,4096]{1,0:T(8,128)(2,1)}, bf16[512,4096]{1,0:T(8,128)(2,1)}, u32[]{:S(2)}, u32[]{:S(2)}) collective-permute-start(bf16[512,4096]{1,0:T(8,128)(2,1)} %bitcast), channel_id=1, source_target_pairs={{0,64},{64,0},{128,192},{192,128},{256,320},{320,256},{384,448},{4... | collective-permute-start | bytes 12582920 | tf_op jit(solution)/shard_map/ppermute | solution.py:83
  85.8 17.3 %all-to-all-start.2 = ((bf16[8,32,128]{2,1,0:T(8,128)(2,1)}), bf16[8,32,128]{2,1,0:T(8,128)(2,1)S(1)}, u32[]{:S(2)}, u32[]{:S(2)}) async-start(bf16[8,32,128]{2,1,0:T(8,128)(2,1)} %copy.15), calls=%async_computation.2 | async-start | bytes 131072 | tf_op jit(solution)/shard_map/all_to_all | solution.py:55
  98.3 3.5 %copy-start.1 = (bf16[1,128,128]{2,1,0:T(8,128)(2,1)S(1)}, bf16[1,128,128]{2,1,0:T(8,128)(2,1)}, u32[]{:S(2)}) copy-start(bf16[1,128,128]{2,1,0:T(8,128)(2,1)} %param.12) | copy-start | bytes 98308
  103.1 21.3 %all-to-all-start.3 = ((f32[8,128,128]{2,1,0:T(8,128)}), f32[8,128,128]{2,1,0:T(8,128)S(1)}, u32[]{:S(2)}, u32[]{:S(2)}) async-start(f32[8,128,128]{2,1,0:T(8,128)} %bitcast.13), calls=%async_computation.3 | async-start | bytes 1048576 | tf_op jit(solution)/shard_map/all_to_all | solution.py:55

commit v2 on v1

v2 whole, which is shorter than its diff:
```python
import math

import jax
import jax.numpy as jnp
from jax import lax
from jax.experimental import pallas as pl
from jax.experimental.pallas import tpu as pltpu
from jax.sharding import PartitionSpec as P

H = 1024
A = 128
CBLK = 8
ALL = ("task", "fsdp")

inv_root_two = 0.7071067811865476
inv_root_two_pi = 0.3989422804014327


def gelu_parts(values):
    normal_cdf = 0.5 * (1.0 + jax.scipy.special.erf(values * inv_root_two))
    density = jnp.exp(-0.5 * values * values) * inv_root_two_pi
    return (values * normal_cdf, normal_cdf + values * density)


def place(i):
    t, f = divmod(i, 64)
    ylo, core = divmod(t, 2)
    x, rest = divmod(f, 16)
    yhi, z = divmod(rest, 8)
    return x, yhi * 4 + ylo, z, core


def flat(x, y, z, core):
    x, y, z = x % 4, y % 8, z % 8
    return (y % 4 * 2 + core) * 64 + x * 16 + y // 4 * 8 + z


def classes():
    groups = {}
    for i in range(512):
        x, y, z, core = place(i)
        groups.setdefault(((2 * x + y + 3 * z) % 8, core), []).append(i)
    return [sorted(groups[k], key=place) for k in sorted(groups)]


def from_chip(dx, dy, dz):
    pairs = []
    for i in range(512):
        x, y, z, core = place(i)
        s = 1 - 2 * core
        pairs.append((flat(x + s * dx, y + s * dy, z + s * dz, core), i))
    return pairs


CLASSES = classes()
CORES = [(i, i ^ 64) for i in range(512)]
HELD = [(0, 0), (0, 1), (2, 0), (2, 1), (1, 0), (1, 1), (3, 0), (3, 1), (4, 0)]
HELD += [(-2, 1), (-2, 0), (-1, 1), (-1, 0), (-3, 1), (-3, 0), (4, 1)]
DIRECT = 9
ALONG_Z = [[8 * j + z for z in range(8)] for j in range(8)]
ACROSS_Z = [[8 * j + z for j in range(8)] for z in range(8)]


def exchange(blocks, axis, groups):
    return lax.all_to_all(blocks, axis, 0, 0, tiled=True, axis_index_groups=groups)


def spread(block, axis, groups):
    copies = jnp.broadcast_to(block[None], (len(groups[0]),) + block.shape)
    return exchange(copies, axis, groups)


def send(block, pairs):
    return lax.ppermute(block, ALL, pairs)


def shares_kernel(spots, direct, swapped, head_out, out):
    for part, start in ((direct, 0), (swapped, DIRECT)):
        share = jnp.dot(part[...], head_out[...], preferred_element_type=jnp.float32)
        for j in range(part.shape[0] // 64):
            out[:, spots[start + j]] = share[64 * j : 64 * j + 64].reshape(8, 8, A)


def backward_kernel(
    spots, back, hidden_d, hidden_s, slopes_d, slopes_s, head_out, grad_d, grad_s, bias, out, wide, rows
):
    for z in range(8):
        wide[z] = back[z].astype(jnp.float32).reshape(16, 8, A)
    for j in range(16):
        rows[64 * j : 64 * j + 64] = wide[:, spots[j]].reshape(64, A)
    bias_sum = jnp.zeros((1, A), jnp.float32)
    out_sum = jnp.zeros((A, A), jnp.float32)
    start = 0
    for hidden, slopes, grad in ((hidden_d, slopes_d, grad_d), (hidden_s, slopes_s, grad_s)):
        count = hidden.shape[0]
        res = rows[start : start + count].astype(jnp.bfloat16)
        start += count
        held = lax.dot_general(
            res, head_out[...], (((1,), (1,)), ((), ())), preferred_element_type=jnp.float32
        )
        rounded = (held * slopes[...]).astype(jnp.bfloat16)
        grad[...] = rounded
        bias_sum += jnp.sum(rounded.astype(jnp.float32), axis=0, keepdims=True)
        out_sum += lax.dot_general(
            hidden[...], res, (((0,), (0,)), ((), ())), preferred_element_type=jnp.float32
        )
    bias[...] = bias_sum
    out[...] = out_sum


def call(kernel, outs, operands, scratch=()):
    vmem = pl.BlockSpec(memory_space=pltpu.VMEM)
    return pl.pallas_call(
        kernel,
        out_shape=[jax.ShapeDtypeStruct(shape, dtype) for shape, dtype in outs],
        in_specs=[pl.BlockSpec(memory_space=pltpu.SMEM)] + [vmem] * (len(operands) - 1),
        out_specs=[vmem] * len(outs),
        scratch_shapes=list(scratch),
        compiler_params=pltpu.CompilerParams(vmem_limit_bytes=32 * 1024 * 1024),
    )(*operands)


def local(
    embeddings, head_in, bias_in, head_out, bias_out, block_owner, targets, entry_mask, block_mask
):
    task, fsdp = lax.axis_index("task"), lax.axis_index("fsdp")
    core, ylo = task % 2, task // 2
    x, yhi, z = fsdp // 16, fsdp // 8 % 2, fsdp % 8
    slot = fsdp // 8
    scaling = 1.0 / math.sqrt(1024)
    bf16, f32, i32 = jnp.bfloat16, jnp.float32, jnp.int32

    offset = jnp.array([d for d, _ in HELD], i32) * (1 - 2 * core)
    whose = jnp.array([w for _, w in HELD], i32)
    spots = (2 * x + yhi * 4 + ylo + 3 * z + offset + 16) % 8 * 2 + (whose + core) % 2

    measured = entry_mask.reshape(16, 8, A) * jnp.repeat(block_mask, CBLK, axis=0)[:, :, None]
    pair = jnp.stack([targets.reshape(16, 8, A), measured.astype(bf16)])
    pair = pair.transpose(2, 0, 1, 3).reshape(8, 2 * 16 * A)
    selector = (block_owner[0][:, None] == jnp.arange(8, dtype=i32)[None, :]).astype(bf16)
    pair = jnp.dot(selector, pair, preferred_element_type=f32).astype(bf16).reshape(8, 32, A)
    bias_slot = lax.dynamic_slice_in_dim(
        bias_out.reshape(8, A), lax.dynamic_index_in_dim(block_owner[0], slot, keepdims=False), 1
    )

    mine = spread(embeddings, ALL, CLASSES).reshape(64, -1)
    mine, pair = lax.optimization_barrier((mine, pair))
    both = jnp.concatenate([mine, send(mine, CORES)])
    fourth = send(mine, from_chip(0, 1, 1))
    fetched = [send(both, from_chip(*d)) for d in ((1, 0, 0), (0, 1, 0), (0, 0, 1))]
    fetched = jnp.concatenate(fetched + [fourth])
    swapped = send(fetched, CORES)
    pair = exchange(pair, "fsdp", ACROSS_Z).reshape(8, 2, 16, A)

    r, q = jnp.arange(128, dtype=i32)[:, None], jnp.arange(128, dtype=i32)[None, :]
    row_z = (3 * (r // 16 + 32 - 2 * (z // 2) - z % 2 * 4 - r // 2 % 4)) % 8
    order = (q == r // 2 % 4 * 32 + r // 8 % 2 * 16 + row_z * 2 + r % 2).astype(bf16)
    target = jnp.dot(order, pair[:, 0].reshape(128, A), preferred_element_type=f32)
    measured = jnp.dot(order, pair[:, 1].reshape(128, A), preferred_element_type=f32)

    def forward(*parts):
        pre = [jnp.dot(part, head_in[0], preferred_element_type=f32) for part in parts]
        pre = jnp.concatenate(pre) + bias_in[0][None, :]
        activated, slopes = gelu_parts(pre)
        return activated.astype(bf16), slopes

    direct = jnp.concatenate([both, fetched])
    hidden_d, slopes_d = forward(direct)
    hidden_s, slopes_s = forward(swapped)
    weights = head_out[0]
    (shares,) = call(
        shares_kernel, [((8, 16, 8, A), f32)], (spots, hidden_d, hidden_s, weights)
    )
    sums = exchange(shares.reshape(8, 128, A), "fsdp", ALONG_Z).reshape(8, 128, A)
    logits = jnp.sum(sums, axis=0) + bias_slot
    residual = (measured * (logits - target) * scaling).astype(bf16)
    back = spread(residual, "fsdp", ALONG_Z).reshape(8, 128, A)
    grad_d, grad_s, bias_in_grad, head_out_grad = call(
        backward_kernel,
        [(hidden_d.shape, bf16), (hidden_s.shape, bf16), ((1, A), f32), ((A, A), f32)],
        (spots, back, hidden_d, hidden_s, slopes_d, slopes_s, weights),
        [pltpu.VMEM((8, 16, 8, A), f32), pltpu.VMEM((1024, A), f32)],
    )

    def rows_first(left, right):
        return lax.dot_general(left, right, (((0,), (0,)), ((), ())), preferred_element_type=f32)

    head_in_grad = rows_first(direct, grad_d) + rows_first(swapped, grad_s)
    return head_in_grad[None], bias_in_grad, head_out_grad[None]


def solution(mesh):
    in_specs = (
        P(("task", "fsdp"), None),
        P("task", None, "fsdp"),
        P("task", "fsdp"),
        P("task", "fsdp", None),
        P("task"),
        P("task", None),
        P("fsdp", "task"),
        P("fsdp", "task"),
        P("fsdp", "task"),
    )
    out_specs = (P("task", None, "fsdp"), P("task", "fsdp"), P("task", "fsdp", None))
    return jax.shard_map(local, mesh=mesh, in_specs=in_specs, out_specs=out_specs, check_vma=False)
```

time: 150 us -> 149 us (level)
  the two profiles are of different devices: /device:TPU:56 before, /device:TPU:1 now
where the time goes in v2:
time: 149 us; the launch traced here: 148 us
  waiting for transfers between devices  47.9 us (32%)
  starting transfers between devices  46.8 us (31%)
  matrix products  16.9 us (11%)
  blocking collectives  14.6 us (10%)
  local copies, waits for them, and re-layouts  13.3 us (9%)
  Pallas kernels  3.07 us (2%)
  between operations  2.89 us (2%)
  other arithmetic  2.23 us (1%)
    all_to_all x3, waiting for transfers between devices, exchange(): lax.all_to_all(blocks, axis, 0, 0, tiled=True, axis_index_groups=groups)  30.8 us
    all_to_all x3, starting transfers between devices, exchange(): lax.all_to_all(blocks, axis, 0, 0, tiled=True, axis_index_groups=groups)  28.1 us
    ppermute x6, starting transfers between devices, send(): return lax.ppermute(block, ALL, pairs)  18.7 us
    ppermute x6, waiting for transfers between devices, send(): return lax.ppermute(block, ALL, pairs)  17.1 us
    all_to_all x1, blocking collectives, exchange(): lax.all_to_all(blocks, axis, 0, 0, tiled=True, axis_index_groups=groups)  14.6 us
    dot_general x2, matrix products, rows_first(): lax.dot_general(left, right, (((0,), (0,)), ((), ())), preferred_element_...  8.7 us
    unnamed x29, local copies, waits for them, and re-layouts  7.59 us
    dot_general x2, matrix products, forward(): jnp.dot(part, head_in[0], preferred_element_type=f32)  6.92 us
  transfers between devices with their start and end apart: 9, of which 5 were waited for; matrix products, arithmetic and copies ran while one was open for 12% of the time, Pallas kernels for 1%

profile of v2, /device:TPU:1, one launch (start us, length us, event | category | flops | bytes accessed | tf_op | source)
XLA Modules:
  0.0 147.7 jit_solution(9271813160237357221)
XLA Ops:
  0.6 0.0 copy-start
  0.6 2.1 %broadcast_in_dim.10 = bf16[32,2,4096]{2,1,0:T(2,128)(2,1)} broadcast(bf16[2,4096]{1,0:T(2,128)(2,1)} %param.11), dimensions={1,2} | broadcast | bytes 540672 | tf_op jit(solution)/shard_map/broadcast_in_dim | solution.py:69
  2.7 18.2 %all-to-all-start = ((bf16[32,2,4096]{2,1,0:T(2,128)(2,1)}), bf16[32,2,4096]{2,1,0:T(2,128)(2,1)S(1)}, u32[]{:S(2)}, u32[]{:S(2)}) async-start(bf16[32,2,4096]{2,1,0:T(2,128)(2,1)} %broadcast_in_dim.10), calls=%async_computation | async-start | bytes 1048576 | tf_op jit(solution)/shard_map/all_to_all | solution.py:65
  20.9 0.9 copy.24
  21.8 0.8 copy.23
  22.5 0.7 broadcast_bitcast_fusion
  23.2 0.1 fusion.15
  23.3 0.9 fusion.1
  24.2 16.4 %all-to-all-done = bf16[32,2,4096]{2,1,0:T(2,128)(2,1)S(1)} async-done(((bf16[32,2,4096]{2,1,0:T(2,128)(2,1)}), bf16[32,2,4096]{2,1,0:T(2,128)(2,1)S(1)}, u32[]{:S(2)}, u32[]{:S(2)}) %all-to-all-start) | async-done | bytes 524320 | tf_op jit(solution)/shard_map/all_to_all | solution.py:65
  40.6 0.2 reshape.232
  40.8 0.0 copy-start.6
  40.8 4.2 %collective-permute-start = (bf16[64,4096]{1,0:T(8,128)(2,1)S(1)}, bf16[64,4096]{1,0:T(8,128)(2,1)S(1)}, u32[]{:S(2)}, u32[]{:S(2)}) collective-permute-start(bf16[64,4096]{1,0:T(8,128)(2,1)S(1)} %reshape.232), channel_id=1, source_target_pairs={{0,64},{1,65},{2,66},{3,67},{4,68},{5,69},{6,70},{7,71},{8,72},{9,... | collective-permute-start | bytes 1572872 | tf_op jit(solution)/shard_map/ppermute | solution.py:74
  45.0 0.9 constant_dynamic-update-slice_fusion.7
  45.9 0.6 collective-permute-done
  46.5 0.9 constant_dynamic-update-slice_fusion.6
  47.4 1.9 %collective-permute-start.1 = (bf16[128,4096]{1,0:T(8,128)(2,1)S(1)}, bf16[128,4096]{1,0:T(8,128)(2,1)S(1)}, u32[]{:S(2)}, u32[]{:S(2)}) collective-permute-start(bf16[128,4096]{1,0:T(8,128)(2,1)S(1)} %get-tuple-element.16), channel_id=1, source_target_pairs={{16,0},{17,1},{18,2},{19,3},{20,4},{21,5},{22,6},{23,7},{24,8},{25... | collective-permute-start | bytes 3145736 | tf_op jit(solution)/shard_map/ppermute | solution.py:74
  49.3 3.0 %collective-permute-start.2 = (bf16[128,4096]{1,0:T(8,128)(2,1)S(1)}, bf16[128,4096]{1,0:T(8,128)(2,1)S(1)}, u32[]{:S(2)}, u32[]{:S(2)}) collective-permute-start(bf16[128,4096]{1,0:T(8,128)(2,1)S(1)} %get-tuple-element.16), channel_id=1, source_target_pairs={{128,0},{129,1},{130,2},{131,3},{132,4},{133,5},{134,6},{135,7},{1... | collective-permute-start | bytes 3145736 | tf_op jit(solution)/shard_map/ppermute | solution.py:74
  52.3 3.2 %collective-permute-start.3 = (bf16[128,4096]{1,0:T(8,128)(2,1)S(1)}, bf16[128,4096]{1,0:T(8,128)(2,1)S(1)}, u32[]{:S(2)}, u32[]{:S(2)}) collective-permute-start(bf16[128,4096]{1,0:T(8,128)(2,1)S(1)} %get-tuple-element.16), channel_id=1, source_target_pairs={{1,0},{2,1},{3,2},{4,3},{5,4},{6,5},{7,6},{0,7},{9,8},{10,9},{11,1... | collective-permute-start | bytes 3145736 | tf_op jit(solution)/shard_map/ppermute | solution.py:74
  55.5 2.7 %collective-permute-start.4 = (bf16[64,4096]{1,0:T(8,128)(2,1)}, bf16[64,4096]{1,0:T(8,128)(2,1)S(1)}, u32[]{:S(2)}, u32[]{:S(2)}) collective-permute-start(bf16[64,4096]{1,0:T(8,128)(2,1)} %copy-done.6), channel_id=1, source_target_pairs={{129,0},{130,1},{131,2},{132,3},{133,4},{134,5},{135,6},{128,7},{1... | collective-permute-start | bytes 1572872 | tf_op jit(solution)/shard_map/ppermute | solution.py:74
  58.2 15.0 %collective-permute-done.4 = bf16[64,4096]{1,0:T(8,128)(2,1)S(1)} collective-permute-done((bf16[64,4096]{1,0:T(8,128)(2,1)}, bf16[64,4096]{1,0:T(8,128)(2,1)S(1)}, u32[]{:S(2)}, u32[]{:S(2)}) %collective-permute-start.4) | collective-permute-done | bytes 524320 | tf_op jit(solution)/shard_map/ppermute | solution.py:74
  73.2 0.0 collective-permute-done.1
  73.2 0.0 collective-permute-done.2
  73.2 1.5 %collective-permute-done.3 = bf16[128,4096]{1,0:T(8,128)(2,1)S(1)} collective-permute-done((bf16[128,4096]{1,0:T(8,128)(2,1)S(1)}, bf16[128,4096]{1,0:T(8,128)(2,1)S(1)}, u32[]{:S(2)}, u32[]{:S(2)}) %collective-permute-start.3) | collective-permute-done | bytes 1048608 | tf_op jit(solution)/shard_map/ppermute | solution.py:74
  74.7 1.0 copy-done.2
  75.7 2.1 %pad_maximum_fusion = bf16[448,4096]{1,0:T(8,128)(2,1)} fusion(bf16[64,4096]{1,0:T(8,128)(2,1)S(1)} %collective-permute-done.4, bf16[128,4096]{1,0:T(8,128)(2,1)S(1)} %collective-permute-done.3, bf16[128,4096]{1,0:T(8,128)(2,1)S(1)} %collective-permute-done.2, bf16[128,4096]{1,0:T(8,128)(2,1)S(1)} %collective-permute-done.1), kind=kLoop, calls=%fused_computation.3 | loop fusion | flops 14680064 | bytes 7340032 | tf_op jit(solution)/shard_map/concatenate | solution.py:151
  77.8 3.7 %collective-permute-start.5 = (bf16[448,4096]{1,0:T(8,128)(2,1)}, bf16[448,4096]{1,0:T(8,128)(2,1)}, u32[]{:S(2)}, u32[]{:S(2)}) collective-permute-start(bf16[448,4096]{1,0:T(8,128)(2,1)} %pad_maximum_fusion), channel_id=1, source_target_pairs={{0,64},{1,65},{2,66},{3,67},{4,68},{5,69},{6,70},{7,71},{8,72},{9,... | collective-permute-start | bytes 11010056 | tf_op jit(solution)/shard_map/ppermute | solution.py:74
  81.6 0.6 copy.20
  82.2 4.7 %all-to-all-start.1 = ((bf16[8,32,128]{2,1,0:T(8,128)(2,1)}), bf16[8,32,128]{2,1,0:T(8,128)(2,1)S(1)}, u32[]{:S(2)}, u32[]{:S(2)}) async-start(bf16[8,32,128]{2,1,0:T(8,128)(2,1)} %copy.20), calls=%async_computation.1 | async-start | bytes 131072 | tf_op jit(solution)/shard_map/all_to_all | solution.py:65
  87.0 1.0 constant_dynamic-update-slice_fusion.5
  88.0 1.1 constant_dynamic-update-slice_fusion.4
  89.1 1.0 constant_dynamic-update-slice_fusion.3
  90.1 0.8 constant_dynamic-update-slice_fusion.2
  91.0 3.7 %fusion.10 = (f32[576,128]{1,0:T(8,128)S(1)}, bf16[576,128]{1,0:T(8,128)(2,1)S(1)}) fusion(f32[128]{0:T(128)S(1)} %bitcast.62, bf16[576,4096]{1,0:T(8,128)(2,1)} %constant_dynamic-update-slice_fusion.2, bf16[1,4096,128]{2,1,0:T(8,128)(2,1)S(1)} %copy-done), kind=kOutput, calls=%fused_computation.18 | convolution fusion | flops 604790784 | bytes 6210048 | tf_op jit(solution)/shard_map/dot_general | solution.py:162
  94.7 0.0 copy-start.1
  94.7 0.0 copy-start.7
  94.8 0.0 collective-permute-done.5
  94.8 3.2 %fusion.14 = (f32[448,128]{1,0:T(8,128)S(1)}, bf16[448,128]{1,0:T(8,128)(2,1)S(1)}) fusion(f32[128]{0:T(128)S(1)} %bitcast.63, bf16[448,4096]{1,0:T(8,128)(2,1)} %collective-permute-done.5, bf16[1,4096,128]{2,1,0:T(8,128)(2,1)S(1)} %copy-done), kind=kOutput, calls=%fused_computation.24 | convolution fusion | flops 470392832 | bytes 5063168 | tf_op jit(solution)/shard_map/dot_general | solution.py:162
  98.0 1.6 %shard_map.130 = f32[8,16,8,128]{3,2,1,0:T(8,128)} custom-call(s32[16]{0:T(128)S(1)} %fusion.21.spots, bf16[576,128]{1,0:T(8,128)(2,1)S(1)} %get-tuple-element.20.direct.hidden_d, bf16[448,128]{1,0:T(8,128)(2,1)S(1)} %get-tuple-element.22.swapped.hidden_s, bf16[128,128]{1,0:T(8,128)(2,1)S(1)} %bitcast.49), custom_call_target="tpu_custom_call" | custom-call | tf_op jit(solution)/shard_map/pallas_call | solution.py:113
  99.5 5.2 %all-to-all-start.2 = ((f32[8,128,128]{2,1,0:T(8,128)}), f32[8,128,128]{2,1,0:T(8,128)S(1)}, u32[]{:S(2)}, u32[]{:S(2)}) async-start(f32[8,128,128]{2,1,0:T(8,128)} %bitcast.10), calls=%async_computation.2 | async-start | bytes 1048576 | tf_op jit(solution)/shard_map/all_to_all | solution.py:65
  104.7 0.6 constant_dynamic-slice_fusion
  107.3 0.7 dynamic-slice_bitcast_fusion
  108.0 0.2 fusion.16
  108.2 14.5 %all-to-all-done.2 = f32[8,128,128]{2,1,0:T(8,128)S(1)} async-done(((f32[8,128,128]{2,1,0:T(8,128)}), f32[8,128,128]{2,1,0:T(8,128)S(1)}, u32[]{:S(2)}, u32[]{:S(2)}) %all-to-all-start.2) | async-done | bytes 524320 | tf_op jit(solution)/shard_map/all_to_all | solution.py:65
  122.7 0.2 fusion.4
  122.9 14.6 %all_to_all.20.back = bf16[8,128,128]{2,1,0:T(8,128)(2,1)S(1)} all-to-all(bf16[8,128,128]{2,1,0:T(8,128)(2,1)S(1)} %broadcast_in_dim.12), channel_id=1, replica_groups={{0,1,2,3,4,5,6,7},{8,9,10,11,12,13,14,15},{16,17,18,19,20,21,22,23},{24..., dimensions={0} | all-to-all | bytes 524288 | tf_op jit(solution)/shard_map/all_to_all | solution.py:65
  137.5 1.5 %shard_map.131 = (bf16[576,128]{1,0:T(8,128)(2,1)S(1)}, bf16[448,128]{1,0:T(8,128)(2,1)S(1)}, f32[1,128]{1,0:T(1,128)}, f32[128,128]{1,0:T(8,128)}) custom-call(s32[16]{0:T(128)S(1)} %fusion.21.spots, bf16[8,128,128]{2,1,0:T(8,128)(2,1)S(1)} %all_to_all.20.back, bf16[576,128]{1,0:T(8,128)(2,1)S(1)} %get-tuple-element.20.direct.hidden_d, ...), custom_call_target="tpu_custom_call" | custom-call | tf_op jit(solution)/shard_map/pallas_call | solution.py:113
  139.0 3.4 %fusion.38 = f32[4096,128]{1,0:T(8,128)S(1)} fusion(bf16[448,4096]{1,0:T(8,128)(2,1)} %collective-permute-done.5, bf16[448,128]{1,0:T(8,128)(2,1)S(1)} %get-tuple-element.12), kind=kOutput, calls=%fused_computation.91 | convolution fusion | flops 469762048 | bytes 5881856 | tf_op jit(solution)/shard_map/dot_general | solution.py:186
  142.4 5.3 %fusion = f32[1,4096,128]{2,1,0:T(8,128)} fusion(f32[4096,128]{1,0:T(8,128)S(1)} %fusion.38, bf16[576,4096]{1,0:T(8,128)(2,1)} %constant_dynamic-update-slice_fusion.2, bf16[576,128]{1,0:T(8,128)(2,1)S(1)} %get-tuple-element.11), kind=kOutput, calls=%fused_computation.1 | convolution fusion | flops 604504064 | bytes 9060352 | tf_op jit(solution)/shard_map/dot_general | solution.py:186
  (24 shorter events, 0.1 us)
Async XLA Ops:
  0.6 90.3 %copy-start = (bf16[1,4096,128]{2,1,0:T(8,128)(2,1)S(1)}, bf16[1,4096,128]{2,1,0:T(8,128)(2,1)}, u32[]{:S(2)}) copy-start(bf16[1,4096,128]{2,1,0:T(8,128)(2,1)} %param.12) | copy-start | bytes 3145732
  2.7 37.8 %all-to-all-start = ((bf16[32,2,4096]{2,1,0:T(2,128)(2,1)}), bf16[32,2,4096]{2,1,0:T(2,128)(2,1)S(1)}, u32[]{:S(2)}, u32[]{:S(2)}) async-start(bf16[32,2,4096]{2,1,0:T(2,128)(2,1)} %broadcast_in_dim.10), calls=%async_computation | async-start | bytes 1048576 | tf_op jit(solution)/shard_map/all_to_all | solution.py:65
  40.8 6.7 %copy-start.6 = (bf16[64,4096]{1,0:T(8,128)(2,1)}, bf16[64,4096]{1,0:T(8,128)(2,1)S(1)}, u32[]{:S(2)}) copy-start(bf16[64,4096]{1,0:T(8,128)(2,1)S(1)} %reshape.232) | copy-start | bytes 1572868
  40.8 5.7 %collective-permute-start = (bf16[64,4096]{1,0:T(8,128)(2,1)S(1)}, bf16[64,4096]{1,0:T(8,128)(2,1)S(1)}, u32[]{:S(2)}, u32[]{:S(2)}) collective-permute-start(bf16[64,4096]{1,0:T(8,128)(2,1)S(1)} %reshape.232), channel_id=1, source_target_pairs={{0,64},{1,65},{2,66},{3,67},{4,68},{5,69},{6,70},{7,71},{8,72},{9,... | collective-permute-start | bytes 1572872 | tf_op jit(solution)/shard_map/ppermute | solution.py:74
  45.9 35.7 %copy-start.8 = (s32[16]{0:T(128)S(1)}, s32[16]{0:T(128)}, u32[]{:S(2)}) copy-start(s32[16]{0:T(128)} %constant.194.clone) | copy-start | bytes 196
  45.9 35.7 %copy-start.9 = (s32[16]{0:T(128)S(1)}, s32[16]{0:T(128)}, u32[]{:S(2)}) copy-start(s32[16]{0:T(128)} %constant.195.clone) | copy-start | bytes 196
  47.4 25.8 %collective-permute-start.1 = (bf16[128,4096]{1,0:T(8,128)(2,1)S(1)}, bf16[128,4096]{1,0:T(8,128)(2,1)S(1)}, u32[]{:S(2)}, u32[]{:S(2)}) collective-permute-start(bf16[128,4096]{1,0:T(8,128)(2,1)S(1)} %get-tuple-element.16), channel_id=1, source_target_pairs={{16,0},{17,1},{18,2},{19,3},{20,4},{21,5},{22,6},{23,7},{24,8},{25... | collective-permute-start | bytes 3145736 | tf_op jit(solution)/shard_map/ppermute | solution.py:74
  49.3 23.9 %collective-permute-start.2 = (bf16[128,4096]{1,0:T(8,128)(2,1)S(1)}, bf16[128,4096]{1,0:T(8,128)(2,1)S(1)}, u32[]{:S(2)}, u32[]{:S(2)}) collective-permute-start(bf16[128,4096]{1,0:T(8,128)(2,1)S(1)} %get-tuple-element.16), channel_id=1, source_target_pairs={{128,0},{129,1},{130,2},{131,3},{132,4},{133,5},{134,6},{135,7},{1... | collective-permute-start | bytes 3145736 | tf_op jit(solution)/shard_map/ppermute | solution.py:74
  52.3 22.4 %collective-permute-start.3 = (bf16[128,4096]{1,0:T(8,128)(2,1)S(1)}, bf16[128,4096]{1,0:T(8,128)(2,1)S(1)}, u32[]{:S(2)}, u32[]{:S(2)}) collective-permute-start(bf16[128,4096]{1,0:T(8,128)(2,1)S(1)} %get-tuple-element.16), channel_id=1, source_target_pairs={{1,0},{2,1},{3,2},{4,3},{5,4},{6,5},{7,6},{0,7},{9,8},{10,9},{11,1... | collective-permute-start | bytes 3145736 | tf_op jit(solution)/shard_map/ppermute | solution.py:74
  55.5 17.7 %collective-permute-start.4 = (bf16[64,4096]{1,0:T(8,128)(2,1)}, bf16[64,4096]{1,0:T(8,128)(2,1)S(1)}, u32[]{:S(2)}, u32[]{:S(2)}) collective-permute-start(bf16[64,4096]{1,0:T(8,128)(2,1)} %copy-done.6), channel_id=1, source_target_pairs={{129,0},{130,1},{131,2},{132,3},{133,4},{134,5},{135,6},{128,7},{1... | collective-permute-start | bytes 1572872 | tf_op jit(solution)/shard_map/ppermute | solution.py:74
  73.2 4.6 %copy-start.4 = (bf16[64,4096]{1,0:T(8,128)(2,1)}, bf16[64,4096]{1,0:T(8,128)(2,1)S(1)}, u32[]{:S(2)}) copy-start(bf16[64,4096]{1,0:T(8,128)(2,1)S(1)} %collective-permute-done.4) | copy-start | bytes 1572868
  74.7 1.0 copy-start.2
  77.8 13.2 %copy-start.10 = (f32[1,128]{1,0:T(1,128)S(1)}, f32[1,128]{1,0:T(1,128)}, u32[]{:S(2)}) copy-start(f32[1,128]{1,0:T(1,128)} %param.13) | copy-start | bytes 1540
  77.8 17.0 %collective-permute-start.5 = (bf16[448,4096]{1,0:T(8,128)(2,1)}, bf16[448,4096]{1,0:T(8,128)(2,1)}, u32[]{:S(2)}, u32[]{:S(2)}) collective-permute-start(bf16[448,4096]{1,0:T(8,128)(2,1)} %pad_maximum_fusion), channel_id=1, source_target_pairs={{0,64},{1,65},{2,66},{3,67},{4,68},{5,69},{6,70},{7,71},{8,72},{9,... | collective-permute-start | bytes 11010056 | tf_op jit(solution)/shard_map/ppermute | solution.py:74
  82.2 17.3 %all-to-all-start.1 = ((bf16[8,32,128]{2,1,0:T(8,128)(2,1)}), bf16[8,32,128]{2,1,0:T(8,128)(2,1)S(1)}, u32[]{:S(2)}, u32[]{:S(2)}) async-start(bf16[8,32,128]{2,1,0:T(8,128)(2,1)} %copy.20), calls=%async_computation.1 | async-start | bytes 131072 | tf_op jit(solution)/shard_map/all_to_all | solution.py:65
  87.0 2.1 %copy-start.3 = (bf16[128,4096]{1,0:T(8,128)(2,1)S(1)}, bf16[128,4096]{1,0:T(8,128)(2,1)}, u32[]{:S(2)}) copy-start(bf16[128,4096]{1,0:T(8,128)(2,1)} %copy-done.2) | copy-start | bytes 3145732
  87.0 3.1 %copy-start.5 = (bf16[64,4096]{1,0:T(8,128)(2,1)S(1)}, bf16[64,4096]{1,0:T(8,128)(2,1)}, u32[]{:S(2)}) copy-start(bf16[64,4096]{1,0:T(8,128)(2,1)} %copy-done.4) | copy-start | bytes 1572868
  94.7 3.2 %copy-start.1 = (bf16[1,128,128]{2,1,0:T(8,128)(2,1)S(1)}, bf16[1,128,128]{2,1,0:T(8,128)(2,1)}, u32[]{:S(2)}) copy-start(bf16[1,128,128]{2,1,0:T(8,128)(2,1)} %param.14) | copy-start | bytes 98308
  94.7 9.9 %copy-start.7 = (s32[1,8]{1,0:T(1,128)S(1)}, s32[1,8]{1,0:T(1,128)}, u32[]{:S(2)}) copy-start(s32[1,8]{1,0:T(1,128)} %param.16) | copy-start | bytes 100
  99.5 23.1 %all-to-all-start.2 = ((f32[8,128,128]{2,1,0:T(8,128)}), f32[8,128,128]{2,1,0:T(8,128)S(1)}, u32[]{:S(2)}, u32[]{:S(2)}) async-start(f32[8,128,128]{2,1,0:T(8,128)} %bitcast.10), calls=%async_computation.2 | async-start | bytes 1048576 | tf_op jit(solution)/shard_map/all_to_all | solution.py:65

commit v3 on v2

--- a/solution.py
+++ b/solution.py
@@ -17,7 +17,7 @@
 
 
 def gelu_parts(values):
-    normal_cdf = 0.5 * (1.0 + jax.scipy.special.erf(values * inv_root_two))
+    normal_cdf = 0.5 * (1.0 + lax.erf(values * inv_root_two))
     density = jnp.exp(-0.5 * values * values) * inv_root_two_pi
     return (values * normal_cdf, normal_cdf + values * density)
 
@@ -54,9 +54,8 @@
 
 CLASSES = classes()
 CORES = [(i, i ^ 64) for i in range(512)]
-HELD = [(0, 0), (0, 1), (2, 0), (2, 1), (1, 0), (1, 1), (3, 0), (3, 1), (4, 0)]
-HELD += [(-2, 1), (-2, 0), (-1, 1), (-1, 0), (-3, 1), (-3, 0), (4, 1)]
-DIRECT = 9
+HELD = [(0, 0), (0, 1), (2, 0), (2, 1), (1, 0), (1, 1), (3, 0), (3, 1)]
+HELD += [(-2, 1), (-2, 0), (-1, 1), (-1, 0), (-3, 1), (-3, 0), (4, 0), (4, 1)]
 ALONG_Z = [[8 * j + z for z in range(8)] for j in range(8)]
 ACROSS_Z = [[8 * j + z for j in range(8)] for z in range(8)]
 
@@ -74,15 +73,39 @@
     return lax.ppermute(block, ALL, pairs)
 
 
-def shares_kernel(spots, direct, swapped, head_out, out):
-    for part, start in ((direct, 0), (swapped, DIRECT)):
+def join_kernel(*refs):
+    start = 0
+    for piece in refs[:-1]:
+        refs[-1][start : start + piece.shape[0]] = piece[...]
+        start += piece.shape[0]
+
+
+def forward_kernel(pieces, head_in, bias_in, hidden, slopes):
+    start = 0
+    for piece in pieces:
+        span = slice(start, start + piece.shape[0])
+        start += piece.shape[0]
+        pre = jnp.dot(piece[...], head_in[...], preferred_element_type=jnp.float32) + bias_in[...]
+        activated, slope = gelu_parts(pre)
+        hidden[span] = activated.astype(jnp.bfloat16)
+        slopes[span] = slope
+
+
+def direct_kernel(head_in, bias_in, *refs):
+    forward_kernel(refs[:-2], head_in, bias_in, *refs[-2:])
+
+
+def late_kernel(spots, hidden_d, head_in, bias_in, head_out, *refs):
+    *pieces, hidden_s, slopes_s, out = refs
+    forward_kernel(pieces, head_in, bias_in, hidden_s, slopes_s)
+    for part, start in ((hidden_d, 0), (hidden_s, 8)):
         share = jnp.dot(part[...], head_out[...], preferred_element_type=jnp.float32)
-        for j in range(part.shape[0] // 64):
+        for j in range(8):
             out[:, spots[start + j]] = share[64 * j : 64 * j + 64].reshape(8, 8, A)
 
 
 def backward_kernel(
-    spots, back, hidden_d, hidden_s, slopes_d, slopes_s, head_out, grad_d, grad_s, bias, out, wide, rows
+    spots, back, hidden_d, hidden_s, slopes_d, slopes_s, head_out, grad, bias, out, wide, rows
 ):
     for z in range(8):
         wide[z] = back[z].astype(jnp.float32).reshape(16, 8, A)
@@ -91,15 +114,15 @@
     bias_sum = jnp.zeros((1, A), jnp.float32)
     out_sum = jnp.zeros((A, A), jnp.float32)
     start = 0
-    for hidden, slopes, grad in ((hidden_d, slopes_d, grad_d), (hidden_s, slopes_s, grad_s)):
-        count = hidden.shape[0]
-        res = rows[start : start + count].astype(jnp.bfloat16)
-        start += count
+    for hidden, slopes in ((hidden_d, slopes_d), (hidden_s, slopes_s)):
+        span = slice(start, start + hidden.shape[0])
+        start += hidden.shape[0]
+        res = rows[span].astype(jnp.bfloat16)
         held = lax.dot_general(
             res, head_out[...], (((1,), (1,)), ((), ())), preferred_element_type=jnp.float32
         )
         rounded = (held * slopes[...]).astype(jnp.bfloat16)
-        grad[...] = rounded
+        grad[span] = rounded
         bias_sum += jnp.sum(rounded.astype(jnp.float32), axis=0, keepdims=True)
         out_sum += lax.dot_general(
             hidden[...], res, (((0,), (0,)), ((), ())), preferred_element_type=jnp.float32
@@ -108,16 +131,17 @@
     out[...] = out_sum
 
 
-def call(kernel, outs, operands, scratch=()):
+def call(kernel, outs, operands, spots=None, scratch=()):
     vmem = pl.BlockSpec(memory_space=pltpu.VMEM)
+    first = [] if spots is None else [spots]
     return pl.pallas_call(
         kernel,
         out_shape=[jax.ShapeDtypeStruct(shape, dtype) for shape, dtype in outs],
-        in_specs=[pl.BlockSpec(memory_space=pltpu.SMEM)] + [vmem] * (len(operands) - 1),
+        in_specs=[pl.BlockSpec(memory_space=pltpu.SMEM)] * len(first) + [vmem] * len(operands),
         out_specs=[vmem] * len(outs),
         scratch_shapes=list(scratch),
-        compiler_params=pltpu.CompilerParams(vmem_limit_bytes=32 * 1024 * 1024),
-    )(*operands)
+        compiler_params=pltpu.CompilerParams(vmem_limit_bytes=20 * 1024 * 1024),
+    )(*first, *operands)
 
 
 def local(
@@ -144,13 +168,14 @@
     )
 
     mine = spread(embeddings, ALL, CLASSES).reshape(64, -1)
-    mine, pair = lax.optimization_barrier((mine, pair))
-    both = jnp.concatenate([mine, send(mine, CORES)])
     fourth = send(mine, from_chip(0, 1, 1))
+    (both,) = call(join_kernel, [((128, mine.shape[1]), bf16)], (mine, send(mine, CORES)))
     fetched = [send(both, from_chip(*d)) for d in ((1, 0, 0), (0, 1, 0), (0, 0, 1))]
-    fetched = jnp.concatenate(fetched + [fourth])
-    swapped = send(fetched, CORES)
+    fourth, pair = lax.optimization_barrier((fourth, pair))
     pair = exchange(pair, "fsdp", ACROSS_Z).reshape(8, 2, 16, A)
+    fetched[2], pair = lax.optimization_barrier((fetched[2], pair))
+    direct = [both] + fetched
+    late = [send(piece, CORES) for piece in fetched] + [fourth, send(fourth, CORES)]
 
     r, q = jnp.arange(128, dtype=i32)[:, None], jnp.arange(128, dtype=i32)[None, :]
     row_z = (3 * (r // 16 + 32 - 2 * (z // 2) - z % 2 * 4 - r // 2 % 4)) % 8
@@ -158,34 +183,32 @@
     target = jnp.dot(order, pair[:, 0].reshape(128, A), preferred_element_type=f32)
     measured = jnp.dot(order, pair[:, 1].reshape(128, A), preferred_element_type=f32)
 
-    def forward(*parts):
-        pre = [jnp.dot(part, head_in[0], preferred_element_type=f32) for part in parts]
-        pre = jnp.concatenate(pre) + bias_in[0][None, :]
-        activated, slopes = gelu_parts(pre)
-        return activated.astype(bf16), slopes
-
-    direct = jnp.concatenate([both, fetched])
-    hidden_d, slopes_d = forward(direct)
-    hidden_s, slopes_s = forward(swapped)
-    weights = head_out[0]
-    (shares,) = call(
-        shares_kernel, [((8, 16, 8, A), f32)], (spots, hidden_d, hidden_s, weights)
-    )
+    first, second = head_in[0], head_out[0]
+    activations = [((512, A), bf16), ((512, A), f32)]
+    hidden_d, slopes_d = call(direct_kernel, activations, (first, bias_in, *direct))
+    hidden_s, slopes_s, shares = call(
+        late_kernel,
+        activations + [((8, 16, 8, A), f32)],
+        (hidden_d, first, bias_in, second, *late),
+        spots,
+    )
+    shares, direct, late = lax.optimization_barrier((shares, direct, late))
+    (gathered,) = call(join_kernel, [((1024, first.shape[0]), bf16)], direct + late)
     sums = exchange(shares.reshape(8, 128, A), "fsdp", ALONG_Z).reshape(8, 128, A)
     logits = jnp.sum(sums, axis=0) + bias_slot
     residual = (measured * (logits - target) * scaling).astype(bf16)
+    residual, gathered = lax.optimization_barrier((residual, gathered))
     back = spread(residual, "fsdp", ALONG_Z).reshape(8, 128, A)
-    grad_d, grad_s, bias_in_grad, head_out_grad = call(
+    grad, bias_in_grad, head_out_grad = call(
         backward_kernel,
-        [(hidden_d.shape, bf16), (hidden_s.shape, bf16), ((1, A), f32), ((A, A), f32)],
-        (spots, back, hidden_d, hidden_s, slopes_d, slopes_s, weights),
+        [((1024, A), bf16), ((1, A), f32), ((A, A), f32)],
+        (back, hidden_d, hidden_s, slopes_d, slopes_s, second),
+        spots,
         [pltpu.VMEM((8, 16, 8, A), f32), pltpu.VMEM((1024, A), f32)],
     )
-
-    def rows_first(left, right):
-        return lax.dot_general(left, right, (((0,), (0,)), ((), ())), preferred_element_type=f32)
-
-    head_in_grad = rows_first(direct, grad_d) + rows_first(swapped, grad_s)
+    head_in_grad = lax.dot_general(
+        gathered, grad, (((0,), (0,)), ((), ())), preferred_element_type=f32
+    )
     return head_in_grad[None], bias_in_grad, head_out_grad[None]
 
 

time: 149 us -> 159 us (1.067)
  blocking collectives: 14.6 us -> 65.7 us
  waiting for transfers between devices: 47.9 us -> 21.2 us
  starting transfers between devices: 46.8 us -> 27.9 us
  Pallas kernels: 3.07 us -> 10.7 us
  matrix products: 16.9 us -> 9.84 us
  local copies, waits for them, and re-layouts: 13.3 us -> 17.6 us
    all_to_all x1 -> x3, blocking collectives: 14.6 us -> 65.7 us  [exchange(): lax.all_to_all(blocks, axis, 0, 0, tiled=True, axis_index_groups=groups)]
    all_to_all x3 -> x1, waiting for transfers between devices: 30.8 us -> 6.96 us  [exchange(): lax.all_to_all(blocks, axis, 0, 0, tiled=True, axis_index_groups=groups)]
    all_to_all x3 -> x1, starting transfers between devices: 28.1 us -> 4.2 us  [exchange(): lax.all_to_all(blocks, axis, 0, 0, tiled=True, axis_index_groups=groups)]
    dot_general x4 -> x1, matrix products: 15.6 us -> 7.09 us  [local(): lax.dot_general(gathered, grad, (((0,), (0,)), ((), ())), preferred_eleme...]
    pallas_call x2 -> x5, Pallas kernels: 3.07 us -> 10.7 us  [call(): pl.pallas_call(kernel, out_shape=[jax.ShapeDtypeStruct(shape, dtype) for...]
    unnamed x29 -> x32, local copies, waits for them, and re-layouts: 7.59 us -> 13.5 us
    ppermute x6 -> x9, starting transfers between devices: 18.7 us -> 23.7 us  [send(): return lax.ppermute(block, ALL, pairs)]
    ppermute x6 -> x9, waiting for transfers between devices: 17.1 us -> 14.2 us  [send(): return lax.ppermute(block, ALL, pairs)]
  transfers between devices with their start and end apart: 9 -> 10, of which waited for: 5 -> 3; matrix products, arithmetic and copies ran while one was open for 12% -> 4% of each run, Pallas kernels for 1% -> 4%
where the time goes in v3:
time: 159 us; the launch traced here: 158 us
  blocking collectives  65.7 us (41%)
  starting transfers between devices  27.9 us (18%)
  waiting for transfers between devices  21.2 us (13%)
  local copies, waits for them, and re-layouts  17.6 us (11%)
  Pallas kernels  10.7 us (7%)
  matrix products  9.84 us (6%)
  between operations  2.95 us (2%)
  other arithmetic  1.88 us (1%)
    all_to_all x3, blocking collectives, exchange(): lax.all_to_all(blocks, axis, 0, 0, tiled=True, axis_index_groups=groups)  65.7 us
    ppermute x9, starting transfers between devices, send(): return lax.ppermute(block, ALL, pairs)  23.7 us
    ppermute x9, waiting for transfers between devices, send(): return lax.ppermute(block, ALL, pairs)  14.2 us
    unnamed x32, local copies, waits for them, and re-layouts  13.5 us
    pallas_call x5, Pallas kernels, call(): pl.pallas_call(kernel, out_shape=[jax.ShapeDtypeStruct(shape, dtype) for...  10.7 us
    dot_general x1, matrix products, local(): lax.dot_general(gathered, grad, (((0,), (0,)), ((), ())), preferred_eleme...  7.09 us
    all_to_all x1, waiting for transfers between devices, exchange(): lax.all_to_all(blocks, axis, 0, 0, tiled=True, axis_index_groups=groups)  6.96 us
    all_to_all x1, starting transfers between devices, exchange(): lax.all_to_all(blocks, axis, 0, 0, tiled=True, axis_index_groups=groups)  4.2 us
  transfers between devices with their start and end apart: 10, of which 3 were waited for; matrix products, arithmetic and copies ran while one was open for 4% of the time, Pallas kernels for 4%

profile of v3, /device:TPU:1, one launch (start us, length us, event | category | flops | bytes accessed | tf_op | source)
XLA Modules:
  0.0 157.8 jit_solution(12638064206475676214)
XLA Ops:
  0.6 0.0 copy-start
  0.6 0.0 copy-start.13
  0.7 1.2 broadcast_in_dim.10
  1.9 37.6 %all_to_all.20 = bf16[32,2,4096]{2,1,0:T(2,128)(2,1)S(1)} all-to-all(bf16[32,2,4096]{2,1,0:T(2,128)(2,1)S(1)} %broadcast_in_dim.10), channel_id=1, replica_groups={{0,133,258,391,12,137,270,395,18,151,276,401,30,155,280,413,36,161,294,..., dimensions={0} | all-to-all | bytes 1048576 | tf_op jit(solution)/shard_map/all_to_all | solution.py:64
  39.5 0.2 reshape.232.refs_0_
  39.7 4.2 %collective-permute-start = (bf16[64,4096]{1,0:T(8,128)(2,1)S(1)}, bf16[64,4096]{1,0:T(8,128)(2,1)S(1)}, u32[]{:S(2)}, u32[]{:S(2)}) collective-permute-start(bf16[64,4096]{1,0:T(8,128)(2,1)S(1)} %reshape.232.refs_0_), channel_id=1, source_target_pairs={{0,64},{1,65},{2,66},{3,67},{4,68},{5,69},{6,70},{7,71},{8,72},{9,... | collective-permute-start | bytes 1572872 | tf_op jit(solution)/shard_map/ppermute | solution.py:73
  43.9 1.5 collective-permute-done.refs_1_
  45.4 0.1 shard_map.130.refs_0_
  45.5 2.9 %collective-permute-start.1 = (bf16[128,4096]{1,0:T(8,128)(2,1)S(1)}, bf16[128,4096]{1,0:T(8,128)(2,1)S(1)}, u32[]{:S(2)}, u32[]{:S(2)}) collective-permute-start(bf16[128,4096]{1,0:T(8,128)(2,1)S(1)} %shard_map.130.refs_0_), channel_id=1, source_target_pairs={{1,0},{2,1},{3,2},{4,3},{5,4},{6,5},{7,6},{0,7},{9,8},{10,9},{11,1... | collective-permute-start | bytes 3145736 | tf_op jit(solution)/shard_map/ppermute | solution.py:73
  48.4 2.1 %collective-permute-start.4 = (bf16[128,4096]{1,0:T(8,128)(2,1)S(1)}, bf16[128,4096]{1,0:T(8,128)(2,1)S(1)}, u32[]{:S(2)}, u32[]{:S(2)}) collective-permute-start(bf16[128,4096]{1,0:T(8,128)(2,1)S(1)} %shard_map.130.refs_0_), channel_id=1, source_target_pairs={{128,0},{129,1},{130,2},{131,3},{132,4},{133,5},{134,6},{135,7},{1... | collective-permute-start | bytes 3145736 | tf_op jit(solution)/shard_map/ppermute | solution.py:73
  50.4 3.2 %collective-permute-start.3 = (bf16[128,4096]{1,0:T(8,128)(2,1)S(1)}, bf16[128,4096]{1,0:T(8,128)(2,1)}, u32[]{:S(2)}, u32[]{:S(2)}) collective-permute-start(bf16[128,4096]{1,0:T(8,128)(2,1)S(1)} %shard_map.130.refs_0_), channel_id=1, source_target_pairs={{16,0},{17,1},{18,2},{19,3},{20,4},{21,5},{22,6},{23,7},{24,8},{25... | collective-permute-start | bytes 3145736 | tf_op jit(solution)/shard_map/ppermute | solution.py:73
  53.6 2.7 %collective-permute-start.2 = (bf16[64,4096]{1,0:T(8,128)(2,1)}, bf16[64,4096]{1,0:T(8,128)(2,1)}, u32[]{:S(2)}, u32[]{:S(2)}) collective-permute-start(bf16[64,4096]{1,0:T(8,128)(2,1)} %copy-done.4), channel_id=1, source_target_pairs={{129,0},{130,1},{131,2},{132,3},{133,4},{134,5},{135,6},{128,7},{1... | collective-permute-start | bytes 1572872 | tf_op jit(solution)/shard_map/ppermute | solution.py:73
  56.3 0.7 broadcast_bitcast_fusion
  57.0 0.8 copy.23
  57.8 0.9 copy.24
  58.6 0.1 fusion.4
  58.7 0.9 fusion
  59.6 12.7 %collective-permute-done.2.refs_3_.refs_7_ = bf16[64,4096]{1,0:T(8,128)(2,1)} collective-permute-done((bf16[64,4096]{1,0:T(8,128)(2,1)}, bf16[64,4096]{1,0:T(8,128)(2,1)}, u32[]{:S(2)}, u32[]{:S(2)}) %collective-permute-start.2) | collective-permute-done | bytes 524320 | tf_op jit(solution)/shard_map/ppermute | solution.py:73
  72.3 13.5 %all_to_all.21 = bf16[8,32,128]{2,1,0:T(8,128)(2,1)} all-to-all(bf16[8,32,128]{2,1,0:T(8,128)(2,1)S(1)} %copy.20), channel_id=1, replica_groups={{0,8,16,24,32,40,48,56},{1,9,17,25,33,41,49,57},{2,10,18,26,34,42,50,58..., dimensions={0} | all-to-all | bytes 131072 | tf_op jit(solution)/shard_map/all_to_all | solution.py:64
  85.8 2.5 %collective-permute-start.6 = (bf16[128,4096]{1,0:T(8,128)(2,1)S(1)}, bf16[128,4096]{1,0:T(8,128)(2,1)}, u32[]{:S(2)}, u32[]{:S(2)}) collective-permute-start(bf16[128,4096]{1,0:T(8,128)(2,1)S(1)} %collective-permute-done.4.refs_2_), channel_id=1, source_target_pairs={{0,64},{1,65},{2,66},{3,67},{4,68},{5,69},{6,70},{7,71},{8,72},{9,... | collective-permute-start | bytes 3145736 | tf_op jit(solution)/shard_map/ppermute | solution.py:73
  88.3 1.9 %collective-permute-start.5 = (bf16[128,4096]{1,0:T(8,128)(2,1)}, bf16[128,4096]{1,0:T(8,128)(2,1)}, u32[]{:S(2)}, u32[]{:S(2)}) collective-permute-start(bf16[128,4096]{1,0:T(8,128)(2,1)} %collective-permute-done.3.refs_1_), channel_id=1, source_target_pairs={{0,64},{1,65},{2,66},{3,67},{4,68},{5,69},{6,70},{7,71},{8,72},{9,... | collective-permute-start | bytes 3145736 | tf_op jit(solution)/shard_map/ppermute | solution.py:73
  90.2 2.4 %collective-permute-start.7 = (bf16[128,4096]{1,0:T(8,128)(2,1)S(1)}, bf16[128,4096]{1,0:T(8,128)(2,1)}, u32[]{:S(2)}, u32[]{:S(2)}) collective-permute-start(bf16[128,4096]{1,0:T(8,128)(2,1)S(1)} %collective-permute-done.1.refs_3_), channel_id=1, source_target_pairs={{0,64},{1,65},{2,66},{3,67},{4,68},{5,69},{6,70},{7,71},{8,72},{9,... | collective-permute-start | bytes 3145736 | tf_op jit(solution)/shard_map/ppermute | solution.py:73
  92.7 1.9 %collective-permute-start.8 = (bf16[64,4096]{1,0:T(8,128)(2,1)}, bf16[64,4096]{1,0:T(8,128)(2,1)}, u32[]{:S(2)}, u32[]{:S(2)}) collective-permute-start(bf16[64,4096]{1,0:T(8,128)(2,1)} %collective-permute-done.2.refs_3_.refs_7_), channel_id=1, source_target_pairs={{0,64},{1,65},{2,66},{3,67},{4,68},{5,69},{6,70},{7,71},{8,72},{9,... | collective-permute-start | bytes 1572872 | tf_op jit(solution)/shard_map/ppermute | solution.py:73
  94.7 0.7 fusion.10.spots
  95.4 1.2 copy-done.2
  96.6 0.7 copy-done.12
  97.2 2.5 %shard_map.131 = (bf16[512,128]{1,0:T(8,128)(2,1)S(1)}, f32[512,128]{1,0:T(8,128)S(1)}) custom-call(bf16[4096,128]{1,0:T(8,128)(2,1)S(1)} %bitcast.37, f32[1,128]{1,0:T(1,128)S(1)} %copy-done.12, bf16[128,4096]{1,0:T(8,128)(2,1)S(1)} %shard_map.130.refs_0_, bf16[128,4096]{1,0:T(8,128)(2,1)} %collective-permute-done.3.refs_1_, ...), custom_call_target="tpu_custom_call" | custom-call | tf_op jit(solution)/shard_map/pallas_call | solution.py:137
  99.8 1.2 copy-done.3
  101.1 0.8 copy-done.8
  101.8 3.6 %shard_map.132 = (bf16[512,128]{1,0:T(8,128)(2,1)S(1)}, f32[512,128]{1,0:T(8,128)S(1)}, f32[8,16,8,128]{3,2,1,0:T(8,128)S(1)}) custom-call(s32[16]{0:T(128)S(1)} %fusion.10.spots, bf16[512,128]{1,0:T(8,128)(2,1)S(1)} %get-tuple-element.30.hidden_d, bf16[4096,128]{1,0:T(8,128)(2,1)S(1)} %bitcast.38, f32[1,128]{1,0:T(1,128)S(1)} %copy-done.13, ...), custom_call_target="tpu_custom_call" | custom-call | tf_op jit(solution)/shard_map/pallas_call | solution.py:137
  105.4 0.8 copy-done.5
  106.2 0.7 copy-done.6
  106.9 0.6 copy-done.10
  107.6 4.2 %all-to-all-start.2 = ((f32[8,128,128]{2,1,0:T(8,128)}), f32[8,128,128]{2,1,0:T(8,128)}, u32[]{:S(2)}, u32[]{:S(2)}) async-start(f32[8,128,128]{2,1,0:T(8,128)} %bitcast.39), calls=%async_computation.2 | async-start | bytes 1048576 | tf_op jit(solution)/shard_map/all_to_all | solution.py:64
  111.8 0.6 constant_dynamic-slice_fusion
  114.4 1.4 fusion.26
  115.8 0.8 fusion.5
  116.6 3.0 %shard_map.133 = bf16[1024,4096]{1,0:T(8,128)(2,1)S(1)} custom-call(bf16[128,4096]{1,0:T(8,128)(2,1)S(1)} %shard_map.130.refs_0_, bf16[128,4096]{1,0:T(8,128)(2,1)} %collective-permute-done.3.refs_1_, bf16[128,4096]{1,0:T(8,128)(2,1)S(1)} %collective-permute-done.4.refs_2_, bf16[128,4096]{1,0:T(8,128)(2,1)S(1)} %collective-permute-done.1.refs_3_, ...), custom_call_target="tpu_custom_call" | custom-call | tf_op jit(solution)/shard_map/pallas_call | solution.py:137
  119.6 3.3 %copy-done.1 = bf16[1024,4096]{1,0:T(8,128)(2,1)} copy-done((bf16[1024,4096]{1,0:T(8,128)(2,1)}, bf16[1024,4096]{1,0:T(8,128)(2,1)S(1)}, u32[]{:S(2)}) %copy-start.1) | copy-done | bytes 8388632
  122.9 7.0 %all-to-all-done.2 = f32[8,128,128]{2,1,0:T(8,128)} async-done(((f32[8,128,128]{2,1,0:T(8,128)}), f32[8,128,128]{2,1,0:T(8,128)}, u32[]{:S(2)}, u32[]{:S(2)}) %all-to-all-start.2) | async-done | bytes 524320 | tf_op jit(solution)/shard_map/all_to_all | solution.py:64
  129.8 1.1 reduce_sum.9
  130.9 1.1 fusion.3
  132.0 14.6 %all_to_all.22.back = bf16[8,128,128]{2,1,0:T(8,128)(2,1)S(1)} all-to-all(bf16[8,128,128]{2,1,0:T(8,128)(2,1)S(1)} %broadcast_in_dim.12), channel_id=1, replica_groups={{0,1,2,3,4,5,6,7},{8,9,10,11,12,13,14,15},{16,17,18,19,20,21,22,23},{24..., dimensions={0} | all-to-all | bytes 524288 | tf_op jit(solution)/shard_map/all_to_all | solution.py:64
  146.6 0.9 copy-done.7
  147.5 0.8 copy-done.9
  148.3 0.9 copy-done.11
  149.2 1.5 shard_map.134
  150.7 7.1 %convolution_bitcast_fusion = f32[1,4096,128]{2,1,0:T(8,128)} fusion(bf16[1024,4096]{1,0:T(8,128)(2,1)} %copy-done.1, bf16[1024,128]{1,0:T(8,128)(2,1)S(1)} %get-tuple-element.48), kind=kOutput, calls=%fused_computation | convolution fusion | flops 1073741824 | bytes 10747904 | tf_op jit(solution)/shard_map/dot_general | solution.py:209
  (29 shorter events, 0.1 us)
Async XLA Ops:
  0.6 113.7 %copy-start = (f32[1024]{0:T(1024)S(1)}, f32[1024]{0:T(1024)}, u32[]{:S(2)}) copy-start(f32[1024]{0:T(1024)} %param.15) | copy-start | bytes 12292
  0.6 99.2 %copy-start.13 = (f32[1,128]{1,0:T(1,128)S(1)}, f32[1,128]{1,0:T(1,128)}, u32[]{:S(2)}) copy-start(f32[1,128]{1,0:T(1,128)} %bias_in.3) | copy-start | bytes 1540
  1.9 109.9 %copy-start.14 = (s32[1,8]{1,0:T(1,128)S(1)}, s32[1,8]{1,0:T(1,128)}, u32[]{:S(2)}) copy-start(s32[1,8]{1,0:T(1,128)} %param.16) | copy-start | bytes 100
  39.7 5.8 %copy-start.4 = (bf16[64,4096]{1,0:T(8,128)(2,1)}, bf16[64,4096]{1,0:T(8,128)(2,1)S(1)}, u32[]{:S(2)}) copy-start(bf16[64,4096]{1,0:T(8,128)(2,1)S(1)} %reshape.232.refs_0_) | copy-start | bytes 1572868
  39.7 5.7 %collective-permute-start = (bf16[64,4096]{1,0:T(8,128)(2,1)S(1)}, bf16[64,4096]{1,0:T(8,128)(2,1)S(1)}, u32[]{:S(2)}, u32[]{:S(2)}) collective-permute-start(bf16[64,4096]{1,0:T(8,128)(2,1)S(1)} %reshape.232.refs_0_), channel_id=1, source_target_pairs={{0,64},{1,65},{2,66},{3,67},{4,68},{5,69},{6,70},{7,71},{8,72},{9,... | collective-permute-start | bytes 1572872 | tf_op jit(solution)/shard_map/ppermute | solution.py:73
  45.5 40.3 %collective-permute-start.1 = (bf16[128,4096]{1,0:T(8,128)(2,1)S(1)}, bf16[128,4096]{1,0:T(8,128)(2,1)S(1)}, u32[]{:S(2)}, u32[]{:S(2)}) collective-permute-start(bf16[128,4096]{1,0:T(8,128)(2,1)S(1)} %shard_map.130.refs_0_), channel_id=1, source_target_pairs={{1,0},{2,1},{3,2},{4,3},{5,4},{6,5},{7,6},{0,7},{9,8},{10,9},{11,1... | collective-permute-start | bytes 3145736 | tf_op jit(solution)/shard_map/ppermute | solution.py:73
  48.4 37.4 %collective-permute-start.4 = (bf16[128,4096]{1,0:T(8,128)(2,1)S(1)}, bf16[128,4096]{1,0:T(8,128)(2,1)S(1)}, u32[]{:S(2)}, u32[]{:S(2)}) collective-permute-start(bf16[128,4096]{1,0:T(8,128)(2,1)S(1)} %shard_map.130.refs_0_), channel_id=1, source_target_pairs={{128,0},{129,1},{130,2},{131,3},{132,4},{133,5},{134,6},{135,7},{1... | collective-permute-start | bytes 3145736 | tf_op jit(solution)/shard_map/ppermute | solution.py:73
  50.4 37.9 %collective-permute-start.3 = (bf16[128,4096]{1,0:T(8,128)(2,1)S(1)}, bf16[128,4096]{1,0:T(8,128)(2,1)}, u32[]{:S(2)}, u32[]{:S(2)}) collective-permute-start(bf16[128,4096]{1,0:T(8,128)(2,1)S(1)} %shard_map.130.refs_0_), channel_id=1, source_target_pairs={{16,0},{17,1},{18,2},{19,3},{20,4},{21,5},{22,6},{23,7},{24,8},{25... | collective-permute-start | bytes 3145736 | tf_op jit(solution)/shard_map/ppermute | solution.py:73
  53.6 18.7 %collective-permute-start.2 = (bf16[64,4096]{1,0:T(8,128)(2,1)}, bf16[64,4096]{1,0:T(8,128)(2,1)}, u32[]{:S(2)}, u32[]{:S(2)}) collective-permute-start(bf16[64,4096]{1,0:T(8,128)(2,1)} %copy-done.4), channel_id=1, source_target_pairs={{129,0},{130,1},{131,2},{132,3},{133,4},{134,5},{135,6},{128,7},{1... | collective-permute-start | bytes 1572872 | tf_op jit(solution)/shard_map/ppermute | solution.py:73
  85.8 14.0 %collective-permute-start.6 = (bf16[128,4096]{1,0:T(8,128)(2,1)S(1)}, bf16[128,4096]{1,0:T(8,128)(2,1)}, u32[]{:S(2)}, u32[]{:S(2)}) collective-permute-start(bf16[128,4096]{1,0:T(8,128)(2,1)S(1)} %collective-permute-done.4.refs_2_), channel_id=1, source_target_pairs={{0,64},{1,65},{2,66},{3,67},{4,68},{5,69},{6,70},{7,71},{8,72},{9,... | collective-permute-start | bytes 3145736 | tf_op jit(solution)/shard_map/ppermute | solution.py:73
  88.3 11.5 %collective-permute-start.5 = (bf16[128,4096]{1,0:T(8,128)(2,1)}, bf16[128,4096]{1,0:T(8,128)(2,1)}, u32[]{:S(2)}, u32[]{:S(2)}) collective-permute-start(bf16[128,4096]{1,0:T(8,128)(2,1)} %collective-permute-done.3.refs_1_), channel_id=1, source_target_pairs={{0,64},{1,65},{2,66},{3,67},{4,68},{5,69},{6,70},{7,71},{8,72},{9,... | collective-permute-start | bytes 3145736 | tf_op jit(solution)/shard_map/ppermute | solution.py:73
  90.2 9.6 %collective-permute-start.7 = (bf16[128,4096]{1,0:T(8,128)(2,1)S(1)}, bf16[128,4096]{1,0:T(8,128)(2,1)}, u32[]{:S(2)}, u32[]{:S(2)}) collective-permute-start(bf16[128,4096]{1,0:T(8,128)(2,1)S(1)} %collective-permute-done.1.refs_3_), channel_id=1, source_target_pairs={{0,64},{1,65},{2,66},{3,67},{4,68},{5,69},{6,70},{7,71},{8,72},{9,... | collective-permute-start | bytes 3145736 | tf_op jit(solution)/shard_map/ppermute | solution.py:73
  92.7 7.1 %collective-permute-start.8 = (bf16[64,4096]{1,0:T(8,128)(2,1)}, bf16[64,4096]{1,0:T(8,128)(2,1)}, u32[]{:S(2)}, u32[]{:S(2)}) collective-permute-start(bf16[64,4096]{1,0:T(8,128)(2,1)} %collective-permute-done.2.refs_3_.refs_7_), channel_id=1, source_target_pairs={{0,64},{1,65},{2,66},{3,67},{4,68},{5,69},{6,70},{7,71},{8,72},{9,... | collective-permute-start | bytes 1572872 | tf_op jit(solution)/shard_map/ppermute | solution.py:73
  95.3 1.2 copy-start.2
  96.6 0.7 copy-start.12
  99.8 1.2 copy-start.3
  101.1 0.8 copy-start.8
  105.4 0.8 copy-start.5
  106.2 0.7 copy-start.6
  106.9 0.6 copy-start.10
  107.6 22.3 %all-to-all-start.2 = ((f32[8,128,128]{2,1,0:T(8,128)}), f32[8,128,128]{2,1,0:T(8,128)}, u32[]{:S(2)}, u32[]{:S(2)}) async-start(f32[8,128,128]{2,1,0:T(8,128)} %bitcast.39), calls=%async_computation.2 | async-start | bytes 1048576 | tf_op jit(solution)/shard_map/all_to_all | solution.py:64
  119.6 3.3 %copy-start.1 = (bf16[1024,4096]{1,0:T(8,128)(2,1)}, bf16[1024,4096]{1,0:T(8,128)(2,1)S(1)}, u32[]{:S(2)}) copy-start(bf16[1024,4096]{1,0:T(8,128)(2,1)S(1)} %shard_map.133) | copy-start | bytes 25165828
  146.6 1.0 copy-start.7
  147.5 0.8 copy-start.9
  148.3 0.9 copy-start.11

commit v4 on v3

v4 whole, which is shorter than its diff:
```python
import math

import jax
import jax.numpy as jnp
from jax import lax
from jax.experimental import pallas as pl
from jax.experimental.pallas import tpu as pltpu
from jax.sharding import Mesh
from jax.sharding import PartitionSpec as P

H = 1024
A = 128
CBLK = 8
TASK, FSDP = ("ylo", "core"), ("x", "yhi", "z")
ALL = TASK + FSDP

inv_root_two = 0.7071067811865476
inv_root_two_pi = 0.3989422804014327


def gelu_parts(values):
    normal_cdf = 0.5 * (1.0 + lax.erf(values * inv_root_two))
    density = jnp.exp(-0.5 * values * values) * inv_root_two_pi
    return (values * normal_cdf, normal_cdf + values * density)


def place(i):
    t, f = divmod(i, 64)
    ylo, core = divmod(t, 2)
    x, rest = divmod(f, 16)
    yhi, z = divmod(rest, 8)
    return x, yhi * 4 + ylo, z, core


def flat(x, y, z, core):
    x, y, z = x % 4, y % 8, z % 8
    return (y % 4 * 2 + core) * 64 + x * 16 + y // 4 * 8 + z


def classes():
    groups = {}
    for i in range(512):
        x, y, z, core = place(i)
        groups.setdefault(((2 * x + y + 3 * z) % 8, core), []).append(i)
    return [sorted(groups[k], key=place) for k in sorted(groups)]


def from_chip(dx, dy, dz):
    pairs = []
    for i in range(512):
        x, y, z, core = place(i)
        s = 1 - 2 * core
        pairs.append((flat(x + s * dx, y + s * dy, z + s * dz, core), i))
    return pairs


CLASSES = classes()
CORES = [(i, i ^ 64) for i in range(512)]
HELD = [(0, 0), (0, 1), (2, 0), (2, 1), (1, 0), (1, 1), (3, 0), (3, 1)]
HELD += [(-2, 1), (-2, 0), (-1, 1), (-1, 0), (-3, 1), (-3, 0), (4, 0), (4, 1)]


def exchange(blocks, axis, groups=None):
    return lax.all_to_all(blocks, axis, 0, 0, tiled=True, axis_index_groups=groups)


def spread(block, axis, count, groups=None):
    return exchange(jnp.broadcast_to(block[None], (count,) + block.shape), axis, groups)


def send(block, pairs):
    return lax.ppermute(block, ALL, pairs)


def join_kernel(*refs):
    start = 0
    for piece in refs[:-1]:
        refs[-1][start : start + piece.shape[0]] = piece[...]
        start += piece.shape[0]


def prepare_kernel(block_owner, block_mask, targets, entry_mask, out):
    row = lax.broadcasted_iota(jnp.int32, (16, A), 0)
    for b in range(8):
        o = block_owner[0, b]
        lanes = pl.ds(pl.multiple_of(o * A, A), A)
        measured = entry_mask[:, lanes] * jnp.where(row < 8, block_mask[0, o], block_mask[1, o])
        out[b, 0] = targets[:, lanes]
        out[b, 1] = measured.astype(jnp.float32).astype(jnp.bfloat16)


def gather_rows_kernel(*refs):
    *pieces, out, sems = refs
    copies, start = [], 0
    for j, piece in enumerate(pieces):
        rows = piece.shape[0]
        copies.append(pltpu.make_async_copy(piece, out.at[pl.ds(start, rows)], sems.at[j]))
        start += rows
    for copy in copies:
        copy.start()
    for copy in copies:
        copy.wait()


def residual_kernel(places, sums, pair, bias_out, out):
    owner, z = places[16], places[17]
    lanes = pl.ds(pl.multiple_of(owner * A, A), A)
    r = lax.broadcasted_iota(jnp.int32, (A, A), 0)
    q = lax.broadcasted_iota(jnp.int32, (A, A), 1)
    row_ylo = (r >> 1) & 3
    row_z = (3 * ((r >> 4) + 32 - 2 * (z >> 1) - 4 * (z & 1) - row_ylo)) & 7
    source = row_ylo * 32 + ((r >> 3) & 1) * 16 + row_z * 2 + (r & 1)
    order = jnp.where(q == source, 1.0, 0.0).astype(jnp.bfloat16)
    target = jnp.dot(
        order, pair[:, 0].reshape(A, A), preferred_element_type=jnp.float32
    )
    measured = jnp.dot(
        order, pair[:, 1].reshape(A, A), preferred_element_type=jnp.float32
    )
    total = sums[0].astype(jnp.float32)
    for j in range(1, 8):
        total = total + sums[j].astype(jnp.float32)
    logits = total + bias_out[:, lanes]
    residual = (measured * (logits - target) * (1.0 / math.sqrt(1024))).astype(jnp.bfloat16)
    for j in range(8):
        out[j] = residual


def forward_kernel(pieces, head_in, bias_in, hidden, slopes):
    start = 0
    for piece in pieces:
        span = slice(start, start + piece.shape[0])
        start += piece.shape[0]
        pre = jnp.dot(piece[...], head_in[...], preferred_element_type=jnp.float32) + bias_in[...]
        activated, slope = gelu_parts(pre)
        hidden[span] = activated.astype(jnp.bfloat16)
        slopes[span] = slope


def direct_kernel(head_in, bias_in, *refs):
    forward_kernel(refs[:-2], head_in, bias_in, *refs[-2:])


def late_kernel(spots, hidden_d, head_in, bias_in, head_out, *refs):
    *pieces, hidden_s, slopes_s, out, wide = refs
    forward_kernel(pieces, head_in, bias_in, hidden_s, slopes_s)
    for part, start in ((hidden_d, 0), (hidden_s, 8)):
        share = jnp.dot(part[...], head_out[...], preferred_element_type=jnp.float32)
        for j in range(8):
            wide[:, spots[start + j]] = share[64 * j : 64 * j + 64].reshape(8, 8, A)
    for z in range(8):
        out[z] = wide[z].reshape(A, A).astype(jnp.bfloat16)


def backward_kernel(
    spots, back, hidden_d, hidden_s, slopes_d, slopes_s, head_out, grad, bias, out, wide, rows
):
    for z in range(8):
        wide[z] = back[z].astype(jnp.float32).reshape(16, 8, A)
    for j in range(16):
        rows[64 * j : 64 * j + 64] = wide[:, spots[j]].reshape(64, A)
    bias_sum = jnp.zeros((1, A), jnp.float32)
    out_sum = jnp.zeros((A, A), jnp.float32)
    start = 0
    for hidden, slopes in ((hidden_d, slopes_d), (hidden_s, slopes_s)):
        span = slice(start, start + hidden.shape[0])
        start += hidden.shape[0]
        res = rows[span].astype(jnp.bfloat16)
        held = lax.dot_general(
            res, head_out[...], (((1,), (1,)), ((), ())), preferred_element_type=jnp.float32
        )
        rounded = (held * slopes[...]).astype(jnp.bfloat16)
        grad[span] = rounded
        bias_sum += jnp.sum(rounded.astype(jnp.float32), axis=0, keepdims=True)
        out_sum += lax.dot_general(
            hidden[...], res, (((0,), (0,)), ((), ())), preferred_element_type=jnp.float32
        )
    bias[...] = bias_sum
    out[...] = out_sum


def call(kernel, outs, operands, *scalars, scratch=()):
    vmem = pl.BlockSpec(memory_space=pltpu.VMEM)
    return pl.pallas_call(
        kernel,
        out_shape=[jax.ShapeDtypeStruct(shape, dtype) for shape, dtype in outs],
        in_specs=[pl.BlockSpec(memory_space=pltpu.SMEM)] * len(scalars) + [vmem] * len(operands),
        out_specs=[vmem] * len(outs),
        scratch_shapes=list(scratch),
        compiler_params=pltpu.CompilerParams(vmem_limit_bytes=10 * 1024 * 1024),
    )(*scalars, *operands)


def local(
    embeddings, head_in, bias_in, head_out, bias_out, block_owner, targets, entry_mask, block_mask
):
    ylo, core, x, yhi, z = [lax.axis_index(name) for name in ALL]
    bf16, f32, i32 = jnp.bfloat16, jnp.float32, jnp.int32

    offset = jnp.array([d for d, _ in HELD], i32) * (1 - 2 * core)
    whose = jnp.array([w for _, w in HELD], i32)
    spots = (2 * x + yhi * 4 + ylo + 3 * z + offset + 16) % 8 * 2 + (whose + core) % 2
    owner = lax.dynamic_index_in_dim(block_owner[0], x * 2 + yhi)
    places = jnp.concatenate([spots, owner, z[None]])

    (pair,) = call(
        prepare_kernel,
        [((8, 2, 16, A), bf16)],
        (targets, entry_mask),
        block_owner,
        block_mask,
    )
    embeddings, pair, places = lax.optimization_barrier((embeddings, pair, places))
    mine = spread(embeddings, ALL, 32, CLASSES).reshape(64, -1)
    fourth = send(mine, from_chip(0, 1, 1))
    mine, pair = lax.optimization_barrier((mine, pair))
    (both,) = call(join_kernel, [((128, mine.shape[1]), bf16)], (mine, send(mine, CORES)))
    fetched = [send(both, from_chip(*d)) for d in ((1, 0, 0), (0, 1, 0), (0, 0, 1))]
    direct = [both] + fetched
    late = [send(piece, CORES) for piece in fetched] + [fourth, send(fourth, CORES)]

    first, second = head_in[0], head_out[0]
    activations = [((512, A), bf16), ((512, A), f32)]
    hidden_d, slopes_d = call(direct_kernel, activations, (first, bias_in, *direct))
    hidden_s, slopes_s, shares = call(
        late_kernel,
        activations + [((8, A, A), bf16)],
        (hidden_d, first, bias_in, second, *late),
        places,
        scratch=[pltpu.VMEM((8, 16, 8, A), f32)],
    )
    shares, direct, late = lax.optimization_barrier((shares, direct, late))
    pair = exchange(pair, ("x", "yhi"))
    held = direct + late
    gathered = pl.pallas_call(
        gather_rows_kernel,
        out_shape=jax.ShapeDtypeStruct((1024, first.shape[0]), bf16),
        in_specs=[pl.BlockSpec(memory_space=pl.ANY)] * len(held),
        out_specs=pl.BlockSpec(memory_space=pl.ANY),
        scratch_shapes=[pltpu.SemaphoreType.DMA((len(held),))],
        compiler_params=pltpu.CompilerParams(vmem_limit_bytes=2 * 1024 * 1024),
    )(*held)
    sums = exchange(shares, "z")
    (copies,) = call(
        residual_kernel, [((8, A, A), bf16)], (sums, pair, bias_out[None]), places
    )
    copies, gathered = lax.optimization_barrier((copies, gathered))
    back = exchange(copies, "z")
    grad, bias_in_grad, head_out_grad = call(
        backward_kernel,
        [((1024, A), bf16), ((1, A), f32), ((A, A), f32)],
        (back, hidden_d, hidden_s, slopes_d, slopes_s, second),
        places,
        scratch=[pltpu.VMEM((8, 16, 8, A), f32), pltpu.VMEM((1024, A), f32)],
    )
    head_in_grad = lax.dot_general(
        gathered, grad, (((0,), (0,)), ((), ())), preferred_element_type=f32
    )
    return head_in_grad[None], bias_in_grad, head_out_grad[None]


def solution(mesh):
    mesh = Mesh(mesh.devices.reshape(4, 2, 4, 2, 8), ALL)
    in_specs = (
        P(ALL, None),
        P(TASK, None, FSDP),
        P(TASK, FSDP),
        P(TASK, FSDP, None),
        P(TASK),
        P(TASK, None),
        P(FSDP, TASK),
        P(FSDP, TASK),
        P(FSDP, TASK),
    )
    out_specs = (P(TASK, None, FSDP), P(TASK, FSDP), P(TASK, FSDP, None))
    return jax.shard_map(local, mesh=mesh, in_specs=in_specs, out_specs=out_specs, check_vma=False)
```

time: 159 us -> 143 us (0.90)
  the two profiles are of different devices: /device:TPU:1 before, /device:TPU:56 now
where the time goes in v4:
time: 143 us; the launch traced here: 142 us
  blocking collectives  49.1 us (34%)
  starting transfers between devices  36.8 us (26%)
  local copies, waits for them, and re-layouts  20.5 us (14%)
  waiting for transfers between devices  14.2 us (10%)
  Pallas kernels  12.2 us (9%)
  matrix products  7.08 us (5%)
    all_to_all x2, blocking collectives, exchange(): lax.all_to_all(blocks, axis, 0, 0, tiled=True, axis_index_groups=groups)  49.1 us
    ppermute x9, starting transfers between devices, send(): return lax.ppermute(block, ALL, pairs)  24.5 us
    unnamed x42, local copies, waits for them, and re-layouts  17.9 us
    all_to_all x2, starting transfers between devices, exchange(): lax.all_to_all(blocks, axis, 0, 0, tiled=True, axis_index_groups=groups)  12.3 us
    pallas_call x6, Pallas kernels, call(): pl.pallas_call(kernel, out_shape=[jax.ShapeDtypeStruct(shape, dtype) for...  9.55 us
    ppermute x9, waiting for transfers between devices, send(): return lax.ppermute(block, ALL, pairs)  8.18 us
    dot_general x1, matrix products, local(): lax.dot_general(gathered, grad, (((0,), (0,)), ((), ())), preferred_eleme...  7.08 us
    all_to_all x2, waiting for transfers between devices, exchange(): lax.all_to_all(blocks, axis, 0, 0, tiled=True, axis_index_groups=groups)  6.04 us
  transfers between devices with their start and end apart: 11, of which 5 were waited for; matrix products, arithmetic and copies ran while one was open for 0% of the time, Pallas kernels for 6%

profile of v4, /device:TPU:56, one launch (start us, length us, event | category | flops | bytes accessed | tf_op | source)
XLA Modules:
  0.0 142.2 jit_solution(8123249088977211047)
XLA Ops:
  0.7 1.2 constant_dynamic-slice_fusion
  1.9 0.7 fusion
  2.6 0.7 pad_add_fusion.spots.places
  3.3 0.8 copy-done.15
  4.1 0.8 copy-done.16
  4.9 0.7 copy-done.19
  5.6 0.7 copy-done.20
  6.2 1.2 shard_map.130
  7.5 1.2 broadcast_in_dim.19
  8.6 36.1 %all_to_all.20 = bf16[32,2,4096]{2,1,0:T(2,128)(2,1)S(1)} all-to-all(bf16[32,2,4096]{2,1,0:T(2,128)(2,1)S(1)} %broadcast_in_dim.19), channel_id=1, replica_groups={{0,133,258,391,12,137,270,395,18,151,276,401,30,155,280,413,36,161,294,..., dimensions={0} | all-to-all | bytes 1048576 | tf_op jit(solution)/shard_map/all_to_all | solution.py:64
  45.0 1.9 %collective-permute-start = (bf16[64,4096]{1,0:T(8,128)(2,1)S(1)}, bf16[64,4096]{1,0:T(8,128)(2,1)S(1)}, u32[]{:S(2)}, u32[]{:S(2)}) collective-permute-start(bf16[64,4096]{1,0:T(8,128)(2,1)S(1)} %reshape.11.refs_0_), channel_id=1, source_target_pairs={{0,64},{1,65},{2,66},{3,67},{4,68},{5,69},{6,70},{7,71},{8,72},{9,... | collective-permute-start | bytes 1572872 | tf_op jit(solution)/shard_map/ppermute | solution.py:72
  46.9 1.9 %collective-permute-done.refs_1_ = bf16[64,4096]{1,0:T(8,128)(2,1)S(1)} collective-permute-done((bf16[64,4096]{1,0:T(8,128)(2,1)S(1)}, bf16[64,4096]{1,0:T(8,128)(2,1)S(1)}, u32[]{:S(2)}, u32[]{:S(2)}) %collective-permute-start) | collective-permute-done | bytes 524320 | tf_op jit(solution)/shard_map/ppermute | solution.py:72
  48.8 0.8 copy-done.3
  49.6 3.2 %collective-permute-start.3 = (bf16[128,4096]{1,0:T(8,128)(2,1)S(1)}, bf16[128,4096]{1,0:T(8,128)(2,1)S(1)}, u32[]{:S(2)}, u32[]{:S(2)}) collective-permute-start(bf16[128,4096]{1,0:T(8,128)(2,1)S(1)} %shard_map.131.refs_0_), channel_id=1, source_target_pairs={{1,0},{2,1},{3,2},{4,3},{5,4},{6,5},{7,6},{0,7},{9,8},{10,9},{11,1... | collective-permute-start | bytes 3145736 | tf_op jit(solution)/shard_map/ppermute | solution.py:72
  52.9 2.5 %collective-permute-start.2 = (bf16[128,4096]{1,0:T(8,128)(2,1)S(1)}, bf16[128,4096]{1,0:T(8,128)(2,1)S(1)}, u32[]{:S(2)}, u32[]{:S(2)}) collective-permute-start(bf16[128,4096]{1,0:T(8,128)(2,1)S(1)} %shard_map.131.refs_0_), channel_id=1, source_target_pairs={{128,0},{129,1},{130,2},{131,3},{132,4},{133,5},{134,6},{135,7},{1... | collective-permute-start | bytes 3145736 | tf_op jit(solution)/shard_map/ppermute | solution.py:72
  55.4 3.0 %collective-permute-start.1 = (bf16[128,4096]{1,0:T(8,128)(2,1)S(1)}, bf16[128,4096]{1,0:T(8,128)(2,1)}, u32[]{:S(2)}, u32[]{:S(2)}) collective-permute-start(bf16[128,4096]{1,0:T(8,128)(2,1)S(1)} %shard_map.131.refs_0_), channel_id=1, source_target_pairs={{16,0},{17,1},{18,2},{19,3},{20,4},{21,5},{22,6},{23,7},{24,8},{25... | collective-permute-start | bytes 3145736 | tf_op jit(solution)/shard_map/ppermute | solution.py:72
  58.4 4.9 %collective-permute-start.7 = (bf16[64,4096]{1,0:T(8,128)(2,1)}, bf16[64,4096]{1,0:T(8,128)(2,1)}, u32[]{:S(2)}, u32[]{:S(2)}) collective-permute-start(bf16[64,4096]{1,0:T(8,128)(2,1)} %copy-done.3), channel_id=1, source_target_pairs={{129,0},{130,1},{131,2},{132,3},{133,4},{134,5},{135,6},{128,7},{1... | collective-permute-start | bytes 1572872 | tf_op jit(solution)/shard_map/ppermute | solution.py:72
  63.3 3.0 %collective-permute-done.3.refs_3_ = bf16[128,4096]{1,0:T(8,128)(2,1)S(1)} collective-permute-done((bf16[128,4096]{1,0:T(8,128)(2,1)S(1)}, bf16[128,4096]{1,0:T(8,128)(2,1)S(1)}, u32[]{:S(2)}, u32[]{:S(2)}) %collective-permute-start.3) | collective-permute-done | bytes 1048608 | tf_op jit(solution)/shard_map/ppermute | solution.py:72
  66.3 2.4 %collective-permute-start.6 = (bf16[128,4096]{1,0:T(8,128)(2,1)S(1)}, bf16[128,4096]{1,0:T(8,128)(2,1)}, u32[]{:S(2)}, u32[]{:S(2)}) collective-permute-start(bf16[128,4096]{1,0:T(8,128)(2,1)S(1)} %collective-permute-done.3.refs_3_), channel_id=1, source_target_pairs={{0,64},{1,65},{2,66},{3,67},{4,68},{5,69},{6,70},{7,71},{8,72},{9,... | collective-permute-start | bytes 3145736 | tf_op jit(solution)/shard_map/ppermute | solution.py:72
  68.7 2.1 %collective-permute-done.2.refs_2_ = bf16[128,4096]{1,0:T(8,128)(2,1)S(1)} collective-permute-done((bf16[128,4096]{1,0:T(8,128)(2,1)S(1)}, bf16[128,4096]{1,0:T(8,128)(2,1)S(1)}, u32[]{:S(2)}, u32[]{:S(2)}) %collective-permute-start.2) | collective-permute-done | bytes 1048608 | tf_op jit(solution)/shard_map/ppermute | solution.py:72
  70.8 1.9 %collective-permute-start.5 = (bf16[128,4096]{1,0:T(8,128)(2,1)S(1)}, bf16[128,4096]{1,0:T(8,128)(2,1)}, u32[]{:S(2)}, u32[]{:S(2)}) collective-permute-start(bf16[128,4096]{1,0:T(8,128)(2,1)S(1)} %collective-permute-done.2.refs_2_), channel_id=1, source_target_pairs={{0,64},{1,65},{2,66},{3,67},{4,68},{5,69},{6,70},{7,71},{8,72},{9,... | collective-permute-start | bytes 3145736 | tf_op jit(solution)/shard_map/ppermute | solution.py:72
  72.7 2.7 %collective-permute-start.4 = (bf16[128,4096]{1,0:T(8,128)(2,1)}, bf16[128,4096]{1,0:T(8,128)(2,1)}, u32[]{:S(2)}, u32[]{:S(2)}) collective-permute-start(bf16[128,4096]{1,0:T(8,128)(2,1)} %collective-permute-done.1.refs_1_), channel_id=1, source_target_pairs={{0,64},{1,65},{2,66},{3,67},{4,68},{5,69},{6,70},{7,71},{8,72},{9,... | collective-permute-start | bytes 3145736 | tf_op jit(solution)/shard_map/ppermute | solution.py:72
  75.4 1.2 collective-permute-done.7.refs_3_.refs_7_
  76.6 1.9 %collective-permute-start.8 = (bf16[64,4096]{1,0:T(8,128)(2,1)}, bf16[64,4096]{1,0:T(8,128)(2,1)}, u32[]{:S(2)}, u32[]{:S(2)}) collective-permute-start(bf16[64,4096]{1,0:T(8,128)(2,1)} %collective-permute-done.7.refs_3_.refs_7_), channel_id=1, source_target_pairs={{0,64},{1,65},{2,66},{3,67},{4,68},{5,69},{6,70},{7,71},{8,72},{9,... | collective-permute-start | bytes 1572872 | tf_op jit(solution)/shard_map/ppermute | solution.py:72
  78.5 8.3 %all-to-all-start.2 = ((bf16[8,2,16,128]{3,2,1,0:T(8,128)(2,1)}), bf16[8,2,16,128]{3,2,1,0:T(8,128)(2,1)S(1)}, u32[]{:S(2)}, u32[]{:S(2)}) async-start(bf16[8,2,16,128]{3,2,1,0:T(8,128)(2,1)} %shard_map.130), calls=%async_computation.2 | async-start | bytes 131072 | tf_op jit(solution)/shard_map/all_to_all | solution.py:64
  86.9 1.2 copy-done.1
  88.1 0.7 copy-done.18
  88.7 2.5 %shard_map.132 = (bf16[512,128]{1,0:T(8,128)(2,1)S(1)}, f32[512,128]{1,0:T(8,128)S(1)}) custom-call(bf16[4096,128]{1,0:T(8,128)(2,1)S(1)} %bitcast.10, f32[1,128]{1,0:T(1,128)S(1)} %copy-done.18, bf16[128,4096]{1,0:T(8,128)(2,1)S(1)} %shard_map.131.refs_0_, bf16[128,4096]{1,0:T(8,128)(2,1)} %collective-permute-done.1.refs_1_, ...), custom_call_target="tpu_custom_call" | custom-call | tf_op jit(solution)/shard_map/pallas_call | solution.py:184
  91.2 0.7 copy-done.5
  92.0 1.2 copy-done.2
  93.2 3.6 %shard_map.133 = (bf16[512,128]{1,0:T(8,128)(2,1)S(1)}, f32[512,128]{1,0:T(8,128)S(1)}, bf16[8,128,128]{2,1,0:T(8,128)(2,1)S(1)}) custom-call(s32[18]{0:T(128)S(1)} %pad_add_fusion.spots.places, bf16[512,128]{1,0:T(8,128)(2,1)S(1)} %get-tuple-element.32.hidden_d, bf16[4096,128]{1,0:T(8,128)(2,1)S(1)} %bitcast.11, f32[1,128]{1,0:T(1,128)S(1)} %copy-done.18, ...), custom_call_target="tpu_custom_call" | custom-call | tf_op jit(solution)/shard_map/pallas_call | solution.py:184
  96.8 0.7 copy-done.4
  97.5 0.7 copy-done.7
  98.2 0.7 copy-done.13
  98.9 0.6 copy-done.9
  99.5 4.0 %all-to-all-start.1 = ((bf16[8,128,128]{2,1,0:T(8,128)(2,1)}), bf16[8,128,128]{2,1,0:T(8,128)(2,1)S(1)}, u32[]{:S(2)}, u32[]{:S(2)}) async-start(bf16[8,128,128]{2,1,0:T(8,128)(2,1)} %copy-done.4), calls=%async_computation.1 | async-start | bytes 524288 | tf_op jit(solution)/shard_map/all_to_all | solution.py:64
  103.5 2.6 %shard_map.135 = bf16[1024,4096]{1,0:T(8,128)(2,1)S(1)} custom-call(bf16[128,4096]{1,0:T(8,128)(2,1)S(1)} %shard_map.131.refs_0_, bf16[128,4096]{1,0:T(8,128)(2,1)} %collective-permute-done.1.refs_1_, bf16[128,4096]{1,0:T(8,128)(2,1)S(1)} %collective-permute-done.2.refs_2_, bf16[128,4096]{1,0:T(8,128)(2,1)S(1)} %collective-permute-done.3.refs_3_, ...), custom_call_target="tpu_custom_call" | custom-call | tf_op jit(solution)/shard_map/pallas_call | solution.py:235
  106.2 3.3 %copy-done = bf16[1024,4096]{1,0:T(8,128)(2,1)} copy-done((bf16[1024,4096]{1,0:T(8,128)(2,1)}, bf16[1024,4096]{1,0:T(8,128)(2,1)S(1)}, u32[]{:S(2)}) %copy-start) | copy-done | bytes 8388632
  109.4 6.0 %all-to-all-done.1.sums = bf16[8,128,128]{2,1,0:T(8,128)(2,1)S(1)} async-done(((bf16[8,128,128]{2,1,0:T(8,128)(2,1)}), bf16[8,128,128]{2,1,0:T(8,128)(2,1)S(1)}, u32[]{:S(2)}, u32[]{:S(2)}) %all-to-all-start.1) | async-done | bytes 262176 | tf_op jit(solution)/shard_map/all_to_all | solution.py:64
  115.5 0.8 copy-done.10
  116.3 0.7 shard_map.134
  117.0 13.0 %all_to_all.21.back = bf16[8,128,128]{2,1,0:T(8,128)(2,1)S(1)} all-to-all(bf16[8,128,128]{2,1,0:T(8,128)(2,1)S(1)} %shard_map.134), channel_id=1, replica_groups=mesh['ylo'=4,'core'=2,'x'=4,'yhi'=2,'z'=8] {'z'}, dimensions={0} | all-to-all | bytes 524288 | tf_op jit(solution)/shard_map/all_to_all | solution.py:64
  130.0 0.9 copy-done.6
  131.0 0.9 copy-done.8
  131.9 0.8 copy-done.12
  132.7 0.9 copy-done.14
  133.6 1.5 %shard_map.136 = (bf16[1024,128]{1,0:T(8,128)(2,1)S(1)}, f32[1,128]{1,0:T(1,128)}, f32[128,128]{1,0:T(8,128)}) custom-call(s32[18]{0:T(128)S(1)} %pad_add_fusion.spots.places, bf16[8,128,128]{2,1,0:T(8,128)(2,1)S(1)} %all_to_all.21.back, bf16[512,128]{1,0:T(8,128)(2,1)S(1)} %get-tuple-element.32.hidden_d, bf16[512,128]{1,0:T(8,128)(2,1)S(1)} %copy-done.14, ...), custom_call_target="tpu_custom_call" | custom-call | tf_op jit(solution)/shard_map/pallas_call | solution.py:184
  135.1 7.1 %convolution_bitcast_fusion = f32[1,4096,128]{2,1,0:T(8,128)} fusion(bf16[1024,4096]{1,0:T(8,128)(2,1)} %copy-done, bf16[1024,128]{1,0:T(8,128)(2,1)S(1)} %get-tuple-element.50), kind=kOutput, calls=%fused_computation | convolution fusion | flops 1073741824 | bytes 10747904 | tf_op jit(solution)/shard_map/dot_general | solution.py:256
  (31 shorter events, 0.3 us)
Async XLA Ops:
  0.6 91.4 %copy-start.11 = (bf16[1,128,128]{2,1,0:T(8,128)(2,1)S(1)}, bf16[1,128,128]{2,1,0:T(8,128)(2,1)}, u32[]{:S(2)}) copy-start(bf16[1,128,128]{2,1,0:T(8,128)(2,1)} %param.14) | copy-start | bytes 98308
  3.3 0.8 copy-start.15
  4.1 0.8 copy-start.16
  4.9 0.7 copy-start.19
  5.6 0.7 copy-start.20
  45.0 3.8 %collective-permute-start = (bf16[64,4096]{1,0:T(8,128)(2,1)S(1)}, bf16[64,4096]{1,0:T(8,128)(2,1)S(1)}, u32[]{:S(2)}, u32[]{:S(2)}) collective-permute-start(bf16[64,4096]{1,0:T(8,128)(2,1)S(1)} %reshape.11.refs_0_), channel_id=1, source_target_pairs={{0,64},{1,65},{2,66},{3,67},{4,68},{5,69},{6,70},{7,71},{8,72},{9,... | collective-permute-start | bytes 1572872 | tf_op jit(solution)/shard_map/ppermute | solution.py:72
  48.8 0.8 copy-start.3
  49.6 16.7 %collective-permute-start.3 = (bf16[128,4096]{1,0:T(8,128)(2,1)S(1)}, bf16[128,4096]{1,0:T(8,128)(2,1)S(1)}, u32[]{:S(2)}, u32[]{:S(2)}) collective-permute-start(bf16[128,4096]{1,0:T(8,128)(2,1)S(1)} %shard_map.131.refs_0_), channel_id=1, source_target_pairs={{1,0},{2,1},{3,2},{4,3},{5,4},{6,5},{7,6},{0,7},{9,8},{10,9},{11,1... | collective-permute-start | bytes 3145736 | tf_op jit(solution)/shard_map/ppermute | solution.py:72
  52.9 17.9 %collective-permute-start.2 = (bf16[128,4096]{1,0:T(8,128)(2,1)S(1)}, bf16[128,4096]{1,0:T(8,128)(2,1)S(1)}, u32[]{:S(2)}, u32[]{:S(2)}) collective-permute-start(bf16[128,4096]{1,0:T(8,128)(2,1)S(1)} %shard_map.131.refs_0_), channel_id=1, source_target_pairs={{128,0},{129,1},{130,2},{131,3},{132,4},{133,5},{134,6},{135,7},{1... | collective-permute-start | bytes 3145736 | tf_op jit(solution)/shard_map/ppermute | solution.py:72
  55.4 17.3 %collective-permute-start.1 = (bf16[128,4096]{1,0:T(8,128)(2,1)S(1)}, bf16[128,4096]{1,0:T(8,128)(2,1)}, u32[]{:S(2)}, u32[]{:S(2)}) collective-permute-start(bf16[128,4096]{1,0:T(8,128)(2,1)S(1)} %shard_map.131.refs_0_), channel_id=1, source_target_pairs={{16,0},{17,1},{18,2},{19,3},{20,4},{21,5},{22,6},{23,7},{24,8},{25... | collective-permute-start | bytes 3145736 | tf_op jit(solution)/shard_map/ppermute | solution.py:72
  58.4 18.2 %collective-permute-start.7 = (bf16[64,4096]{1,0:T(8,128)(2,1)}, bf16[64,4096]{1,0:T(8,128)(2,1)}, u32[]{:S(2)}, u32[]{:S(2)}) collective-permute-start(bf16[64,4096]{1,0:T(8,128)(2,1)} %copy-done.3), channel_id=1, source_target_pairs={{129,0},{130,1},{131,2},{132,3},{133,4},{134,5},{135,6},{128,7},{1... | collective-permute-start | bytes 1572872 | tf_op jit(solution)/shard_map/ppermute | solution.py:72
  66.3 25.7 %collective-permute-start.6 = (bf16[128,4096]{1,0:T(8,128)(2,1)S(1)}, bf16[128,4096]{1,0:T(8,128)(2,1)}, u32[]{:S(2)}, u32[]{:S(2)}) collective-permute-start(bf16[128,4096]{1,0:T(8,128)(2,1)S(1)} %collective-permute-done.3.refs_3_), channel_id=1, source_target_pairs={{0,64},{1,65},{2,66},{3,67},{4,68},{5,69},{6,70},{7,71},{8,72},{9,... | collective-permute-start | bytes 3145736 | tf_op jit(solution)/shard_map/ppermute | solution.py:72
  70.8 21.2 %collective-permute-start.5 = (bf16[128,4096]{1,0:T(8,128)(2,1)S(1)}, bf16[128,4096]{1,0:T(8,128)(2,1)}, u32[]{:S(2)}, u32[]{:S(2)}) collective-permute-start(bf16[128,4096]{1,0:T(8,128)(2,1)S(1)} %collective-permute-done.2.refs_2_), channel_id=1, source_target_pairs={{0,64},{1,65},{2,66},{3,67},{4,68},{5,69},{6,70},{7,71},{8,72},{9,... | collective-permute-start | bytes 3145736 | tf_op jit(solution)/shard_map/ppermute | solution.py:72
  72.7 19.3 %collective-permute-start.4 = (bf16[128,4096]{1,0:T(8,128)(2,1)}, bf16[128,4096]{1,0:T(8,128)(2,1)}, u32[]{:S(2)}, u32[]{:S(2)}) collective-permute-start(bf16[128,4096]{1,0:T(8,128)(2,1)} %collective-permute-done.1.refs_1_), channel_id=1, source_target_pairs={{0,64},{1,65},{2,66},{3,67},{4,68},{5,69},{6,70},{7,71},{8,72},{9,... | collective-permute-start | bytes 3145736 | tf_op jit(solution)/shard_map/ppermute | solution.py:72
  76.6 15.3 %collective-permute-start.8 = (bf16[64,4096]{1,0:T(8,128)(2,1)}, bf16[64,4096]{1,0:T(8,128)(2,1)}, u32[]{:S(2)}, u32[]{:S(2)}) collective-permute-start(bf16[64,4096]{1,0:T(8,128)(2,1)} %collective-permute-done.7.refs_3_.refs_7_), channel_id=1, source_target_pairs={{0,64},{1,65},{2,66},{3,67},{4,68},{5,69},{6,70},{7,71},{8,72},{9,... | collective-permute-start | bytes 1572872 | tf_op jit(solution)/shard_map/ppermute | solution.py:72
  78.5 20.3 %all-to-all-start.2 = ((bf16[8,2,16,128]{3,2,1,0:T(8,128)(2,1)}), bf16[8,2,16,128]{3,2,1,0:T(8,128)(2,1)S(1)}, u32[]{:S(2)}, u32[]{:S(2)}) async-start(bf16[8,2,16,128]{3,2,1,0:T(8,128)(2,1)} %shard_map.130), calls=%async_computation.2 | async-start | bytes 131072 | tf_op jit(solution)/shard_map/all_to_all | solution.py:64
  86.9 1.2 copy-start.1
  88.1 0.7 copy-start.18
  91.2 0.7 copy-start.5
  92.0 1.2 copy-start.2
  96.8 0.7 copy-start.4
  97.5 0.7 copy-start.7
  98.2 0.7 copy-start.13
  98.9 0.6 copy-start.9
  99.5 16.0 %all-to-all-start.1 = ((bf16[8,128,128]{2,1,0:T(8,128)(2,1)}), bf16[8,128,128]{2,1,0:T(8,128)(2,1)S(1)}, u32[]{:S(2)}, u32[]{:S(2)}) async-start(bf16[8,128,128]{2,1,0:T(8,128)(2,1)} %copy-done.4), calls=%async_computation.1 | async-start | bytes 524288 | tf_op jit(solution)/shard_map/all_to_all | solution.py:64
  103.5 12.0 %copy-start.17 = (f32[1024]{0:T(1024)S(1)}, f32[1024]{0:T(1024)}, u32[]{:S(2)}) copy-start(f32[1024]{0:T(1024)} %param.15) | copy-start | bytes 12292
  106.2 3.3 %copy-start = (bf16[1024,4096]{1,0:T(8,128)(2,1)}, bf16[1024,4096]{1,0:T(8,128)(2,1)S(1)}, u32[]{:S(2)}) copy-start(bf16[1024,4096]{1,0:T(8,128)(2,1)S(1)} %shard_map.135) | copy-start | bytes 25165828
  115.5 0.8 copy-start.10
  130.0 1.0 copy-start.6
  131.0 0.9 copy-start.8
  131.9 0.8 copy-start.12
  132.7 0.9 copy-start.14

commit v5 on v4

--- a/solution.py
+++ b/solution.py
@@ -10,7 +10,7 @@
 
 H = 1024
 A = 128
-CBLK = 8
+KEPT = pltpu.HBM
 TASK, FSDP = ("ylo", "core"), ("x", "yhi", "z")
 ALL = TASK + FSDP
 
@@ -89,17 +89,35 @@
         out[b, 1] = measured.astype(jnp.float32).astype(jnp.bfloat16)
 
 
-def gather_rows_kernel(*refs):
-    *pieces, out, sems = refs
-    copies, start = [], 0
-    for j, piece in enumerate(pieces):
-        rows = piece.shape[0]
-        copies.append(pltpu.make_async_copy(piece, out.at[pl.ds(start, rows)], sems.at[j]))
-        start += rows
-    for copy in copies:
-        copy.start()
-    for copy in copies:
-        copy.wait()
+def last_kernel(*refs):
+    *pieces, grad, out, held, sems = refs
+    width = held.shape[2]
+
+    def copies(step):
+        slot, start, made = step % 2, 0, []
+        for j, piece in enumerate(pieces):
+            rows = piece.shape[0]
+            source = piece.at[:, pl.ds(step * width, width)]
+            target = held.at[slot, pl.ds(start, rows)]
+            made.append(pltpu.make_async_copy(source, target, sems.at[slot, j]))
+            start += rows
+        return made
+
+    steps = out.shape[0] // width
+    for step in range(2):
+        for copy in copies(step):
+            copy.start()
+    weights = grad[...]
+    for step in range(steps):
+        for copy in copies(step):
+            copy.wait()
+        product = lax.dot_general(
+            weights, held[step % 2], (((0,), (0,)), ((), ())), preferred_element_type=jnp.float32
+        )
+        out[step * width : step * width + width] = product.T
+        if step + 2 < steps:
+            for copy in copies(step + 2):
+                copy.start()
 
 
 def residual_kernel(places, sums, pair, bias_out, out):
@@ -179,15 +197,19 @@
     out[...] = out_sum
 
 
+def hbm(*arrays):
+    return [pltpu.with_memory_space_constraint(array, pltpu.HBM) for array in arrays]
+
+
 def call(kernel, outs, operands, *scalars, scratch=()):
     vmem = pl.BlockSpec(memory_space=pltpu.VMEM)
     return pl.pallas_call(
         kernel,
-        out_shape=[jax.ShapeDtypeStruct(shape, dtype) for shape, dtype in outs],
+        out_shape=outs,
         in_specs=[pl.BlockSpec(memory_space=pltpu.SMEM)] * len(scalars) + [vmem] * len(operands),
         out_specs=[vmem] * len(outs),
         scratch_shapes=list(scratch),
-        compiler_params=pltpu.CompilerParams(vmem_limit_bytes=10 * 1024 * 1024),
+        compiler_params=pltpu.CompilerParams(vmem_limit_bytes=12 * 1024 * 1024),
     )(*scalars, *operands)
 
 
@@ -203,59 +225,61 @@
     owner = lax.dynamic_index_in_dim(block_owner[0], x * 2 + yhi)
     places = jnp.concatenate([spots, owner, z[None]])
 
+    def whole(shape, dtype=bf16):
+        return jax.ShapeDtypeStruct(shape, dtype)
+
     (pair,) = call(
         prepare_kernel,
-        [((8, 2, 16, A), bf16)],
+        [whole((8, 2, 16, A))],
         (targets, entry_mask),
         block_owner,
         block_mask,
     )
-    embeddings, pair, places = lax.optimization_barrier((embeddings, pair, places))
     mine = spread(embeddings, ALL, 32, CLASSES).reshape(64, -1)
+    mine, pair, places = lax.optimization_barrier((mine, pair, places))
     fourth = send(mine, from_chip(0, 1, 1))
-    mine, pair = lax.optimization_barrier((mine, pair))
-    (both,) = call(join_kernel, [((128, mine.shape[1]), bf16)], (mine, send(mine, CORES)))
+    (both,) = call(join_kernel, [whole((128, mine.shape[1]))], (mine, send(mine, CORES)))
     fetched = [send(both, from_chip(*d)) for d in ((1, 0, 0), (0, 1, 0), (0, 0, 1))]
     direct = [both] + fetched
     late = [send(piece, CORES) for piece in fetched] + [fourth, send(fourth, CORES)]
+    pair = exchange(pair, ("x", "yhi"))
 
     first, second = head_in[0], head_out[0]
-    activations = [((512, A), bf16), ((512, A), f32)]
-    hidden_d, slopes_d = call(direct_kernel, activations, (first, bias_in, *direct))
+    first_held, bias_held, second_held = hbm(first, bias_in, second)
+    activations = [KEPT((512, A), bf16), KEPT((512, A), f32)]
+    hidden_d, slopes_d = call(direct_kernel, activations, (first_held, bias_held, *direct))
     hidden_s, slopes_s, shares = call(
         late_kernel,
-        activations + [((8, A, A), bf16)],
-        (hidden_d, first, bias_in, second, *late),
+        activations + [KEPT((8, A, A), bf16)],
+        (*hbm(hidden_d), first_held, bias_held, second_held, *late),
         places,
         scratch=[pltpu.VMEM((8, 16, 8, A), f32)],
     )
-    shares, direct, late = lax.optimization_barrier((shares, direct, late))
-    pair = exchange(pair, ("x", "yhi"))
-    held = direct + late
-    gathered = pl.pallas_call(
-        gather_rows_kernel,
-        out_shape=jax.ShapeDtypeStruct((1024, first.shape[0]), bf16),
-        in_specs=[pl.BlockSpec(memory_space=pl.ANY)] * len(held),
-        out_specs=pl.BlockSpec(memory_space=pl.ANY),
-        scratch_shapes=[pltpu.SemaphoreType.DMA((len(held),))],
-        compiler_params=pltpu.CompilerParams(vmem_limit_bytes=2 * 1024 * 1024),
-    )(*held)
     sums = exchange(shares, "z")
     (copies,) = call(
-        residual_kernel, [((8, A, A), bf16)], (sums, pair, bias_out[None]), places
-    )
-    copies, gathered = lax.optimization_barrier((copies, gathered))
+        residual_kernel, [whole((8, A, A))], (sums, pair, *hbm(bias_out[None])), places
+    )
     back = exchange(copies, "z")
     grad, bias_in_grad, head_out_grad = call(
         backward_kernel,
-        [((1024, A), bf16), ((1, A), f32), ((A, A), f32)],
-        (back, hidden_d, hidden_s, slopes_d, slopes_s, second),
+        [whole((1024, A)), whole((1, A), f32), whole((A, A), f32)],
+        (back, *hbm(hidden_d, hidden_s, slopes_d, slopes_s, second)),
         places,
         scratch=[pltpu.VMEM((8, 16, 8, A), f32), pltpu.VMEM((1024, A), f32)],
     )
-    head_in_grad = lax.dot_general(
-        gathered, grad, (((0,), (0,)), ((), ())), preferred_element_type=f32
-    )
+    held = direct + late
+    any_space, vmem = pl.BlockSpec(memory_space=pl.ANY), pl.BlockSpec(memory_space=pltpu.VMEM)
+    head_in_grad = pl.pallas_call(
+        last_kernel,
+        out_shape=whole((first.shape[0], A), f32),
+        in_specs=[any_space] * len(held) + [vmem],
+        out_specs=vmem,
+        scratch_shapes=[
+            pltpu.VMEM((2, 1024, 1024), bf16),
+            pltpu.SemaphoreType.DMA((2, len(held))),
+        ],
+        compiler_params=pltpu.CompilerParams(vmem_limit_bytes=20 * 1024 * 1024),
+    )(*held, grad)
     return head_in_grad[None], bias_in_grad, head_out_grad[None]
 
 

time: 143 us -> 128 us (0.90)
  blocking collectives: 49.1 us -> 29 us
  starting transfers between devices: 36.8 us -> 52.2 us
  local copies, waits for them, and re-layouts: 20.5 us -> 7.14 us
  matrix products: 7.08 us -> 0 us
  Pallas kernels: 12.2 us -> 18.4 us
  waiting for transfers between devices: 14.2 us -> 18.3 us
    all_to_all x2, blocking collectives: 49.1 us -> 29 us  [exchange(): lax.all_to_all(blocks, axis, 0, 0, tiled=True, axis_index_groups=groups)]
    all_to_all x2, starting transfers between devices: 12.3 us -> 27.8 us  [exchange(): lax.all_to_all(blocks, axis, 0, 0, tiled=True, axis_index_groups=groups)]
    unnamed x42 -> x10, local copies, waits for them, and re-layouts: 17.9 us -> 3.72 us
    dot_general x1 -> x0, matrix products: 7.08 us -> none  [local(): lax.dot_general(gathered, grad, (((0,), (0,)), ((), ())), preferred_eleme...]
    pallas_call x7, Pallas kernels: 12.2 us -> 18.4 us  [the longest x6 12.5 us: call(): pl.pallas_call(kernel, out_shape=outs, in_specs=[pl.BlockSpec(memory_spac...]
    all_to_all x2, waiting for transfers between devices: 6.04 us -> 10.1 us  [exchange(): lax.all_to_all(blocks, axis, 0, 0, tiled=True, axis_index_groups=groups)]
  transfers between devices with their start and end apart: 11 -> 11, of which waited for: 5 -> 5; matrix products, arithmetic and copies ran while one was open for 0% -> 2% of each run, Pallas kernels for 6% -> 7%
where the time goes in v5:
time: 128 us; the launch traced here: 127 us
  starting transfers between devices  52.2 us (41%)
  blocking collectives  29 us (23%)
  Pallas kernels  18.4 us (14%)
  waiting for transfers between devices  18.3 us (14%)
  local copies, waits for them, and re-layouts  7.14 us (6%)
  other arithmetic  1.32 us (1%)
    all_to_all x2, blocking collectives, exchange(): lax.all_to_all(blocks, axis, 0, 0, tiled=True, axis_index_groups=groups)  29 us
    all_to_all x2, starting transfers between devices, exchange(): lax.all_to_all(blocks, axis, 0, 0, tiled=True, axis_index_groups=groups)  27.8 us
    ppermute x9, starting transfers between devices, send(): return lax.ppermute(block, ALL, pairs)  24.4 us
    pallas_call x6, Pallas kernels, call(): pl.pallas_call(kernel, out_shape=outs, in_specs=[pl.BlockSpec(memory_spac...  12.5 us
    all_to_all x2, waiting for transfers between devices, exchange(): lax.all_to_all(blocks, axis, 0, 0, tiled=True, axis_index_groups=groups)  10.1 us
    ppermute x9, waiting for transfers between devices, send(): return lax.ppermute(block, ALL, pairs)  8.21 us
    pallas_call x1, Pallas kernels, local(): pl.pallas_call(last_kernel, out_shape=whole((first.shape[0], A), f32), in...  5.9 us
    unnamed x10, local copies, waits for them, and re-layouts  3.72 us
  transfers between devices with their start and end apart: 11, of which 5 were waited for; matrix products, arithmetic and copies ran while one was open for 2% of the time, Pallas kernels for 7%

profile of v5, /device:TPU:56, one launch (start us, length us, event | category | flops | bytes accessed | tf_op | source)
XLA Modules:
  0.0 127.2 jit_solution(7039018289696847425)
XLA Ops:
  0.6 2.0 %broadcast_in_dim.18 = bf16[32,2,4096]{2,1,0:T(2,128)(2,1)} broadcast(bf16[2,4096]{1,0:T(2,128)(2,1)} %param.11), dimensions={1,2} | broadcast | bytes 540672 | tf_op jit(solution)/shard_map/broadcast_in_dim | solution.py:68
  2.6 19.5 %all-to-all-start = ((bf16[32,2,4096]{2,1,0:T(2,128)(2,1)}), bf16[32,2,4096]{2,1,0:T(2,128)(2,1)S(1)}, u32[]{:S(2)}, u32[]{:S(2)}) async-start(bf16[32,2,4096]{2,1,0:T(2,128)(2,1)} %broadcast_in_dim.18), calls=%async_computation | async-start | bytes 1048576 | tf_op jit(solution)/shard_map/all_to_all | solution.py:64
  22.1 1.2 constant_dynamic-slice_fusion
  23.4 0.0 copy-start.1
  23.4 0.8 copy-done.1
  24.2 0.0 copy-start.2
  24.2 0.8 copy-done.2
  25.0 0.0 copy-start.3
  25.0 0.7 copy-done.3
  25.6 0.0 copy-start.4
  25.6 0.7 copy-done.4
  26.3 1.2 shard_map.130
  27.5 0.7 fusion
  28.2 0.6 pad_add_fusion.spots.places
  28.8 10.1 %all-to-all-done = bf16[32,2,4096]{2,1,0:T(2,128)(2,1)S(1)} async-done(((bf16[32,2,4096]{2,1,0:T(2,128)(2,1)}), bf16[32,2,4096]{2,1,0:T(2,128)(2,1)S(1)}, u32[]{:S(2)}, u32[]{:S(2)}) %all-to-all-start) | async-done | bytes 524320 | tf_op jit(solution)/shard_map/all_to_all | solution.py:64
  38.9 0.2 reshape.11.refs_0_
  39.1 1.9 %collective-permute-start = (bf16[64,4096]{1,0:T(8,128)(2,1)S(1)}, bf16[64,4096]{1,0:T(8,128)(2,1)S(1)}, u32[]{:S(2)}, u32[]{:S(2)}) collective-permute-start(bf16[64,4096]{1,0:T(8,128)(2,1)S(1)} %reshape.11.refs_0_), channel_id=1, source_target_pairs={{0,64},{1,65},{2,66},{3,67},{4,68},{5,69},{6,70},{7,71},{8,72},{9,... | collective-permute-start | bytes 1572872 | tf_op jit(solution)/shard_map/ppermute | solution.py:72
  41.1 1.9 %collective-permute-done.refs_1_ = bf16[64,4096]{1,0:T(8,128)(2,1)S(1)} collective-permute-done((bf16[64,4096]{1,0:T(8,128)(2,1)S(1)}, bf16[64,4096]{1,0:T(8,128)(2,1)S(1)}, u32[]{:S(2)}, u32[]{:S(2)}) %collective-permute-start) | collective-permute-done | bytes 524320 | tf_op jit(solution)/shard_map/ppermute | solution.py:72
  42.9 0.1 shard_map.131.refs_0_
  43.0 0.0 copy-start
  43.0 0.8 copy-done
  43.8 3.2 %collective-permute-start.3 = (bf16[128,4096]{1,0:T(8,128)(2,1)S(1)}, bf16[128,4096]{1,0:T(8,128)(2,1)S(1)}, u32[]{:S(2)}, u32[]{:S(2)}) collective-permute-start(bf16[128,4096]{1,0:T(8,128)(2,1)S(1)} %shard_map.131.refs_0_), channel_id=1, source_target_pairs={{1,0},{2,1},{3,2},{4,3},{5,4},{6,5},{7,6},{0,7},{9,8},{10,9},{11,1... | collective-permute-start | bytes 3145736 | tf_op jit(solution)/shard_map/ppermute | solution.py:72
  47.0 2.5 %collective-permute-start.2 = (bf16[128,4096]{1,0:T(8,128)(2,1)S(1)}, bf16[128,4096]{1,0:T(8,128)(2,1)S(1)}, u32[]{:S(2)}, u32[]{:S(2)}) collective-permute-start(bf16[128,4096]{1,0:T(8,128)(2,1)S(1)} %shard_map.131.refs_0_), channel_id=1, source_target_pairs={{128,0},{129,1},{130,2},{131,3},{132,4},{133,5},{134,6},{135,7},{1... | collective-permute-start | bytes 3145736 | tf_op jit(solution)/shard_map/ppermute | solution.py:72
  49.5 3.0 %collective-permute-start.1 = (bf16[128,4096]{1,0:T(8,128)(2,1)S(1)}, bf16[128,4096]{1,0:T(8,128)(2,1)}, u32[]{:S(2)}, u32[]{:S(2)}) collective-permute-start(bf16[128,4096]{1,0:T(8,128)(2,1)S(1)} %shard_map.131.refs_0_), channel_id=1, source_target_pairs={{16,0},{17,1},{18,2},{19,3},{20,4},{21,5},{22,6},{23,7},{24,8},{25... | collective-permute-start | bytes 3145736 | tf_op jit(solution)/shard_map/ppermute | solution.py:72
  52.6 4.9 %collective-permute-start.7 = (bf16[64,4096]{1,0:T(8,128)(2,1)}, bf16[64,4096]{1,0:T(8,128)(2,1)}, u32[]{:S(2)}, u32[]{:S(2)}) collective-permute-start(bf16[64,4096]{1,0:T(8,128)(2,1)} %copy-done), channel_id=1, source_target_pairs={{129,0},{130,1},{131,2},{132,3},{133,4},{134,5},{135,6},{128,7},{1... | collective-permute-start | bytes 1572872 | tf_op jit(solution)/shard_map/ppermute | solution.py:72
  57.5 3.0 %collective-permute-done.3.refs_3_ = bf16[128,4096]{1,0:T(8,128)(2,1)S(1)} collective-permute-done((bf16[128,4096]{1,0:T(8,128)(2,1)S(1)}, bf16[128,4096]{1,0:T(8,128)(2,1)S(1)}, u32[]{:S(2)}, u32[]{:S(2)}) %collective-permute-start.3) | collective-permute-done | bytes 1048608 | tf_op jit(solution)/shard_map/ppermute | solution.py:72
  60.5 2.4 %collective-permute-start.6 = (bf16[128,4096]{1,0:T(8,128)(2,1)S(1)}, bf16[128,4096]{1,0:T(8,128)(2,1)}, u32[]{:S(2)}, u32[]{:S(2)}) collective-permute-start(bf16[128,4096]{1,0:T(8,128)(2,1)S(1)} %collective-permute-done.3.refs_3_), channel_id=1, source_target_pairs={{0,64},{1,65},{2,66},{3,67},{4,68},{5,69},{6,70},{7,71},{8,72},{9,... | collective-permute-start | bytes 3145736 | tf_op jit(solution)/shard_map/ppermute | solution.py:72
  62.9 2.1 %collective-permute-done.2.refs_2_ = bf16[128,4096]{1,0:T(8,128)(2,1)S(1)} collective-permute-done((bf16[128,4096]{1,0:T(8,128)(2,1)S(1)}, bf16[128,4096]{1,0:T(8,128)(2,1)S(1)}, u32[]{:S(2)}, u32[]{:S(2)}) %collective-permute-start.2) | collective-permute-done | bytes 1048608 | tf_op jit(solution)/shard_map/ppermute | solution.py:72
  64.9 1.9 %collective-permute-start.5 = (bf16[128,4096]{1,0:T(8,128)(2,1)S(1)}, bf16[128,4096]{1,0:T(8,128)(2,1)}, u32[]{:S(2)}, u32[]{:S(2)}) collective-permute-start(bf16[128,4096]{1,0:T(8,128)(2,1)S(1)} %collective-permute-done.2.refs_2_), channel_id=1, source_target_pairs={{0,64},{1,65},{2,66},{3,67},{4,68},{5,69},{6,70},{7,71},{8,72},{9,... | collective-permute-start | bytes 3145736 | tf_op jit(solution)/shard_map/ppermute | solution.py:72
  66.9 0.0 collective-permute-done.1.refs_1_
  66.9 2.7 %collective-permute-start.4 = (bf16[128,4096]{1,0:T(8,128)(2,1)}, bf16[128,4096]{1,0:T(8,128)(2,1)}, u32[]{:S(2)}, u32[]{:S(2)}) collective-permute-start(bf16[128,4096]{1,0:T(8,128)(2,1)} %collective-permute-done.1.refs_1_), channel_id=1, source_target_pairs={{0,64},{1,65},{2,66},{3,67},{4,68},{5,69},{6,70},{7,71},{8,72},{9,... | collective-permute-start | bytes 3145736 | tf_op jit(solution)/shard_map/ppermute | solution.py:72
  69.6 1.2 collective-permute-done.7.refs_3_.refs_7_
  70.8 1.9 %collective-permute-start.8 = (bf16[64,4096]{1,0:T(8,128)(2,1)}, bf16[64,4096]{1,0:T(8,128)(2,1)}, u32[]{:S(2)}, u32[]{:S(2)}) collective-permute-start(bf16[64,4096]{1,0:T(8,128)(2,1)} %collective-permute-done.7.refs_3_.refs_7_), channel_id=1, source_target_pairs={{0,64},{1,65},{2,66},{3,67},{4,68},{5,69},{6,70},{7,71},{8,72},{9,... | collective-permute-start | bytes 1572872 | tf_op jit(solution)/shard_map/ppermute | solution.py:72
  72.7 8.3 %all-to-all-start.2 = ((bf16[8,2,16,128]{3,2,1,0:T(8,128)(2,1)}), bf16[8,2,16,128]{3,2,1,0:T(8,128)(2,1)S(1)}, u32[]{:S(2)}, u32[]{:S(2)}) async-start(bf16[8,2,16,128]{3,2,1,0:T(8,128)(2,1)} %shard_map.130), calls=%async_computation.2 | async-start | bytes 131072 | tf_op jit(solution)/shard_map/all_to_all | solution.py:64
  81.0 3.6 %shard_map.132 = (bf16[512,128]{1,0:T(8,128)(2,1)}, f32[512,128]{1,0:T(8,128)}) custom-call(bf16[4096,128]{1,0:T(8,128)(2,1)} %bitcast.7, f32[1,128]{1,0:T(1,128)} %bias_in.3, bf16[128,4096]{1,0:T(8,128)(2,1)S(1)} %shard_map.131.refs_0_, bf16[128,4096]{1,0:T(8,128)(2,1)} %collective-permute-done.1.refs_1_, ...), custom_call_target="tpu_custom_call" | custom-call | tf_op jit(solution)/shard_map/pallas_call | solution.py:206
  84.6 0.0 collective-permute-done.8.refs_4_.refs_8_
  84.6 0.0 collective-permute-done.6.refs_2_.refs_6_
  84.6 0.0 collective-permute-done.5.refs_1_.refs_5_
  84.6 0.0 collective-permute-done.4.refs_0_.refs_4_
  84.6 4.7 %shard_map.133 = (bf16[512,128]{1,0:T(8,128)(2,1)}, f32[512,128]{1,0:T(8,128)}, bf16[8,128,128]{2,1,0:T(8,128)(2,1)}) custom-call(s32[18]{0:T(128)S(1)} %pad_add_fusion.spots.places, bf16[512,128]{1,0:T(8,128)(2,1)} %get-tuple-element.16.hidden_d, bf16[4096,128]{1,0:T(8,128)(2,1)} %bitcast.8, f32[1,128]{1,0:T(1,128)} %bias_in.3, bf16[128,128]{1,0:T(8,128)(2,1)} %bitcast.10, ...), custom_call_target="tpu_custom_call" | custom-call | tf_op jit(solution)/shard_map/pallas_call | solution.py:206
  89.3 0.0 all-to-all-done.2.pair
  89.3 16.0 %all_to_all.20.sums = bf16[8,128,128]{2,1,0:T(8,128)(2,1)S(1)} all-to-all(bf16[8,128,128]{2,1,0:T(8,128)(2,1)} %get-tuple-element.17), channel_id=1, replica_groups=mesh['ylo'=4,'core'=2,'x'=4,'yhi'=2,'z'=8] {'z'}, dimensions={0} | all-to-all | bytes 524288 | tf_op jit(solution)/shard_map/all_to_all | solution.py:64
  105.3 0.9 shard_map.134
  106.2 13.0 %all_to_all.21.back = bf16[8,128,128]{2,1,0:T(8,128)(2,1)S(1)} all-to-all(bf16[8,128,128]{2,1,0:T(8,128)(2,1)S(1)} %shard_map.134), channel_id=1, replica_groups=mesh['ylo'=4,'core'=2,'x'=4,'yhi'=2,'z'=8] {'z'}, dimensions={0} | all-to-all | bytes 524288 | tf_op jit(solution)/shard_map/all_to_all | solution.py:64
  119.1 2.1 %shard_map.135 = (bf16[1024,128]{1,0:T(8,128)(2,1)S(1)}, f32[1,128]{1,0:T(1,128)}, f32[128,128]{1,0:T(8,128)}) custom-call(s32[18]{0:T(128)S(1)} %pad_add_fusion.spots.places, bf16[8,128,128]{2,1,0:T(8,128)(2,1)S(1)} %all_to_all.21.back, bf16[512,128]{1,0:T(8,128)(2,1)} %get-tuple-element.16.hidden_d, bf16[512,128]{1,0:T(8,128)(2,1)} %get-tuple-element.19.hidden_s, ...), custom_call_target="tpu_custom_call" | custom-call | tf_op jit(solution)/shard_map/pallas_call | solution.py:206
  121.3 5.9 %shard_map.136 = f32[4096,128]{1,0:T(8,128)} custom-call(bf16[128,4096]{1,0:T(8,128)(2,1)S(1)} %shard_map.131.refs_0_, bf16[128,4096]{1,0:T(8,128)(2,1)} %collective-permute-done.1.refs_1_, bf16[128,4096]{1,0:T(8,128)(2,1)S(1)} %collective-permute-done.2.refs_2_, bf16[128,4096]{1,0:T(8,128)(2,1)S(1)} %collective-permute-done.3.refs_3_, ...), custom_call_target="tpu_custom_call" | custom-call | tf_op jit(solution)/shard_map/pallas_call | solution.py:272
Async XLA Ops:
  2.6 36.3 %all-to-all-start = ((bf16[32,2,4096]{2,1,0:T(2,128)(2,1)}), bf16[32,2,4096]{2,1,0:T(2,128)(2,1)S(1)}, u32[]{:S(2)}, u32[]{:S(2)}) async-start(bf16[32,2,4096]{2,1,0:T(2,128)(2,1)} %broadcast_in_dim.18), calls=%async_computation | async-start | bytes 1048576 | tf_op jit(solution)/shard_map/all_to_all | solution.py:64
  23.4 0.8 copy-start.1
  24.2 0.8 copy-start.2
  25.0 0.7 copy-start.3
  25.6 0.7 copy-start.4
  39.1 3.8 %collective-permute-start = (bf16[64,4096]{1,0:T(8,128)(2,1)S(1)}, bf16[64,4096]{1,0:T(8,128)(2,1)S(1)}, u32[]{:S(2)}, u32[]{:S(2)}) collective-permute-start(bf16[64,4096]{1,0:T(8,128)(2,1)S(1)} %reshape.11.refs_0_), channel_id=1, source_target_pairs={{0,64},{1,65},{2,66},{3,67},{4,68},{5,69},{6,70},{7,71},{8,72},{9,... | collective-permute-start | bytes 1572872 | tf_op jit(solution)/shard_map/ppermute | solution.py:72
  43.0 0.8 copy-start
  43.8 16.7 %collective-permute-start.3 = (bf16[128,4096]{1,0:T(8,128)(2,1)S(1)}, bf16[128,4096]{1,0:T(8,128)(2,1)S(1)}, u32[]{:S(2)}, u32[]{:S(2)}) collective-permute-start(bf16[128,4096]{1,0:T(8,128)(2,1)S(1)} %shard_map.131.refs_0_), channel_id=1, source_target_pairs={{1,0},{2,1},{3,2},{4,3},{5,4},{6,5},{7,6},{0,7},{9,8},{10,9},{11,1... | collective-permute-start | bytes 3145736 | tf_op jit(solution)/shard_map/ppermute | solution.py:72
  47.0 17.9 %collective-permute-start.2 = (bf16[128,4096]{1,0:T(8,128)(2,1)S(1)}, bf16[128,4096]{1,0:T(8,128)(2,1)S(1)}, u32[]{:S(2)}, u32[]{:S(2)}) collective-permute-start(bf16[128,4096]{1,0:T(8,128)(2,1)S(1)} %shard_map.131.refs_0_), channel_id=1, source_target_pairs={{128,0},{129,1},{130,2},{131,3},{132,4},{133,5},{134,6},{135,7},{1... | collective-permute-start | bytes 3145736 | tf_op jit(solution)/shard_map/ppermute | solution.py:72
  49.5 17.3 %collective-permute-start.1 = (bf16[128,4096]{1,0:T(8,128)(2,1)S(1)}, bf16[128,4096]{1,0:T(8,128)(2,1)}, u32[]{:S(2)}, u32[]{:S(2)}) collective-permute-start(bf16[128,4096]{1,0:T(8,128)(2,1)S(1)} %shard_map.131.refs_0_), channel_id=1, source_target_pairs={{16,0},{17,1},{18,2},{19,3},{20,4},{21,5},{22,6},{23,7},{24,8},{25... | collective-permute-start | bytes 3145736 | tf_op jit(solution)/shard_map/ppermute | solution.py:72
  52.6 18.2 %collective-permute-start.7 = (bf16[64,4096]{1,0:T(8,128)(2,1)}, bf16[64,4096]{1,0:T(8,128)(2,1)}, u32[]{:S(2)}, u32[]{:S(2)}) collective-permute-start(bf16[64,4096]{1,0:T(8,128)(2,1)} %copy-done), channel_id=1, source_target_pairs={{129,0},{130,1},{131,2},{132,3},{133,4},{134,5},{135,6},{128,7},{1... | collective-permute-start | bytes 1572872 | tf_op jit(solution)/shard_map/ppermute | solution.py:72
  60.5 24.1 %collective-permute-start.6 = (bf16[128,4096]{1,0:T(8,128)(2,1)S(1)}, bf16[128,4096]{1,0:T(8,128)(2,1)}, u32[]{:S(2)}, u32[]{:S(2)}) collective-permute-start(bf16[128,4096]{1,0:T(8,128)(2,1)S(1)} %collective-permute-done.3.refs_3_), channel_id=1, source_target_pairs={{0,64},{1,65},{2,66},{3,67},{4,68},{5,69},{6,70},{7,71},{8,72},{9,... | collective-permute-start | bytes 3145736 | tf_op jit(solution)/shard_map/ppermute | solution.py:72
  64.9 19.7 %collective-permute-start.5 = (bf16[128,4096]{1,0:T(8,128)(2,1)S(1)}, bf16[128,4096]{1,0:T(8,128)(2,1)}, u32[]{:S(2)}, u32[]{:S(2)}) collective-permute-start(bf16[128,4096]{1,0:T(8,128)(2,1)S(1)} %collective-permute-done.2.refs_2_), channel_id=1, source_target_pairs={{0,64},{1,65},{2,66},{3,67},{4,68},{5,69},{6,70},{7,71},{8,72},{9,... | collective-permute-start | bytes 3145736 | tf_op jit(solution)/shard_map/ppermute | solution.py:72
  66.9 17.7 %collective-permute-start.4 = (bf16[128,4096]{1,0:T(8,128)(2,1)}, bf16[128,4096]{1,0:T(8,128)(2,1)}, u32[]{:S(2)}, u32[]{:S(2)}) collective-permute-start(bf16[128,4096]{1,0:T(8,128)(2,1)} %collective-permute-done.1.refs_1_), channel_id=1, source_target_pairs={{0,64},{1,65},{2,66},{3,67},{4,68},{5,69},{6,70},{7,71},{8,72},{9,... | collective-permute-start | bytes 3145736 | tf_op jit(solution)/shard_map/ppermute | solution.py:72
  70.8 13.8 %collective-permute-start.8 = (bf16[64,4096]{1,0:T(8,128)(2,1)}, bf16[64,4096]{1,0:T(8,128)(2,1)}, u32[]{:S(2)}, u32[]{:S(2)}) collective-permute-start(bf16[64,4096]{1,0:T(8,128)(2,1)} %collective-permute-done.7.refs_3_.refs_7_), channel_id=1, source_target_pairs={{0,64},{1,65},{2,66},{3,67},{4,68},{5,69},{6,70},{7,71},{8,72},{9,... | collective-permute-start | bytes 1572872 | tf_op jit(solution)/shard_map/ppermute | solution.py:72
  72.7 16.6 %all-to-all-start.2 = ((bf16[8,2,16,128]{3,2,1,0:T(8,128)(2,1)}), bf16[8,2,16,128]{3,2,1,0:T(8,128)(2,1)S(1)}, u32[]{:S(2)}, u32[]{:S(2)}) async-start(bf16[8,2,16,128]{3,2,1,0:T(8,128)(2,1)} %shard_map.130), calls=%async_computation.2 | async-start | bytes 131072 | tf_op jit(solution)/shard_map/all_to_all | solution.py:64

commit v6 on v5

--- a/solution.py
+++ b/solution.py
@@ -87,37 +87,6 @@
         measured = entry_mask[:, lanes] * jnp.where(row < 8, block_mask[0, o], block_mask[1, o])
         out[b, 0] = targets[:, lanes]
         out[b, 1] = measured.astype(jnp.float32).astype(jnp.bfloat16)
-
-
-def last_kernel(*refs):
-    *pieces, grad, out, held, sems = refs
-    width = held.shape[2]
-
-    def copies(step):
-        slot, start, made = step % 2, 0, []
-        for j, piece in enumerate(pieces):
-            rows = piece.shape[0]
-            source = piece.at[:, pl.ds(step * width, width)]
-            target = held.at[slot, pl.ds(start, rows)]
-            made.append(pltpu.make_async_copy(source, target, sems.at[slot, j]))
-            start += rows
-        return made
-
-    steps = out.shape[0] // width
-    for step in range(2):
-        for copy in copies(step):
-            copy.start()
-    weights = grad[...]
-    for step in range(steps):
-        for copy in copies(step):
-            copy.wait()
-        product = lax.dot_general(
-            weights, held[step % 2], (((0,), (0,)), ((), ())), preferred_element_type=jnp.float32
-        )
-        out[step * width : step * width + width] = product.T
-        if step + 2 < steps:
-            for copy in copies(step + 2):
-                copy.start()
 
 
 def residual_kernel(places, sums, pair, bias_out, out):
@@ -144,24 +113,34 @@
         out[j] = residual
 
 
-def forward_kernel(pieces, head_in, bias_in, hidden, slopes):
-    start = 0
-    for piece in pieces:
-        span = slice(start, start + piece.shape[0])
-        start += piece.shape[0]
-        pre = jnp.dot(piece[...], head_in[...], preferred_element_type=jnp.float32) + bias_in[...]
+def forward_kernel(pieces, head_in, bias_in, hidden, slopes, held, weights, sems):
+    copies = [pltpu.make_async_copy(head_in, weights, sems.at[0])]
+    spans, start = [], 0
+    for j, piece in enumerate(pieces):
+        rows = piece.shape[0]
+        target = held.at[pl.ds(start, rows)]
+        copies.append(pltpu.make_async_copy(piece, target, sems.at[j + 1]))
+        spans.append(slice(start, start + rows))
+        start += rows
+    for copy in copies:
+        copy.start()
+    copies[0].wait()
+    for span, copy in zip(spans, copies[1:]):
+        copy.wait()
+        pre = jnp.dot(held[span], weights[...], preferred_element_type=jnp.float32) + bias_in[...]
         activated, slope = gelu_parts(pre)
         hidden[span] = activated.astype(jnp.bfloat16)
         slopes[span] = slope
 
 
-def direct_kernel(head_in, bias_in, *refs):
-    forward_kernel(refs[:-2], head_in, bias_in, *refs[-2:])
-
-
-def late_kernel(spots, hidden_d, head_in, bias_in, head_out, *refs):
-    *pieces, hidden_s, slopes_s, out, wide = refs
-    forward_kernel(pieces, head_in, bias_in, hidden_s, slopes_s)
+def direct_kernel(bias_in, head_in, *refs):
+    *pieces, hidden, slopes, held, weights, sems = refs
+    forward_kernel(pieces, head_in, bias_in, hidden, slopes, held, weights, sems)
+
+
+def late_kernel(spots, hidden_d, bias_in, head_out, head_in, *refs):
+    *pieces, hidden_s, slopes_s, out, held, weights, sems, wide = refs
+    forward_kernel(pieces, head_in, bias_in, hidden_s, slopes_s, held, weights, sems)
     for part, start in ((hidden_d, 0), (hidden_s, 8)):
         share = jnp.dot(part[...], head_out[...], preferred_element_type=jnp.float32)
         for j in range(8):
@@ -197,20 +176,56 @@
     out[...] = out_sum
 
 
+def last_kernel(spots, back, hidden_d, hidden_s, slopes_d, slopes_s, head_out, *refs):
+    *pieces, bias, head_out_grad, out, wide, rows, grad, held, sems = refs
+    width = held.shape[2]
+
+    def copies(step):
+        slot, start, made = step % 2, 0, []
+        for j, piece in enumerate(pieces):
+            count = piece.shape[0]
+            source = piece.at[:, pl.ds(step * width, width)]
+            target = held.at[slot, pl.ds(start, count)]
+            made.append(pltpu.make_async_copy(source, target, sems.at[slot, j]))
+            start += count
+        return made
+
+    steps = out.shape[0] // width
+    for step in range(2):
+        for copy in copies(step):
+            copy.start()
+    backward_kernel(
+        spots, back, hidden_d, hidden_s, slopes_d, slopes_s, head_out, grad, bias, head_out_grad,
+        wide, rows,
+    )
+    weights = grad[...]
+    for step in range(steps):
+        for copy in copies(step):
+            copy.wait()
+        product = lax.dot_general(
+            weights, held[step % 2], (((0,), (0,)), ((), ())), preferred_element_type=jnp.float32
+        )
+        out[step * width : step * width + width] = product.T
+        if step + 2 < steps:
+            for copy in copies(step + 2):
+                copy.start()
+
+
 def hbm(*arrays):
     return [pltpu.with_memory_space_constraint(array, pltpu.HBM) for array in arrays]
 
 
-def call(kernel, outs, operands, *scalars, scratch=()):
-    vmem = pl.BlockSpec(memory_space=pltpu.VMEM)
+def call(kernel, outs, operands, *scalars, fetched=(), scratch=(), limit=12):
+    vmem, anywhere = pl.BlockSpec(memory_space=pltpu.VMEM), pl.BlockSpec(memory_space=pl.ANY)
+    smem = pl.BlockSpec(memory_space=pltpu.SMEM)
     return pl.pallas_call(
         kernel,
         out_shape=outs,
-        in_specs=[pl.BlockSpec(memory_space=pltpu.SMEM)] * len(scalars) + [vmem] * len(operands),
+        in_specs=[smem] * len(scalars) + [vmem] * len(operands) + [anywhere] * len(fetched),
         out_specs=[vmem] * len(outs),
         scratch_shapes=list(scratch),
-        compiler_params=pltpu.CompilerParams(vmem_limit_bytes=12 * 1024 * 1024),
-    )(*scalars, *operands)
+        compiler_params=pltpu.CompilerParams(vmem_limit_bytes=limit * 1024 * 1024),
+    )(*scalars, *operands, *fetched)
 
 
 def local(
@@ -241,45 +256,51 @@
     (both,) = call(join_kernel, [whole((128, mine.shape[1]))], (mine, send(mine, CORES)))
     fetched = [send(both, from_chip(*d)) for d in ((1, 0, 0), (0, 1, 0), (0, 0, 1))]
     direct = [both] + fetched
+    pair, both = lax.optimization_barrier((pair, both))
+    pair = exchange(pair, ("x", "yhi"))
+    fetched[0], pair = lax.optimization_barrier((fetched[0], pair))
     late = [send(piece, CORES) for piece in fetched] + [fourth, send(fourth, CORES)]
-    pair = exchange(pair, ("x", "yhi"))
 
     first, second = head_in[0], head_out[0]
     first_held, bias_held, second_held = hbm(first, bias_in, second)
     activations = [KEPT((512, A), bf16), KEPT((512, A), f32)]
-    hidden_d, slopes_d = call(direct_kernel, activations, (first_held, bias_held, *direct))
+    width = first.shape[0]
+    landing = [
+        pltpu.VMEM((512, width), bf16),
+        pltpu.VMEM((width, A), bf16),
+        pltpu.SemaphoreType.DMA((6,)),
+    ]
+    hidden_d, slopes_d = call(
+        direct_kernel, activations, (bias_held,), fetched=(first_held, *direct), scratch=landing
+    )
     hidden_s, slopes_s, shares = call(
         late_kernel,
         activations + [KEPT((8, A, A), bf16)],
-        (*hbm(hidden_d), first_held, bias_held, second_held, *late),
+        (*hbm(hidden_d), bias_held, second_held),
         places,
-        scratch=[pltpu.VMEM((8, 16, 8, A), f32)],
+        fetched=(first_held, *late),
+        scratch=landing + [pltpu.VMEM((8, 16, 8, A), f32)],
     )
     sums = exchange(shares, "z")
     (copies,) = call(
         residual_kernel, [whole((8, A, A))], (sums, pair, *hbm(bias_out[None])), places
     )
     back = exchange(copies, "z")
-    grad, bias_in_grad, head_out_grad = call(
-        backward_kernel,
-        [whole((1024, A)), whole((1, A), f32), whole((A, A), f32)],
+    bias_in_grad, head_out_grad, head_in_grad = call(
+        last_kernel,
+        [whole((1, A), f32), whole((A, A), f32), whole((width, A), f32)],
         (back, *hbm(hidden_d, hidden_s, slopes_d, slopes_s, second)),
         places,
-        scratch=[pltpu.VMEM((8, 16, 8, A), f32), pltpu.VMEM((1024, A), f32)],
-    )
-    held = direct + late
-    any_space, vmem = pl.BlockSpec(memory_space=pl.ANY), pl.BlockSpec(memory_space=pltpu.VMEM)
-    head_in_grad = pl.pallas_call(
-        last_kernel,
-        out_shape=whole((first.shape[0], A), f32),
-        in_specs=[any_space] * len(held) + [vmem],
-        out_specs=vmem,
-        scratch_shapes=[
+        fetched=direct + late,
+        scratch=[
+            pltpu.VMEM((8, 16, 8, A), f32),
+            pltpu.VMEM((1024, A), f32),
+            pltpu.VMEM((1024, A), bf16),
             pltpu.VMEM((2, 1024, 1024), bf16),
-            pltpu.SemaphoreType.DMA((2, len(held))),
+            pltpu.SemaphoreType.DMA((2, 9)),
         ],
-        compiler_params=pltpu.CompilerParams(vmem_limit_bytes=20 * 1024 * 1024),
-    )(*held, grad)
+        limit=20,
+    )
     return head_in_grad[None], bias_in_grad, head_out_grad[None]
 
 

time: 128 us -> 128 us (level)
  the two profiles are of different devices: /device:TPU:56 before, /device:TPU:8 now
where the time goes in v6:
time: 128 us; the launch traced here: 127 us
  starting transfers between devices  48.9 us (38%)
  blocking collectives  28.9 us (23%)
  waiting for transfers between devices  22.1 us (17%)
  Pallas kernels  18.2 us (14%)
  local copies, waits for them, and re-layouts  7.14 us (6%)
  other arithmetic  1.32 us (1%)
    all_to_all x2, blocking collectives, exchange(): lax.all_to_all(blocks, axis, 0, 0, tiled=True, axis_index_groups=groups)  28.9 us
    all_to_all x2, starting transfers between devices, exchange(): lax.all_to_all(blocks, axis, 0, 0, tiled=True, axis_index_groups=groups)  24.5 us
    ppermute x9, starting transfers between devices, send(): return lax.ppermute(block, ALL, pairs)  24.3 us
    all_to_all x2, waiting for transfers between devices, exchange(): lax.all_to_all(blocks, axis, 0, 0, tiled=True, axis_index_groups=groups)  20.2 us
    pallas_call x6, Pallas kernels, call(): pl.pallas_call(kernel, out_shape=outs, in_specs=[smem] * len(scalars) + [...  18.2 us
    unnamed x10, local copies, waits for them, and re-layouts  3.72 us
  transfers between devices with their start and end apart: 11, of which 3 were waited for; matrix products, arithmetic and copies ran while one was open for 2% of the time, Pallas kernels for 4%

profile of v6, /device:TPU:8, one launch (start us, length us, event | category | flops | bytes accessed | tf_op | source)
XLA Modules:
  0.0 127.3 jit_solution(1700286582810402911)
XLA Ops:
  0.6 2.0 %broadcast_in_dim.18 = bf16[32,2,4096]{2,1,0:T(2,128)(2,1)} broadcast(bf16[2,4096]{1,0:T(2,128)(2,1)} %param.11), dimensions={1,2} | broadcast | bytes 540672 | tf_op jit(solution)/shard_map/broadcast_in_dim | solution.py:68
  2.6 19.5 %all-to-all-start = ((bf16[32,2,4096]{2,1,0:T(2,128)(2,1)}), bf16[32,2,4096]{2,1,0:T(2,128)(2,1)S(1)}, u32[]{:S(2)}, u32[]{:S(2)}) async-start(bf16[32,2,4096]{2,1,0:T(2,128)(2,1)} %broadcast_in_dim.18), calls=%async_computation | async-start | bytes 1048576 | tf_op jit(solution)/shard_map/all_to_all | solution.py:64
  22.1 1.2 constant_dynamic-slice_fusion
  23.4 0.0 copy-start.1
  23.4 0.8 copy-done.1
  24.2 0.0 copy-start.2
  24.2 0.8 copy-done.2
  25.0 0.0 copy-start.3
  25.0 0.7 copy-done.3
  25.7 0.0 copy-start.4
  25.7 0.7 copy-done.4
  26.3 1.2 shard_map.130
  27.5 0.7 fusion
  28.2 0.6 pad_add_fusion.spots.places
  28.8 12.2 %all-to-all-done = bf16[32,2,4096]{2,1,0:T(2,128)(2,1)S(1)} async-done(((bf16[32,2,4096]{2,1,0:T(2,128)(2,1)}), bf16[32,2,4096]{2,1,0:T(2,128)(2,1)S(1)}, u32[]{:S(2)}, u32[]{:S(2)}) %all-to-all-start) | async-done | bytes 524320 | tf_op jit(solution)/shard_map/all_to_all | solution.py:64
  41.0 0.2 reshape.11.refs_0_
  41.2 1.9 %collective-permute-start = (bf16[64,4096]{1,0:T(8,128)(2,1)S(1)}, bf16[64,4096]{1,0:T(8,128)(2,1)S(1)}, u32[]{:S(2)}, u32[]{:S(2)}) collective-permute-start(bf16[64,4096]{1,0:T(8,128)(2,1)S(1)} %reshape.11.refs_0_), channel_id=1, source_target_pairs={{0,64},{1,65},{2,66},{3,67},{4,68},{5,69},{6,70},{7,71},{8,72},{9,... | collective-permute-start | bytes 1572872 | tf_op jit(solution)/shard_map/ppermute | solution.py:72
  43.2 1.9 %collective-permute-done.refs_1_ = bf16[64,4096]{1,0:T(8,128)(2,1)S(1)} collective-permute-done((bf16[64,4096]{1,0:T(8,128)(2,1)S(1)}, bf16[64,4096]{1,0:T(8,128)(2,1)S(1)}, u32[]{:S(2)}, u32[]{:S(2)}) %collective-permute-start) | collective-permute-done | bytes 524320 | tf_op jit(solution)/shard_map/ppermute | solution.py:72
  45.0 0.1 shard_map.131.refs_0_
  45.1 0.0 copy-start
  45.1 0.8 copy-done
  45.9 3.5 %collective-permute-start.1 = (bf16[128,4096]{1,0:T(8,128)(2,1)S(1)}, bf16[128,4096]{1,0:T(8,128)(2,1)S(1)}, u32[]{:S(2)}, u32[]{:S(2)}) collective-permute-start(bf16[128,4096]{1,0:T(8,128)(2,1)S(1)} %shard_map.131.refs_0_), channel_id=1, source_target_pairs={{16,0},{17,1},{18,2},{19,3},{20,4},{21,5},{22,6},{23,7},{24,8},{25... | collective-permute-start | bytes 3145736 | tf_op jit(solution)/shard_map/ppermute | solution.py:72
  49.4 4.0 %collective-permute-start.3 = (bf16[128,4096]{1,0:T(8,128)(2,1)S(1)}, bf16[128,4096]{1,0:T(8,128)(2,1)S(1)}, u32[]{:S(2)}, u32[]{:S(2)}) collective-permute-start(bf16[128,4096]{1,0:T(8,128)(2,1)S(1)} %shard_map.131.refs_0_), channel_id=1, source_target_pairs={{1,0},{2,1},{3,2},{4,3},{5,4},{6,5},{7,6},{0,7},{9,8},{10,9},{11,1... | collective-permute-start | bytes 3145736 | tf_op jit(solution)/shard_map/ppermute | solution.py:72
  53.4 1.9 %collective-permute-start.2 = (bf16[128,4096]{1,0:T(8,128)(2,1)S(1)}, bf16[128,4096]{1,0:T(8,128)(2,1)}, u32[]{:S(2)}, u32[]{:S(2)}) collective-permute-start(bf16[128,4096]{1,0:T(8,128)(2,1)S(1)} %shard_map.131.refs_0_), channel_id=1, source_target_pairs={{128,0},{129,1},{130,2},{131,3},{132,4},{133,5},{134,6},{135,7},{1... | collective-permute-start | bytes 3145736 | tf_op jit(solution)/shard_map/ppermute | solution.py:72
  55.3 5.0 %all-to-all-start.1 = ((bf16[8,2,16,128]{3,2,1,0:T(8,128)(2,1)}), bf16[8,2,16,128]{3,2,1,0:T(8,128)(2,1)S(1)}, u32[]{:S(2)}, u32[]{:S(2)}) async-start(bf16[8,2,16,128]{3,2,1,0:T(8,128)(2,1)} %shard_map.130), calls=%async_computation.1 | async-start | bytes 131072 | tf_op jit(solution)/shard_map/all_to_all | solution.py:64
  60.3 4.4 %collective-permute-start.7 = (bf16[64,4096]{1,0:T(8,128)(2,1)}, bf16[64,4096]{1,0:T(8,128)(2,1)}, u32[]{:S(2)}, u32[]{:S(2)}) collective-permute-start(bf16[64,4096]{1,0:T(8,128)(2,1)} %copy-done), channel_id=1, source_target_pairs={{129,0},{130,1},{131,2},{132,3},{133,4},{134,5},{135,6},{128,7},{1... | collective-permute-start | bytes 1572872 | tf_op jit(solution)/shard_map/ppermute | solution.py:72
  64.7 8.0 %all-to-all-done.1.pair = bf16[8,2,16,128]{3,2,1,0:T(8,128)(2,1)S(1)} async-done(((bf16[8,2,16,128]{3,2,1,0:T(8,128)(2,1)}), bf16[8,2,16,128]{3,2,1,0:T(8,128)(2,1)S(1)}, u32[]{:S(2)}, u32[]{:S(2)}) %all-to-all-start.1) | async-done | bytes 65568 | tf_op jit(solution)/shard_map/all_to_all | solution.py:64
  72.8 0.0 collective-permute-done.1.refs_1_
  72.8 0.0 collective-permute-done.3.refs_3_
  72.8 1.9 %collective-permute-start.6 = (bf16[128,4096]{1,0:T(8,128)(2,1)S(1)}, bf16[128,4096]{1,0:T(8,128)(2,1)S(1)}, u32[]{:S(2)}, u32[]{:S(2)}) collective-permute-start(bf16[128,4096]{1,0:T(8,128)(2,1)S(1)} %collective-permute-done.3.refs_3_), channel_id=1, source_target_pairs={{0,64},{1,65},{2,66},{3,67},{4,68},{5,69},{6,70},{7,71},{8,72},{9,... | collective-permute-start | bytes 3145736 | tf_op jit(solution)/shard_map/ppermute | solution.py:72
  74.7 0.0 collective-permute-done.2.refs_2_
  74.7 2.4 %collective-permute-start.5 = (bf16[128,4096]{1,0:T(8,128)(2,1)}, bf16[128,4096]{1,0:T(8,128)(2,1)S(1)}, u32[]{:S(2)}, u32[]{:S(2)}) collective-permute-start(bf16[128,4096]{1,0:T(8,128)(2,1)} %collective-permute-done.2.refs_2_), channel_id=1, source_target_pairs={{0,64},{1,65},{2,66},{3,67},{4,68},{5,69},{6,70},{7,71},{8,72},{9,... | collective-permute-start | bytes 3145736 | tf_op jit(solution)/shard_map/ppermute | solution.py:72
  77.1 1.9 %collective-permute-start.4 = (bf16[128,4096]{1,0:T(8,128)(2,1)S(1)}, bf16[128,4096]{1,0:T(8,128)(2,1)S(1)}, u32[]{:S(2)}, u32[]{:S(2)}) collective-permute-start(bf16[128,4096]{1,0:T(8,128)(2,1)S(1)} %collective-permute-done.1.refs_1_), channel_id=1, source_target_pairs={{0,64},{1,65},{2,66},{3,67},{4,68},{5,69},{6,70},{7,71},{8,72},{9,... | collective-permute-start | bytes 3145736 | tf_op jit(solution)/shard_map/ppermute | solution.py:72
  79.1 0.0 collective-permute-done.7.refs_3_.refs_7_
  79.1 2.4 %collective-permute-start.8 = (bf16[64,4096]{1,0:T(8,128)(2,1)}, bf16[64,4096]{1,0:T(8,128)(2,1)S(1)}, u32[]{:S(2)}, u32[]{:S(2)}) collective-permute-start(bf16[64,4096]{1,0:T(8,128)(2,1)} %collective-permute-done.7.refs_3_.refs_7_), channel_id=1, source_target_pairs={{0,64},{1,65},{2,66},{3,67},{4,68},{5,69},{6,70},{7,71},{8,72},{9,... | collective-permute-start | bytes 1572872 | tf_op jit(solution)/shard_map/ppermute | solution.py:72
  81.5 4.4 %shard_map.132 = (bf16[512,128]{1,0:T(8,128)(2,1)}, f32[512,128]{1,0:T(8,128)}) custom-call(f32[1,128]{1,0:T(1,128)} %bias_in.3, bf16[4096,128]{1,0:T(8,128)(2,1)} %bitcast.7, bf16[128,4096]{1,0:T(8,128)(2,1)S(1)} %shard_map.131.refs_0_, bf16[128,4096]{1,0:T(8,128)(2,1)S(1)} %collective-permute-done.1.refs_1_, ...), custom_call_target="tpu_custom_call" | custom-call | tf_op jit(solution)/shard_map/pallas_call | solution.py:221
  85.9 0.0 collective-permute-done.8.refs_4_.refs_8_
  85.9 0.0 collective-permute-done.6.refs_2_.refs_6_
  86.0 0.0 collective-permute-done.5.refs_1_.refs_5_
  86.0 0.0 collective-permute-done.4.refs_0_.refs_4_
  86.0 5.0 %shard_map.133 = (bf16[512,128]{1,0:T(8,128)(2,1)}, f32[512,128]{1,0:T(8,128)}, bf16[8,128,128]{2,1,0:T(8,128)(2,1)}) custom-call(s32[18]{0:T(128)S(1)} %pad_add_fusion.spots.places, bf16[512,128]{1,0:T(8,128)(2,1)} %get-tuple-element.19.hidden_d, f32[1,128]{1,0:T(1,128)} %bias_in.3, bf16[128,128]{1,0:T(8,128)(2,1)} %bitcast.9, bf16[4096,128]{1,0:T(8,128)(2,1)} %bitcast.8, ...), custom_call_target="tpu_custom_call" | custom-call | tf_op jit(solution)/shard_map/pallas_call | solution.py:221
  91.0 15.7 %all_to_all.20.sums = bf16[8,128,128]{2,1,0:T(8,128)(2,1)S(1)} all-to-all(bf16[8,128,128]{2,1,0:T(8,128)(2,1)} %get-tuple-element.23), channel_id=1, replica_groups=mesh['ylo'=4,'core'=2,'x'=4,'yhi'=2,'z'=8] {'z'}, dimensions={0} | all-to-all | bytes 524288 | tf_op jit(solution)/shard_map/all_to_all | solution.py:64
  106.8 0.9 shard_map.134
  107.6 13.1 %all_to_all.21.back = bf16[8,128,128]{2,1,0:T(8,128)(2,1)S(1)} all-to-all(bf16[8,128,128]{2,1,0:T(8,128)(2,1)S(1)} %shard_map.134), channel_id=1, replica_groups=mesh['ylo'=4,'core'=2,'x'=4,'yhi'=2,'z'=8] {'z'}, dimensions={0} | all-to-all | bytes 524288 | tf_op jit(solution)/shard_map/all_to_all | solution.py:64
  120.7 6.6 %shard_map.135 = (f32[1,128]{1,0:T(1,128)}, f32[128,128]{1,0:T(8,128)}, f32[4096,128]{1,0:T(8,128)}) custom-call(s32[18]{0:T(128)S(1)} %pad_add_fusion.spots.places, bf16[8,128,128]{2,1,0:T(8,128)(2,1)S(1)} %all_to_all.21.back, bf16[512,128]{1,0:T(8,128)(2,1)} %get-tuple-element.19.hidden_d, bf16[512,128]{1,0:T(8,128)(2,1)} %get-tuple-element.25.hidden_s, ...), custom_call_target="tpu_custom_call" | custom-call | tf_op jit(solution)/shard_map/pallas_call | solution.py:221
Async XLA Ops:
  2.6 38.4 %all-to-all-start = ((bf16[32,2,4096]{2,1,0:T(2,128)(2,1)}), bf16[32,2,4096]{2,1,0:T(2,128)(2,1)S(1)}, u32[]{:S(2)}, u32[]{:S(2)}) async-start(bf16[32,2,4096]{2,1,0:T(2,128)(2,1)} %broadcast_in_dim.18), calls=%async_computation | async-start | bytes 1048576 | tf_op jit(solution)/shard_map/all_to_all | solution.py:64
  23.4 0.8 copy-start.1
  24.2 0.8 copy-start.2
  25.0 0.7 copy-start.3
  25.7 0.7 copy-start.4
  41.2 3.8 %collective-permute-start = (bf16[64,4096]{1,0:T(8,128)(2,1)S(1)}, bf16[64,4096]{1,0:T(8,128)(2,1)S(1)}, u32[]{:S(2)}, u32[]{:S(2)}) collective-permute-start(bf16[64,4096]{1,0:T(8,128)(2,1)S(1)} %reshape.11.refs_0_), channel_id=1, source_target_pairs={{0,64},{1,65},{2,66},{3,67},{4,68},{5,69},{6,70},{7,71},{8,72},{9,... | collective-permute-start | bytes 1572872 | tf_op jit(solution)/shard_map/ppermute | solution.py:72
  45.1 0.8 copy-start
  45.9 26.9 %collective-permute-start.1 = (bf16[128,4096]{1,0:T(8,128)(2,1)S(1)}, bf16[128,4096]{1,0:T(8,128)(2,1)S(1)}, u32[]{:S(2)}, u32[]{:S(2)}) collective-permute-start(bf16[128,4096]{1,0:T(8,128)(2,1)S(1)} %shard_map.131.refs_0_), channel_id=1, source_target_pairs={{16,0},{17,1},{18,2},{19,3},{20,4},{21,5},{22,6},{23,7},{24,8},{25... | collective-permute-start | bytes 3145736 | tf_op jit(solution)/shard_map/ppermute | solution.py:72
  49.4 23.4 %collective-permute-start.3 = (bf16[128,4096]{1,0:T(8,128)(2,1)S(1)}, bf16[128,4096]{1,0:T(8,128)(2,1)S(1)}, u32[]{:S(2)}, u32[]{:S(2)}) collective-permute-start(bf16[128,4096]{1,0:T(8,128)(2,1)S(1)} %shard_map.131.refs_0_), channel_id=1, source_target_pairs={{1,0},{2,1},{3,2},{4,3},{5,4},{6,5},{7,6},{0,7},{9,8},{10,9},{11,1... | collective-permute-start | bytes 3145736 | tf_op jit(solution)/shard_map/ppermute | solution.py:72
  53.4 21.3 %collective-permute-start.2 = (bf16[128,4096]{1,0:T(8,128)(2,1)S(1)}, bf16[128,4096]{1,0:T(8,128)(2,1)}, u32[]{:S(2)}, u32[]{:S(2)}) collective-permute-start(bf16[128,4096]{1,0:T(8,128)(2,1)S(1)} %shard_map.131.refs_0_), channel_id=1, source_target_pairs={{128,0},{129,1},{130,2},{131,3},{132,4},{133,5},{134,6},{135,7},{1... | collective-permute-start | bytes 3145736 | tf_op jit(solution)/shard_map/ppermute | solution.py:72
  55.3 17.5 %all-to-all-start.1 = ((bf16[8,2,16,128]{3,2,1,0:T(8,128)(2,1)}), bf16[8,2,16,128]{3,2,1,0:T(8,128)(2,1)S(1)}, u32[]{:S(2)}, u32[]{:S(2)}) async-start(bf16[8,2,16,128]{3,2,1,0:T(8,128)(2,1)} %shard_map.130), calls=%async_computation.1 | async-start | bytes 131072 | tf_op jit(solution)/shard_map/all_to_all | solution.py:64
  60.3 18.7 %collective-permute-start.7 = (bf16[64,4096]{1,0:T(8,128)(2,1)}, bf16[64,4096]{1,0:T(8,128)(2,1)}, u32[]{:S(2)}, u32[]{:S(2)}) collective-permute-start(bf16[64,4096]{1,0:T(8,128)(2,1)} %copy-done), channel_id=1, source_target_pairs={{129,0},{130,1},{131,2},{132,3},{133,4},{134,5},{135,6},{128,7},{1... | collective-permute-start | bytes 1572872 | tf_op jit(solution)/shard_map/ppermute | solution.py:72
  72.8 13.2 %collective-permute-start.6 = (bf16[128,4096]{1,0:T(8,128)(2,1)S(1)}, bf16[128,4096]{1,0:T(8,128)(2,1)S(1)}, u32[]{:S(2)}, u32[]{:S(2)}) collective-permute-start(bf16[128,4096]{1,0:T(8,128)(2,1)S(1)} %collective-permute-done.3.refs_3_), channel_id=1, source_target_pairs={{0,64},{1,65},{2,66},{3,67},{4,68},{5,69},{6,70},{7,71},{8,72},{9,... | collective-permute-start | bytes 3145736 | tf_op jit(solution)/shard_map/ppermute | solution.py:72
  74.7 11.2 %collective-permute-start.5 = (bf16[128,4096]{1,0:T(8,128)(2,1)}, bf16[128,4096]{1,0:T(8,128)(2,1)S(1)}, u32[]{:S(2)}, u32[]{:S(2)}) collective-permute-start(bf16[128,4096]{1,0:T(8,128)(2,1)} %collective-permute-done.2.refs_2_), channel_id=1, source_target_pairs={{0,64},{1,65},{2,66},{3,67},{4,68},{5,69},{6,70},{7,71},{8,72},{9,... | collective-permute-start | bytes 3145736 | tf_op jit(solution)/shard_map/ppermute | solution.py:72
  77.1 8.8 %collective-permute-start.4 = (bf16[128,4096]{1,0:T(8,128)(2,1)S(1)}, bf16[128,4096]{1,0:T(8,128)(2,1)S(1)}, u32[]{:S(2)}, u32[]{:S(2)}) collective-permute-start(bf16[128,4096]{1,0:T(8,128)(2,1)S(1)} %collective-permute-done.1.refs_1_), channel_id=1, source_target_pairs={{0,64},{1,65},{2,66},{3,67},{4,68},{5,69},{6,70},{7,71},{8,72},{9,... | collective-permute-start | bytes 3145736 | tf_op jit(solution)/shard_map/ppermute | solution.py:72
  79.1 6.9 %collective-permute-start.8 = (bf16[64,4096]{1,0:T(8,128)(2,1)}, bf16[64,4096]{1,0:T(8,128)(2,1)S(1)}, u32[]{:S(2)}, u32[]{:S(2)}) collective-permute-start(bf16[64,4096]{1,0:T(8,128)(2,1)} %collective-permute-done.7.refs_3_.refs_7_), channel_id=1, source_target_pairs={{0,64},{1,65},{2,66},{3,67},{4,68},{5,69},{6,70},{7,71},{8,72},{9,... | collective-permute-start | bytes 1572872 | tf_op jit(solution)/shard_map/ppermute | solution.py:72

commit v7 on v6

--- a/solution.py
+++ b/solution.py
@@ -113,34 +113,24 @@
         out[j] = residual
 
 
-def forward_kernel(pieces, head_in, bias_in, hidden, slopes, held, weights, sems):
-    copies = [pltpu.make_async_copy(head_in, weights, sems.at[0])]
-    spans, start = [], 0
-    for j, piece in enumerate(pieces):
-        rows = piece.shape[0]
-        target = held.at[pl.ds(start, rows)]
-        copies.append(pltpu.make_async_copy(piece, target, sems.at[j + 1]))
-        spans.append(slice(start, start + rows))
-        start += rows
-    for copy in copies:
-        copy.start()
-    copies[0].wait()
-    for span, copy in zip(spans, copies[1:]):
-        copy.wait()
-        pre = jnp.dot(held[span], weights[...], preferred_element_type=jnp.float32) + bias_in[...]
+def forward_kernel(pieces, head_in, bias_in, hidden, slopes):
+    start = 0
+    for piece in pieces:
+        span = slice(start, start + piece.shape[0])
+        start += piece.shape[0]
+        pre = jnp.dot(piece[...], head_in[...], preferred_element_type=jnp.float32) + bias_in[...]
         activated, slope = gelu_parts(pre)
         hidden[span] = activated.astype(jnp.bfloat16)
         slopes[span] = slope
 
 
-def direct_kernel(bias_in, head_in, *refs):
-    *pieces, hidden, slopes, held, weights, sems = refs
-    forward_kernel(pieces, head_in, bias_in, hidden, slopes, held, weights, sems)
-
-
-def late_kernel(spots, hidden_d, bias_in, head_out, head_in, *refs):
-    *pieces, hidden_s, slopes_s, out, held, weights, sems, wide = refs
-    forward_kernel(pieces, head_in, bias_in, hidden_s, slopes_s, held, weights, sems)
+def direct_kernel(head_in, bias_in, *refs):
+    forward_kernel(refs[:-2], head_in, bias_in, *refs[-2:])
+
+
+def late_kernel(spots, hidden_d, head_in, bias_in, head_out, *refs):
+    *pieces, hidden_s, slopes_s, out, wide = refs
+    forward_kernel(pieces, head_in, bias_in, hidden_s, slopes_s)
     for part, start in ((hidden_d, 0), (hidden_s, 8)):
         share = jnp.dot(part[...], head_out[...], preferred_element_type=jnp.float32)
         for j in range(8):
@@ -256,30 +246,23 @@
     (both,) = call(join_kernel, [whole((128, mine.shape[1]))], (mine, send(mine, CORES)))
     fetched = [send(both, from_chip(*d)) for d in ((1, 0, 0), (0, 1, 0), (0, 0, 1))]
     direct = [both] + fetched
+    first, second = head_in[0], head_out[0]
+    width = first.shape[0]
+    first_held, bias_held, second_held = hbm(first, bias_in, second)
+    activations = [KEPT((512, A), bf16), KEPT((512, A), f32)]
+    hidden_d, slopes_d = call(direct_kernel, activations, (first_held, bias_held, *direct))
+
     pair, both = lax.optimization_barrier((pair, both))
     pair = exchange(pair, ("x", "yhi"))
-    fetched[0], pair = lax.optimization_barrier((fetched[0], pair))
-    late = [send(piece, CORES) for piece in fetched] + [fourth, send(fourth, CORES)]
-
-    first, second = head_in[0], head_out[0]
-    first_held, bias_held, second_held = hbm(first, bias_in, second)
-    activations = [KEPT((512, A), bf16), KEPT((512, A), f32)]
-    width = first.shape[0]
-    landing = [
-        pltpu.VMEM((512, width), bf16),
-        pltpu.VMEM((width, A), bf16),
-        pltpu.SemaphoreType.DMA((6,)),
-    ]
-    hidden_d, slopes_d = call(
-        direct_kernel, activations, (bias_held,), fetched=(first_held, *direct), scratch=landing
-    )
+    passed, pair, hidden_d = lax.optimization_barrier((fetched[0], pair, hidden_d))
+    late = [send(piece, CORES) for piece in [passed] + fetched[1:]]
+    late += [fourth, send(fourth, CORES)]
     hidden_s, slopes_s, shares = call(
         late_kernel,
         activations + [KEPT((8, A, A), bf16)],
-        (*hbm(hidden_d), bias_held, second_held),
+        (*hbm(hidden_d), first, bias_in, second, *late),
         places,
-        fetched=(first_held, *late),
-        scratch=landing + [pltpu.VMEM((8, 16, 8, A), f32)],
+        scratch=[pltpu.VMEM((8, 16, 8, A), f32)],
     )
     sums = exchange(shares, "z")
     (copies,) = call(

time: 128 us -> 129 us (level)
  the two profiles are of different devices: /device:TPU:8 before, /device:TPU:1 now
where the time goes in v7:
time: 129 us; the launch traced here: 128 us
  starting transfers between devices  47.7 us (37%)
  blocking collectives  30.9 us (24%)
  waiting for transfers between devices  23 us (18%)
  Pallas kernels  15.6 us (12%)
  local copies, waits for them, and re-layouts  8.43 us (7%)
  other arithmetic  1.38 us (1%)
    all_to_all x2, blocking collectives, exchange(): lax.all_to_all(blocks, axis, 0, 0, tiled=True, axis_index_groups=groups)  30.9 us
    ppermute x9, starting transfers between devices, send(): return lax.ppermute(block, ALL, pairs)  24 us
    all_to_all x2, starting transfers between devices, exchange(): lax.all_to_all(blocks, axis, 0, 0, tiled=True, axis_index_groups=groups)  23.8 us
    pallas_call x6, Pallas kernels, call(): pl.pallas_call(kernel, out_shape=outs, in_specs=[smem] * len(scalars) + [...  15.6 us
    all_to_all x2, waiting for transfers between devices, exchange(): lax.all_to_all(blocks, axis, 0, 0, tiled=True, axis_index_groups=groups)  12.8 us
    ppermute x9, waiting for transfers between devices, send(): return lax.ppermute(block, ALL, pairs)  10.2 us
    unnamed x16, local copies, waits for them, and re-layouts  4.94 us
  transfers between devices with their start and end apart: 11, of which 6 were waited for; matrix products, arithmetic and copies ran while one was open for 2% of the time, Pallas kernels for 4%

profile of v7, /device:TPU:1, one launch (start us, length us, event | category | flops | bytes accessed | tf_op | source)
XLA Modules:
  0.0 127.8 jit_solution(6056441251546363428)
XLA Ops:
  0.6 2.0 %broadcast_in_dim.18 = bf16[32,2,4096]{2,1,0:T(2,128)(2,1)} broadcast(bf16[2,4096]{1,0:T(2,128)(2,1)} %param.11), dimensions={1,2} | broadcast | bytes 540672 | tf_op jit(solution)/shard_map/broadcast_in_dim | solution.py:68
  2.6 18.2 %all-to-all-start = ((bf16[32,2,4096]{2,1,0:T(2,128)(2,1)}), bf16[32,2,4096]{2,1,0:T(2,128)(2,1)S(1)}, u32[]{:S(2)}, u32[]{:S(2)}) async-start(bf16[32,2,4096]{2,1,0:T(2,128)(2,1)} %broadcast_in_dim.18), calls=%async_computation | async-start | bytes 1048576 | tf_op jit(solution)/shard_map/all_to_all | solution.py:64
  20.8 1.3 %constant_dynamic-slice_fusion = s32[1,1]{1,0:T(1,128)} fusion(s32[1,8]{1,0:T(1,128)} %block_owner.1, s32[]{:T(128)S(6)} %select_n.17), kind=kLoop, calls=%fused_computation.11 | loop fusion | bytes 12 | tf_op jit(solution)/shard_map/jit(dynamic_index_in_dim)/dynamic_slice | solution.py:230
  22.1 0.8 copy-done.3
  23.0 0.8 copy-done.4
  23.7 0.0 copy-start.6
  23.7 0.7 copy-done.6
  24.4 0.0 copy-start.7
  24.4 0.7 copy-done.7
  25.0 1.2 shard_map.130
  26.3 0.7 fusion
  26.9 0.7 pad_add_fusion.spots.places
  27.6 12.8 %all-to-all-done = bf16[32,2,4096]{2,1,0:T(2,128)(2,1)S(1)} async-done(((bf16[32,2,4096]{2,1,0:T(2,128)(2,1)}), bf16[32,2,4096]{2,1,0:T(2,128)(2,1)S(1)}, u32[]{:S(2)}, u32[]{:S(2)}) %all-to-all-start) | async-done | bytes 524320 | tf_op jit(solution)/shard_map/all_to_all | solution.py:64
  40.4 0.2 reshape.11.refs_0_
  40.6 4.2 %collective-permute-start = (bf16[64,4096]{1,0:T(8,128)(2,1)S(1)}, bf16[64,4096]{1,0:T(8,128)(2,1)S(1)}, u32[]{:S(2)}, u32[]{:S(2)}) collective-permute-start(bf16[64,4096]{1,0:T(8,128)(2,1)S(1)} %reshape.11.refs_0_), channel_id=1, source_target_pairs={{0,64},{1,65},{2,66},{3,67},{4,68},{5,69},{6,70},{7,71},{8,72},{9,... | collective-permute-start | bytes 1572872 | tf_op jit(solution)/shard_map/ppermute | solution.py:72
  44.9 1.5 %collective-permute-done.refs_1_ = bf16[64,4096]{1,0:T(8,128)(2,1)S(1)} collective-permute-done((bf16[64,4096]{1,0:T(8,128)(2,1)S(1)}, bf16[64,4096]{1,0:T(8,128)(2,1)S(1)}, u32[]{:S(2)}, u32[]{:S(2)}) %collective-permute-start) | collective-permute-done | bytes 524320 | tf_op jit(solution)/shard_map/ppermute | solution.py:72
  46.4 0.1 shard_map.131.refs_0_
  46.4 0.0 copy-start.1
  46.5 0.8 copy-done.1
  47.2 2.8 %collective-permute-start.3 = (bf16[128,4096]{1,0:T(8,128)(2,1)S(1)}, bf16[128,4096]{1,0:T(8,128)(2,1)S(1)}, u32[]{:S(2)}, u32[]{:S(2)}) collective-permute-start(bf16[128,4096]{1,0:T(8,128)(2,1)S(1)} %shard_map.131.refs_0_), channel_id=1, source_target_pairs={{1,0},{2,1},{3,2},{4,3},{5,4},{6,5},{7,6},{0,7},{9,8},{10,9},{11,1... | collective-permute-start | bytes 3145736 | tf_op jit(solution)/shard_map/ppermute | solution.py:72
  50.1 2.1 %collective-permute-start.2 = (bf16[128,4096]{1,0:T(8,128)(2,1)S(1)}, bf16[128,4096]{1,0:T(8,128)(2,1)S(1)}, u32[]{:S(2)}, u32[]{:S(2)}) collective-permute-start(bf16[128,4096]{1,0:T(8,128)(2,1)S(1)} %shard_map.131.refs_0_), channel_id=1, source_target_pairs={{128,0},{129,1},{130,2},{131,3},{132,4},{133,5},{134,6},{135,7},{1... | collective-permute-start | bytes 3145736 | tf_op jit(solution)/shard_map/ppermute | solution.py:72
  52.2 3.2 %collective-permute-start.1 = (bf16[128,4096]{1,0:T(8,128)(2,1)S(1)}, bf16[128,4096]{1,0:T(8,128)(2,1)}, u32[]{:S(2)}, u32[]{:S(2)}) collective-permute-start(bf16[128,4096]{1,0:T(8,128)(2,1)S(1)} %shard_map.131.refs_0_), channel_id=1, source_target_pairs={{16,0},{17,1},{18,2},{19,3},{20,4},{21,5},{22,6},{23,7},{24,8},{25... | collective-permute-start | bytes 3145736 | tf_op jit(solution)/shard_map/ppermute | solution.py:72
  55.4 5.6 %all-to-all-start.1 = ((bf16[8,2,16,128]{3,2,1,0:T(8,128)(2,1)}), bf16[8,2,16,128]{3,2,1,0:T(8,128)(2,1)S(1)}, u32[]{:S(2)}, u32[]{:S(2)}) async-start(bf16[8,2,16,128]{3,2,1,0:T(8,128)(2,1)} %shard_map.130), calls=%async_computation.1 | async-start | bytes 131072 | tf_op jit(solution)/shard_map/all_to_all | solution.py:64
  61.0 1.9 %collective-permute-start.7 = (bf16[64,4096]{1,0:T(8,128)(2,1)}, bf16[64,4096]{1,0:T(8,128)(2,1)}, u32[]{:S(2)}, u32[]{:S(2)}) collective-permute-start(bf16[64,4096]{1,0:T(8,128)(2,1)} %copy-done.1), channel_id=1, source_target_pairs={{129,0},{130,1},{131,2},{132,3},{133,4},{134,5},{135,6},{128,7},{1... | collective-permute-start | bytes 1572872 | tf_op jit(solution)/shard_map/ppermute | solution.py:72
  62.9 1.1 collective-permute-done.3.refs_3_
  64.0 3.2 %collective-permute-done.2.refs_2_ = bf16[128,4096]{1,0:T(8,128)(2,1)S(1)} collective-permute-done((bf16[128,4096]{1,0:T(8,128)(2,1)S(1)}, bf16[128,4096]{1,0:T(8,128)(2,1)S(1)}, u32[]{:S(2)}, u32[]{:S(2)}) %collective-permute-start.2) | collective-permute-done | bytes 1048608 | tf_op jit(solution)/shard_map/ppermute | solution.py:72
  67.2 2.3 %collective-permute-done.1.refs_1_ = bf16[128,4096]{1,0:T(8,128)(2,1)} collective-permute-done((bf16[128,4096]{1,0:T(8,128)(2,1)S(1)}, bf16[128,4096]{1,0:T(8,128)(2,1)}, u32[]{:S(2)}, u32[]{:S(2)}) %collective-permute-start.1) | collective-permute-done | bytes 1048608 | tf_op jit(solution)/shard_map/ppermute | solution.py:72
  69.5 0.0 copy-start.2
  69.5 3.6 %shard_map.132 = (bf16[512,128]{1,0:T(8,128)(2,1)}, f32[512,128]{1,0:T(8,128)}) custom-call(bf16[4096,128]{1,0:T(8,128)(2,1)} %bitcast.7, f32[1,128]{1,0:T(1,128)} %bias_in.3, bf16[128,4096]{1,0:T(8,128)(2,1)S(1)} %shard_map.131.refs_0_, bf16[128,4096]{1,0:T(8,128)(2,1)} %collective-permute-done.1.refs_1_, ...), custom_call_target="tpu_custom_call" | custom-call | tf_op jit(solution)/shard_map/pallas_call | solution.py:211
  73.1 0.0 all-to-all-done.1.pair
  73.1 3.5 %collective-permute-start.6 = (bf16[128,4096]{1,0:T(8,128)(2,1)S(1)}, bf16[128,4096]{1,0:T(8,128)(2,1)S(1)}, u32[]{:S(2)}, u32[]{:S(2)}) collective-permute-start(bf16[128,4096]{1,0:T(8,128)(2,1)S(1)} %collective-permute-done.3.refs_3_), channel_id=1, source_target_pairs={{0,64},{1,65},{2,66},{3,67},{4,68},{5,69},{6,70},{7,71},{8,72},{9,... | collective-permute-start | bytes 3145736 | tf_op jit(solution)/shard_map/ppermute | solution.py:72
  76.6 1.9 %collective-permute-start.5 = (bf16[128,4096]{1,0:T(8,128)(2,1)S(1)}, bf16[128,4096]{1,0:T(8,128)(2,1)S(1)}, u32[]{:S(2)}, u32[]{:S(2)}) collective-permute-start(bf16[128,4096]{1,0:T(8,128)(2,1)S(1)} %collective-permute-done.2.refs_2_), channel_id=1, source_target_pairs={{0,64},{1,65},{2,66},{3,67},{4,68},{5,69},{6,70},{7,71},{8,72},{9,... | collective-permute-start | bytes 3145736 | tf_op jit(solution)/shard_map/ppermute | solution.py:72
  78.5 2.4 %collective-permute-start.4 = (bf16[128,4096]{1,0:T(8,128)(2,1)}, bf16[128,4096]{1,0:T(8,128)(2,1)S(1)}, u32[]{:S(2)}, u32[]{:S(2)}) collective-permute-start(bf16[128,4096]{1,0:T(8,128)(2,1)} %collective-permute-done.1.refs_1_), channel_id=1, source_target_pairs={{0,64},{1,65},{2,66},{3,67},{4,68},{5,69},{6,70},{7,71},{8,72},{9,... | collective-permute-start | bytes 3145736 | tf_op jit(solution)/shard_map/ppermute | solution.py:72
  80.9 0.0 collective-permute-done.7.refs_3_.refs_7_
  80.9 1.9 %collective-permute-start.8 = (bf16[64,4096]{1,0:T(8,128)(2,1)}, bf16[64,4096]{1,0:T(8,128)(2,1)S(1)}, u32[]{:S(2)}, u32[]{:S(2)}) collective-permute-start(bf16[64,4096]{1,0:T(8,128)(2,1)} %collective-permute-done.7.refs_3_.refs_7_), channel_id=1, source_target_pairs={{0,64},{1,65},{2,66},{3,67},{4,68},{5,69},{6,70},{7,71},{8,72},{9,... | collective-permute-start | bytes 1572872 | tf_op jit(solution)/shard_map/ppermute | solution.py:72
  82.9 2.1 %collective-permute-done.8.refs_4_.refs_8_ = bf16[64,4096]{1,0:T(8,128)(2,1)S(1)} collective-permute-done((bf16[64,4096]{1,0:T(8,128)(2,1)}, bf16[64,4096]{1,0:T(8,128)(2,1)S(1)}, u32[]{:S(2)}, u32[]{:S(2)}) %collective-permute-start.8) | collective-permute-done | bytes 524320 | tf_op jit(solution)/shard_map/ppermute | solution.py:72
  85.0 0.0 collective-permute-done.6.refs_2_.refs_6_
  85.0 0.0 collective-permute-done.5.refs_1_.refs_5_
  85.0 0.0 collective-permute-done.4.refs_0_.refs_4_
  85.0 0.0 copy-done.2
  85.0 0.0 copy-done.5
  85.0 0.0 copy-start
  85.0 1.2 copy-done
  86.2 3.3 %shard_map.133 = (bf16[512,128]{1,0:T(8,128)(2,1)}, f32[512,128]{1,0:T(8,128)}, bf16[8,128,128]{2,1,0:T(8,128)(2,1)}) custom-call(s32[18]{0:T(128)S(1)} %pad_add_fusion.spots.places, bf16[512,128]{1,0:T(8,128)(2,1)} %get-tuple-element.23.hidden_d, bf16[4096,128]{1,0:T(8,128)(2,1)S(1)} %bitcast.8, f32[1,128]{1,0:T(1,128)S(1)} %copy-done.5, ...), custom_call_target="tpu_custom_call" | custom-call | tf_op jit(solution)/shard_map/pallas_call | solution.py:211
  89.5 16.7 %all_to_all.20.sums = bf16[8,128,128]{2,1,0:T(8,128)(2,1)S(1)} all-to-all(bf16[8,128,128]{2,1,0:T(8,128)(2,1)} %get-tuple-element.25), channel_id=1, replica_groups=mesh['ylo'=4,'core'=2,'x'=4,'yhi'=2,'z'=8] {'z'}, dimensions={0} | all-to-all | bytes 524288 | tf_op jit(solution)/shard_map/all_to_all | solution.py:64
  106.2 0.9 shard_map.134
  107.1 14.2 %all_to_all.21.back = bf16[8,128,128]{2,1,0:T(8,128)(2,1)S(1)} all-to-all(bf16[8,128,128]{2,1,0:T(8,128)(2,1)S(1)} %shard_map.134), channel_id=1, replica_groups=mesh['ylo'=4,'core'=2,'x'=4,'yhi'=2,'z'=8] {'z'}, dimensions={0} | all-to-all | bytes 524288 | tf_op jit(solution)/shard_map/all_to_all | solution.py:64
  121.2 6.6 %shard_map.135 = (f32[1,128]{1,0:T(1,128)}, f32[128,128]{1,0:T(8,128)}, f32[4096,128]{1,0:T(8,128)}) custom-call(s32[18]{0:T(128)S(1)} %pad_add_fusion.spots.places, bf16[8,128,128]{2,1,0:T(8,128)(2,1)S(1)} %all_to_all.21.back, bf16[512,128]{1,0:T(8,128)(2,1)} %get-tuple-element.23.hidden_d, bf16[512,128]{1,0:T(8,128)(2,1)} %get-tuple-element.27.hidden_s, ...), custom_call_target="tpu_custom_call" | custom-call | tf_op jit(solution)/shard_map/pallas_call | solution.py:211
  (3 shorter events, 0.0 us)
Async XLA Ops:
  2.6 37.8 %all-to-all-start = ((bf16[32,2,4096]{2,1,0:T(2,128)(2,1)}), bf16[32,2,4096]{2,1,0:T(2,128)(2,1)S(1)}, u32[]{:S(2)}, u32[]{:S(2)}) async-start(bf16[32,2,4096]{2,1,0:T(2,128)(2,1)} %broadcast_in_dim.18), calls=%async_computation | async-start | bytes 1048576 | tf_op jit(solution)/shard_map/all_to_all | solution.py:64
  22.1 0.8 copy-start.3
  22.9 0.8 copy-start.4
  23.7 0.7 copy-start.6
  24.4 0.7 copy-start.7
  40.6 5.7 %collective-permute-start = (bf16[64,4096]{1,0:T(8,128)(2,1)S(1)}, bf16[64,4096]{1,0:T(8,128)(2,1)S(1)}, u32[]{:S(2)}, u32[]{:S(2)}) collective-permute-start(bf16[64,4096]{1,0:T(8,128)(2,1)S(1)} %reshape.11.refs_0_), channel_id=1, source_target_pairs={{0,64},{1,65},{2,66},{3,67},{4,68},{5,69},{6,70},{7,71},{8,72},{9,... | collective-permute-start | bytes 1572872 | tf_op jit(solution)/shard_map/ppermute | solution.py:72
  46.4 0.8 copy-start.1
  47.2 16.7 %collective-permute-start.3 = (bf16[128,4096]{1,0:T(8,128)(2,1)S(1)}, bf16[128,4096]{1,0:T(8,128)(2,1)S(1)}, u32[]{:S(2)}, u32[]{:S(2)}) collective-permute-start(bf16[128,4096]{1,0:T(8,128)(2,1)S(1)} %shard_map.131.refs_0_), channel_id=1, source_target_pairs={{1,0},{2,1},{3,2},{4,3},{5,4},{6,5},{7,6},{0,7},{9,8},{10,9},{11,1... | collective-permute-start | bytes 3145736 | tf_op jit(solution)/shard_map/ppermute | solution.py:72
  50.1 17.1 %collective-permute-start.2 = (bf16[128,4096]{1,0:T(8,128)(2,1)S(1)}, bf16[128,4096]{1,0:T(8,128)(2,1)S(1)}, u32[]{:S(2)}, u32[]{:S(2)}) collective-permute-start(bf16[128,4096]{1,0:T(8,128)(2,1)S(1)} %shard_map.131.refs_0_), channel_id=1, source_target_pairs={{128,0},{129,1},{130,2},{131,3},{132,4},{133,5},{134,6},{135,7},{1... | collective-permute-start | bytes 3145736 | tf_op jit(solution)/shard_map/ppermute | solution.py:72
  52.2 17.3 %collective-permute-start.1 = (bf16[128,4096]{1,0:T(8,128)(2,1)S(1)}, bf16[128,4096]{1,0:T(8,128)(2,1)}, u32[]{:S(2)}, u32[]{:S(2)}) collective-permute-start(bf16[128,4096]{1,0:T(8,128)(2,1)S(1)} %shard_map.131.refs_0_), channel_id=1, source_target_pairs={{16,0},{17,1},{18,2},{19,3},{20,4},{21,5},{22,6},{23,7},{24,8},{25... | collective-permute-start | bytes 3145736 | tf_op jit(solution)/shard_map/ppermute | solution.py:72
  55.4 17.7 %all-to-all-start.1 = ((bf16[8,2,16,128]{3,2,1,0:T(8,128)(2,1)}), bf16[8,2,16,128]{3,2,1,0:T(8,128)(2,1)S(1)}, u32[]{:S(2)}, u32[]{:S(2)}) async-start(bf16[8,2,16,128]{3,2,1,0:T(8,128)(2,1)} %shard_map.130), calls=%async_computation.1 | async-start | bytes 131072 | tf_op jit(solution)/shard_map/all_to_all | solution.py:64
  61.0 20.0 %collective-permute-start.7 = (bf16[64,4096]{1,0:T(8,128)(2,1)}, bf16[64,4096]{1,0:T(8,128)(2,1)}, u32[]{:S(2)}, u32[]{:S(2)}) collective-permute-start(bf16[64,4096]{1,0:T(8,128)(2,1)} %copy-done.1), channel_id=1, source_target_pairs={{129,0},{130,1},{131,2},{132,3},{133,4},{134,5},{135,6},{128,7},{1... | collective-permute-start | bytes 1572872 | tf_op jit(solution)/shard_map/ppermute | solution.py:72
  69.5 15.5 %copy-start.2 = (bf16[1,128,128]{2,1,0:T(8,128)(2,1)S(1)}, bf16[1,128,128]{2,1,0:T(8,128)(2,1)}, u32[]{:S(2)}) copy-start(bf16[1,128,128]{2,1,0:T(8,128)(2,1)} %param.14) | copy-start | bytes 98308
  69.5 15.5 %copy-start.5 = (f32[1,128]{1,0:T(1,128)S(1)}, f32[1,128]{1,0:T(1,128)}, u32[]{:S(2)}) copy-start(f32[1,128]{1,0:T(1,128)} %bias_in.3) | copy-start | bytes 1540
  73.1 11.9 %collective-permute-start.6 = (bf16[128,4096]{1,0:T(8,128)(2,1)S(1)}, bf16[128,4096]{1,0:T(8,128)(2,1)S(1)}, u32[]{:S(2)}, u32[]{:S(2)}) collective-permute-start(bf16[128,4096]{1,0:T(8,128)(2,1)S(1)} %collective-permute-done.3.refs_3_), channel_id=1, source_target_pairs={{0,64},{1,65},{2,66},{3,67},{4,68},{5,69},{6,70},{7,71},{8,72},{9,... | collective-permute-start | bytes 3145736 | tf_op jit(solution)/shard_map/ppermute | solution.py:72
  76.6 8.4 %collective-permute-start.5 = (bf16[128,4096]{1,0:T(8,128)(2,1)S(1)}, bf16[128,4096]{1,0:T(8,128)(2,1)S(1)}, u32[]{:S(2)}, u32[]{:S(2)}) collective-permute-start(bf16[128,4096]{1,0:T(8,128)(2,1)S(1)} %collective-permute-done.2.refs_2_), channel_id=1, source_target_pairs={{0,64},{1,65},{2,66},{3,67},{4,68},{5,69},{6,70},{7,71},{8,72},{9,... | collective-permute-start | bytes 3145736 | tf_op jit(solution)/shard_map/ppermute | solution.py:72
  78.5 6.4 %collective-permute-start.4 = (bf16[128,4096]{1,0:T(8,128)(2,1)}, bf16[128,4096]{1,0:T(8,128)(2,1)S(1)}, u32[]{:S(2)}, u32[]{:S(2)}) collective-permute-start(bf16[128,4096]{1,0:T(8,128)(2,1)} %collective-permute-done.1.refs_1_), channel_id=1, source_target_pairs={{0,64},{1,65},{2,66},{3,67},{4,68},{5,69},{6,70},{7,71},{8,72},{9,... | collective-permute-start | bytes 3145736 | tf_op jit(solution)/shard_map/ppermute | solution.py:72
  80.9 4.0 %collective-permute-start.8 = (bf16[64,4096]{1,0:T(8,128)(2,1)}, bf16[64,4096]{1,0:T(8,128)(2,1)S(1)}, u32[]{:S(2)}, u32[]{:S(2)}) collective-permute-start(bf16[64,4096]{1,0:T(8,128)(2,1)} %collective-permute-done.7.refs_3_.refs_7_), channel_id=1, source_target_pairs={{0,64},{1,65},{2,66},{3,67},{4,68},{5,69},{6,70},{7,71},{8,72},{9,... | collective-permute-start | bytes 1572872 | tf_op jit(solution)/shard_map/ppermute | solution.py:72
  85.0 1.2 copy-start

commit v8 on v7

--- a/solution.py
+++ b/solution.py
@@ -72,11 +72,10 @@
     return lax.ppermute(block, ALL, pairs)
 
 
-def join_kernel(*refs):
-    start = 0
-    for piece in refs[:-1]:
-        refs[-1][start : start + piece.shape[0]] = piece[...]
-        start += piece.shape[0]
+def join_kernel(mine, theirs, both, kept):
+    both[:64] = mine[...]
+    both[64:] = theirs[...]
+    kept[...] = mine[...]
 
 
 def prepare_kernel(block_owner, block_mask, targets, entry_mask, out):
@@ -242,8 +241,12 @@
     )
     mine = spread(embeddings, ALL, 32, CLASSES).reshape(64, -1)
     mine, pair, places = lax.optimization_barrier((mine, pair, places))
-    fourth = send(mine, from_chip(0, 1, 1))
-    (both,) = call(join_kernel, [whole((128, mine.shape[1]))], (mine, send(mine, CORES)))
+    both, kept = call(
+        join_kernel,
+        [whole((128, mine.shape[1])), KEPT(mine.shape, bf16)],
+        (mine, send(mine, CORES)),
+    )
+    fourth = send(kept, from_chip(0, 1, 1))
     fetched = [send(both, from_chip(*d)) for d in ((1, 0, 0), (0, 1, 0), (0, 0, 1))]
     direct = [both] + fetched
     first, second = head_in[0], head_out[0]
@@ -260,7 +263,7 @@
     hidden_s, slopes_s, shares = call(
         late_kernel,
         activations + [KEPT((8, A, A), bf16)],
-        (*hbm(hidden_d), first, bias_in, second, *late),
+        (*hbm(hidden_d), first_held, bias_held, second_held, *late),
         places,
         scratch=[pltpu.VMEM((8, 16, 8, A), f32)],
     )

time: 129 us -> 128 us (level)
  local copies, waits for them, and re-layouts: 8.43 us -> 6.35 us
    unnamed x16 -> x8, local copies, waits for them, and re-layouts: 4.94 us -> 2.93 us
where the time goes in v8:
time: 128 us; the launch traced here: 127 us
  starting transfers between devices  47.7 us (37%)
  blocking collectives  30.9 us (24%)
  waiting for transfers between devices  23.1 us (18%)
  Pallas kernels  16.7 us (13%)
  local copies, waits for them, and re-layouts  6.35 us (5%)
  other arithmetic  1.32 us (1%)
    all_to_all x2, blocking collectives, exchange(): lax.all_to_all(blocks, axis, 0, 0, tiled=True, axis_index_groups=groups)  30.9 us
    ppermute x9, starting transfers between devices, send(): return lax.ppermute(block, ALL, pairs)  24 us
    all_to_all x2, starting transfers between devices, exchange(): lax.all_to_all(blocks, axis, 0, 0, tiled=True, axis_index_groups=groups)  23.8 us
    pallas_call x6, Pallas kernels, call(): pl.pallas_call(kernel, out_shape=outs, in_specs=[smem] * len(scalars) + [...  16.7 us
    all_to_all x2, waiting for transfers between devices, exchange(): lax.all_to_all(blocks, axis, 0, 0, tiled=True, axis_index_groups=groups)  12.9 us
    ppermute x9, waiting for transfers between devices, send(): return lax.ppermute(block, ALL, pairs)  10.2 us
    unnamed x8, local copies, waits for them, and re-layouts  2.93 us
  transfers between devices with their start and end apart: 11, of which 6 were waited for; matrix products, arithmetic and copies ran while one was open for 2% of the time, Pallas kernels for 4%

profile of v8, /device:TPU:1, one launch (start us, length us, event | category | flops | bytes accessed | tf_op | source)
XLA Modules:
  0.0 126.9 jit_solution(1737567388350544758)
XLA Ops:
  0.6 2.0 %broadcast_in_dim.18 = bf16[32,2,4096]{2,1,0:T(2,128)(2,1)} broadcast(bf16[2,4096]{1,0:T(2,128)(2,1)} %param.11), dimensions={1,2} | broadcast | bytes 540672 | tf_op jit(solution)/shard_map/broadcast_in_dim | solution.py:68
  2.6 18.2 %all-to-all-start = ((bf16[32,2,4096]{2,1,0:T(2,128)(2,1)}), bf16[32,2,4096]{2,1,0:T(2,128)(2,1)S(1)}, u32[]{:S(2)}, u32[]{:S(2)}) async-start(bf16[32,2,4096]{2,1,0:T(2,128)(2,1)} %broadcast_in_dim.18), calls=%async_computation | async-start | bytes 1048576 | tf_op jit(solution)/shard_map/all_to_all | solution.py:64
  20.8 1.2 constant_dynamic-slice_fusion
  22.0 0.0 copy-start
  22.0 0.8 copy-done
  22.9 0.0 copy-start.1
  22.9 0.8 copy-done.1
  23.6 0.0 copy-start.2
  23.6 0.7 copy-done.2
  24.3 0.0 copy-start.3
  24.3 0.7 copy-done.3
  25.0 1.2 shard_map.130
  26.2 0.7 fusion
  26.9 0.6 pad_add_fusion.spots.places
  27.5 12.9 %all-to-all-done = bf16[32,2,4096]{2,1,0:T(2,128)(2,1)S(1)} async-done(((bf16[32,2,4096]{2,1,0:T(2,128)(2,1)}), bf16[32,2,4096]{2,1,0:T(2,128)(2,1)S(1)}, u32[]{:S(2)}, u32[]{:S(2)}) %all-to-all-start) | async-done | bytes 524320 | tf_op jit(solution)/shard_map/all_to_all | solution.py:64
  40.4 0.2 reshape.11.mine
  40.6 4.2 %collective-permute-start = (bf16[64,4096]{1,0:T(8,128)(2,1)S(1)}, bf16[64,4096]{1,0:T(8,128)(2,1)S(1)}, u32[]{:S(2)}, u32[]{:S(2)}) collective-permute-start(bf16[64,4096]{1,0:T(8,128)(2,1)S(1)} %reshape.11.mine), channel_id=1, source_target_pairs={{0,64},{1,65},{2,66},{3,67},{4,68},{5,69},{6,70},{7,71},{8,72},{9,... | collective-permute-start | bytes 1572872 | tf_op jit(solution)/shard_map/ppermute | solution.py:72
  44.9 1.5 %collective-permute-done.theirs = bf16[64,4096]{1,0:T(8,128)(2,1)S(1)} collective-permute-done((bf16[64,4096]{1,0:T(8,128)(2,1)S(1)}, bf16[64,4096]{1,0:T(8,128)(2,1)S(1)}, u32[]{:S(2)}, u32[]{:S(2)}) %collective-permute-start) | collective-permute-done | bytes 524320 | tf_op jit(solution)/shard_map/ppermute | solution.py:72
  46.4 0.9 shard_map.131
  47.3 2.8 %collective-permute-start.3 = (bf16[128,4096]{1,0:T(8,128)(2,1)S(1)}, bf16[128,4096]{1,0:T(8,128)(2,1)S(1)}, u32[]{:S(2)}, u32[]{:S(2)}) collective-permute-start(bf16[128,4096]{1,0:T(8,128)(2,1)S(1)} %get-tuple-element.22.refs_0_), channel_id=1, source_target_pairs={{1,0},{2,1},{3,2},{4,3},{5,4},{6,5},{7,6},{0,7},{9,8},{10,9},{11,1... | collective-permute-start | bytes 3145736 | tf_op jit(solution)/shard_map/ppermute | solution.py:72
  50.1 2.1 %collective-permute-start.2 = (bf16[128,4096]{1,0:T(8,128)(2,1)S(1)}, bf16[128,4096]{1,0:T(8,128)(2,1)S(1)}, u32[]{:S(2)}, u32[]{:S(2)}) collective-permute-start(bf16[128,4096]{1,0:T(8,128)(2,1)S(1)} %get-tuple-element.22.refs_0_), channel_id=1, source_target_pairs={{128,0},{129,1},{130,2},{131,3},{132,4},{133,5},{134,6},{135,7},{1... | collective-permute-start | bytes 3145736 | tf_op jit(solution)/shard_map/ppermute | solution.py:72
  52.2 3.2 %collective-permute-start.1 = (bf16[128,4096]{1,0:T(8,128)(2,1)S(1)}, bf16[128,4096]{1,0:T(8,128)(2,1)}, u32[]{:S(2)}, u32[]{:S(2)}) collective-permute-start(bf16[128,4096]{1,0:T(8,128)(2,1)S(1)} %get-tuple-element.22.refs_0_), channel_id=1, source_target_pairs={{16,0},{17,1},{18,2},{19,3},{20,4},{21,5},{22,6},{23,7},{24,8},{25... | collective-permute-start | bytes 3145736 | tf_op jit(solution)/shard_map/ppermute | solution.py:72
  55.4 5.6 %all-to-all-start.1 = ((bf16[8,2,16,128]{3,2,1,0:T(8,128)(2,1)}), bf16[8,2,16,128]{3,2,1,0:T(8,128)(2,1)S(1)}, u32[]{:S(2)}, u32[]{:S(2)}) async-start(bf16[8,2,16,128]{3,2,1,0:T(8,128)(2,1)} %shard_map.130), calls=%async_computation.1 | async-start | bytes 131072 | tf_op jit(solution)/shard_map/all_to_all | solution.py:64
  61.0 1.9 %collective-permute-start.7 = (bf16[64,4096]{1,0:T(8,128)(2,1)}, bf16[64,4096]{1,0:T(8,128)(2,1)}, u32[]{:S(2)}, u32[]{:S(2)}) collective-permute-start(bf16[64,4096]{1,0:T(8,128)(2,1)} %get-tuple-element.28), channel_id=1, source_target_pairs={{129,0},{130,1},{131,2},{132,3},{133,4},{134,5},{135,6},{128,7},{1... | collective-permute-start | bytes 1572872 | tf_op jit(solution)/shard_map/ppermute | solution.py:72
  62.9 1.1 collective-permute-done.3.refs_3_
  64.0 3.2 %collective-permute-done.2.refs_2_ = bf16[128,4096]{1,0:T(8,128)(2,1)S(1)} collective-permute-done((bf16[128,4096]{1,0:T(8,128)(2,1)S(1)}, bf16[128,4096]{1,0:T(8,128)(2,1)S(1)}, u32[]{:S(2)}, u32[]{:S(2)}) %collective-permute-start.2) | collective-permute-done | bytes 1048608 | tf_op jit(solution)/shard_map/ppermute | solution.py:72
  67.2 2.3 %collective-permute-done.1.refs_1_ = bf16[128,4096]{1,0:T(8,128)(2,1)} collective-permute-done((bf16[128,4096]{1,0:T(8,128)(2,1)S(1)}, bf16[128,4096]{1,0:T(8,128)(2,1)}, u32[]{:S(2)}, u32[]{:S(2)}) %collective-permute-start.1) | collective-permute-done | bytes 1048608 | tf_op jit(solution)/shard_map/ppermute | solution.py:72
  69.5 3.6 %shard_map.132 = (bf16[512,128]{1,0:T(8,128)(2,1)}, f32[512,128]{1,0:T(8,128)}) custom-call(bf16[4096,128]{1,0:T(8,128)(2,1)} %bitcast.7, f32[1,128]{1,0:T(1,128)} %bias_in.3, bf16[128,4096]{1,0:T(8,128)(2,1)S(1)} %get-tuple-element.22.refs_0_, bf16[128,4096]{1,0:T(8,128)(2,1)} %collective-permute-done.1.refs_1_, ...), custom_call_target="tpu_custom_call" | custom-call | tf_op jit(solution)/shard_map/pallas_call | solution.py:210
  73.1 0.0 all-to-all-done.1.pair
  73.1 3.5 %collective-permute-start.6 = (bf16[128,4096]{1,0:T(8,128)(2,1)S(1)}, bf16[128,4096]{1,0:T(8,128)(2,1)S(1)}, u32[]{:S(2)}, u32[]{:S(2)}) collective-permute-start(bf16[128,4096]{1,0:T(8,128)(2,1)S(1)} %collective-permute-done.3.refs_3_), channel_id=1, source_target_pairs={{0,64},{1,65},{2,66},{3,67},{4,68},{5,69},{6,70},{7,71},{8,72},{9,... | collective-permute-start | bytes 3145736 | tf_op jit(solution)/shard_map/ppermute | solution.py:72
  76.6 1.9 %collective-permute-start.5 = (bf16[128,4096]{1,0:T(8,128)(2,1)S(1)}, bf16[128,4096]{1,0:T(8,128)(2,1)S(1)}, u32[]{:S(2)}, u32[]{:S(2)}) collective-permute-start(bf16[128,4096]{1,0:T(8,128)(2,1)S(1)} %collective-permute-done.2.refs_2_), channel_id=1, source_target_pairs={{0,64},{1,65},{2,66},{3,67},{4,68},{5,69},{6,70},{7,71},{8,72},{9,... | collective-permute-start | bytes 3145736 | tf_op jit(solution)/shard_map/ppermute | solution.py:72
  78.6 2.4 %collective-permute-start.4 = (bf16[128,4096]{1,0:T(8,128)(2,1)}, bf16[128,4096]{1,0:T(8,128)(2,1)S(1)}, u32[]{:S(2)}, u32[]{:S(2)}) collective-permute-start(bf16[128,4096]{1,0:T(8,128)(2,1)} %collective-permute-done.1.refs_1_), channel_id=1, source_target_pairs={{0,64},{1,65},{2,66},{3,67},{4,68},{5,69},{6,70},{7,71},{8,72},{9,... | collective-permute-start | bytes 3145736 | tf_op jit(solution)/shard_map/ppermute | solution.py:72
  81.0 0.0 collective-permute-done.7.refs_3_.refs_7_
  81.0 1.9 %collective-permute-start.8 = (bf16[64,4096]{1,0:T(8,128)(2,1)}, bf16[64,4096]{1,0:T(8,128)(2,1)S(1)}, u32[]{:S(2)}, u32[]{:S(2)}) collective-permute-start(bf16[64,4096]{1,0:T(8,128)(2,1)} %collective-permute-done.7.refs_3_.refs_7_), channel_id=1, source_target_pairs={{0,64},{1,65},{2,66},{3,67},{4,68},{5,69},{6,70},{7,71},{8,72},{9,... | collective-permute-start | bytes 1572872 | tf_op jit(solution)/shard_map/ppermute | solution.py:72
  82.9 2.1 %collective-permute-done.8.refs_4_.refs_8_ = bf16[64,4096]{1,0:T(8,128)(2,1)S(1)} collective-permute-done((bf16[64,4096]{1,0:T(8,128)(2,1)}, bf16[64,4096]{1,0:T(8,128)(2,1)S(1)}, u32[]{:S(2)}, u32[]{:S(2)}) %collective-permute-start.8) | collective-permute-done | bytes 524320 | tf_op jit(solution)/shard_map/ppermute | solution.py:72
  85.0 0.0 collective-permute-done.6.refs_2_.refs_6_
  85.0 0.0 collective-permute-done.5.refs_1_.refs_5_
  85.0 0.0 collective-permute-done.4.refs_0_.refs_4_
  85.0 3.6 %shard_map.133 = (bf16[512,128]{1,0:T(8,128)(2,1)}, f32[512,128]{1,0:T(8,128)}, bf16[8,128,128]{2,1,0:T(8,128)(2,1)}) custom-call(s32[18]{0:T(128)S(1)} %pad_add_fusion.spots.places, bf16[512,128]{1,0:T(8,128)(2,1)} %get-tuple-element.26.hidden_d, bf16[4096,128]{1,0:T(8,128)(2,1)} %bitcast.8, f32[1,128]{1,0:T(1,128)} %bias_in.3, bf16[128,128]{1,0:T(8,128)(2,1)} %bitcast.9, ...), custom_call_target="tpu_custom_call" | custom-call | tf_op jit(solution)/shard_map/pallas_call | solution.py:210
  88.6 16.7 %all_to_all.20.sums = bf16[8,128,128]{2,1,0:T(8,128)(2,1)S(1)} all-to-all(bf16[8,128,128]{2,1,0:T(8,128)(2,1)} %get-tuple-element.29), channel_id=1, replica_groups=mesh['ylo'=4,'core'=2,'x'=4,'yhi'=2,'z'=8] {'z'}, dimensions={0} | all-to-all | bytes 524288 | tf_op jit(solution)/shard_map/all_to_all | solution.py:64
  105.3 0.9 shard_map.134
  106.2 14.2 %all_to_all.21.back = bf16[8,128,128]{2,1,0:T(8,128)(2,1)S(1)} all-to-all(bf16[8,128,128]{2,1,0:T(8,128)(2,1)S(1)} %shard_map.134), channel_id=1, replica_groups=mesh['ylo'=4,'core'=2,'x'=4,'yhi'=2,'z'=8] {'z'}, dimensions={0} | all-to-all | bytes 524288 | tf_op jit(solution)/shard_map/all_to_all | solution.py:64
  120.4 6.6 %shard_map.135 = (f32[1,128]{1,0:T(1,128)}, f32[128,128]{1,0:T(8,128)}, f32[4096,128]{1,0:T(8,128)}) custom-call(s32[18]{0:T(128)S(1)} %pad_add_fusion.spots.places, bf16[8,128,128]{2,1,0:T(8,128)(2,1)S(1)} %all_to_all.21.back, bf16[512,128]{1,0:T(8,128)(2,1)} %get-tuple-element.26.hidden_d, bf16[512,128]{1,0:T(8,128)(2,1)} %get-tuple-element.31.hidden_s, ...), custom_call_target="tpu_custom_call" | custom-call | tf_op jit(solution)/shard_map/pallas_call | solution.py:210
Async XLA Ops:
  2.6 37.8 %all-to-all-start = ((bf16[32,2,4096]{2,1,0:T(2,128)(2,1)}), bf16[32,2,4096]{2,1,0:T(2,128)(2,1)S(1)}, u32[]{:S(2)}, u32[]{:S(2)}) async-start(bf16[32,2,4096]{2,1,0:T(2,128)(2,1)} %broadcast_in_dim.18), calls=%async_computation | async-start | bytes 1048576 | tf_op jit(solution)/shard_map/all_to_all | solution.py:64
  22.0 0.8 copy-start
  22.9 0.8 copy-start.1
  23.6 0.7 copy-start.2
  24.3 0.7 copy-start.3
  40.6 5.7 %collective-permute-start = (bf16[64,4096]{1,0:T(8,128)(2,1)S(1)}, bf16[64,4096]{1,0:T(8,128)(2,1)S(1)}, u32[]{:S(2)}, u32[]{:S(2)}) collective-permute-start(bf16[64,4096]{1,0:T(8,128)(2,1)S(1)} %reshape.11.mine), channel_id=1, source_target_pairs={{0,64},{1,65},{2,66},{3,67},{4,68},{5,69},{6,70},{7,71},{8,72},{9,... | collective-permute-start | bytes 1572872 | tf_op jit(solution)/shard_map/ppermute | solution.py:72
  47.3 16.7 %collective-permute-start.3 = (bf16[128,4096]{1,0:T(8,128)(2,1)S(1)}, bf16[128,4096]{1,0:T(8,128)(2,1)S(1)}, u32[]{:S(2)}, u32[]{:S(2)}) collective-permute-start(bf16[128,4096]{1,0:T(8,128)(2,1)S(1)} %get-tuple-element.22.refs_0_), channel_id=1, source_target_pairs={{1,0},{2,1},{3,2},{4,3},{5,4},{6,5},{7,6},{0,7},{9,8},{10,9},{11,1... | collective-permute-start | bytes 3145736 | tf_op jit(solution)/shard_map/ppermute | solution.py:72
  50.1 17.1 %collective-permute-start.2 = (bf16[128,4096]{1,0:T(8,128)(2,1)S(1)}, bf16[128,4096]{1,0:T(8,128)(2,1)S(1)}, u32[]{:S(2)}, u32[]{:S(2)}) collective-permute-start(bf16[128,4096]{1,0:T(8,128)(2,1)S(1)} %get-tuple-element.22.refs_0_), channel_id=1, source_target_pairs={{128,0},{129,1},{130,2},{131,3},{132,4},{133,5},{134,6},{135,7},{1... | collective-permute-start | bytes 3145736 | tf_op jit(solution)/shard_map/ppermute | solution.py:72
  52.2 17.3 %collective-permute-start.1 = (bf16[128,4096]{1,0:T(8,128)(2,1)S(1)}, bf16[128,4096]{1,0:T(8,128)(2,1)}, u32[]{:S(2)}, u32[]{:S(2)}) collective-permute-start(bf16[128,4096]{1,0:T(8,128)(2,1)S(1)} %get-tuple-element.22.refs_0_), channel_id=1, source_target_pairs={{16,0},{17,1},{18,2},{19,3},{20,4},{21,5},{22,6},{23,7},{24,8},{25... | collective-permute-start | bytes 3145736 | tf_op jit(solution)/shard_map/ppermute | solution.py:72
  55.4 17.7 %all-to-all-start.1 = ((bf16[8,2,16,128]{3,2,1,0:T(8,128)(2,1)}), bf16[8,2,16,128]{3,2,1,0:T(8,128)(2,1)S(1)}, u32[]{:S(2)}, u32[]{:S(2)}) async-start(bf16[8,2,16,128]{3,2,1,0:T(8,128)(2,1)} %shard_map.130), calls=%async_computation.1 | async-start | bytes 131072 | tf_op jit(solution)/shard_map/all_to_all | solution.py:64
  61.0 20.0 %collective-permute-start.7 = (bf16[64,4096]{1,0:T(8,128)(2,1)}, bf16[64,4096]{1,0:T(8,128)(2,1)}, u32[]{:S(2)}, u32[]{:S(2)}) collective-permute-start(bf16[64,4096]{1,0:T(8,128)(2,1)} %get-tuple-element.28), channel_id=1, source_target_pairs={{129,0},{130,1},{131,2},{132,3},{133,4},{134,5},{135,6},{128,7},{1... | collective-permute-start | bytes 1572872 | tf_op jit(solution)/shard_map/ppermute | solution.py:72
  73.1 11.9 %collective-permute-start.6 = (bf16[128,4096]{1,0:T(8,128)(2,1)S(1)}, bf16[128,4096]{1,0:T(8,128)(2,1)S(1)}, u32[]{:S(2)}, u32[]{:S(2)}) collective-permute-start(bf16[128,4096]{1,0:T(8,128)(2,1)S(1)} %collective-permute-done.3.refs_3_), channel_id=1, source_target_pairs={{0,64},{1,65},{2,66},{3,67},{4,68},{5,69},{6,70},{7,71},{8,72},{9,... | collective-permute-start | bytes 3145736 | tf_op jit(solution)/shard_map/ppermute | solution.py:72
  76.6 8.4 %collective-permute-start.5 = (bf16[128,4096]{1,0:T(8,128)(2,1)S(1)}, bf16[128,4096]{1,0:T(8,128)(2,1)S(1)}, u32[]{:S(2)}, u32[]{:S(2)}) collective-permute-start(bf16[128,4096]{1,0:T(8,128)(2,1)S(1)} %collective-permute-done.2.refs_2_), channel_id=1, source_target_pairs={{0,64},{1,65},{2,66},{3,67},{4,68},{5,69},{6,70},{7,71},{8,72},{9,... | collective-permute-start | bytes 3145736 | tf_op jit(solution)/shard_map/ppermute | solution.py:72
  78.6 6.4 %collective-permute-start.4 = (bf16[128,4096]{1,0:T(8,128)(2,1)}, bf16[128,4096]{1,0:T(8,128)(2,1)S(1)}, u32[]{:S(2)}, u32[]{:S(2)}) collective-permute-start(bf16[128,4096]{1,0:T(8,128)(2,1)} %collective-permute-done.1.refs_1_), channel_id=1, source_target_pairs={{0,64},{1,65},{2,66},{3,67},{4,68},{5,69},{6,70},{7,71},{8,72},{9,... | collective-permute-start | bytes 3145736 | tf_op jit(solution)/shard_map/ppermute | solution.py:72
  81.0 4.0 %collective-permute-start.8 = (bf16[64,4096]{1,0:T(8,128)(2,1)}, bf16[64,4096]{1,0:T(8,128)(2,1)S(1)}, u32[]{:S(2)}, u32[]{:S(2)}) collective-permute-start(bf16[64,4096]{1,0:T(8,128)(2,1)} %collective-permute-done.7.refs_3_.refs_7_), channel_id=1, source_target_pairs={{0,64},{1,65},{2,66},{3,67},{4,68},{5,69},{6,70},{7,71},{8,72},{9,... | collective-permute-start | bytes 1572872 | tf_op jit(solution)/shard_map/ppermute | solution.py:72
